TPU v7x, 32 devices: a whole 2x2x4 slice. The times are simulated.
32 devices in a mesh: det: 4 (over y, x), tm: 8 (over z, core).
Axes of the slice: x: 2, y: 2, z: 4, core: 2. Of those that a mesh axis runs over, the one named last changes fastest.
Arguments:
- samples: float32 [4, 8, 32, 256], P('det', 'tm')
- pointing: int32 [4, 8, 32, 256], P('det', 'tm'), may hold values from 0 to 16383, as said below
- angles: float32 [4, 8, 32, 256], P('det', 'tm'), may hold values from -3.1415927 to 3.1415927
- counts: int32 [4, 8, 32], P('det', 'tm'), may hold values from 1 to 256, as said below
- sky_map: float32 [3, 64, 8192], P(None, ('det', 'tm'))
- prior_precision: float32 [3, 64, 4096], P(None, 'det', 'tm'), may hold values from 0.5 to 5
- omega_noise: float32 [6, 64, 4096], P(None, 'det', 'tm'), may hold values from -6 to 6
- omega_prior: float32 [6, 64, 4096], P(None, 'det', 'tm'), may hold values from -6 to 6
Outputs:
- gains: float32 [4, 8], P('det', 'tm')
- binned: float32 [3, 64, 8192], P(None, ('det', 'tm'))
- solution: float32 [6, 64, 4096], P(None, 'det', 'tm')
Inputs may be any that keep to these rules, and one draw needn't show every extreme that they name: The first counts[g, t, k] slots of a row hold samples; some sky tile takes 256 samples from every device, and every device fills at least one tile. `pointing`: pixel within the destination tile, cycle-major with 8192 pixels a cycle.
All inputs are finite; a program needn't handle non-finite values.
Results may differ from a plain program's by a relative error of at most 0.0003.
Values sent between devices are 32-bit elements; how exact they have to be, the bound alone decides.
No kernel may reach another device: no remote copies, remote signals or barrier semaphores. Data moves between devices by JAX's collectives and lax.ppermute only.
A program may use at most 128 MiB of HBM per device.

v0:
```python
import math

import jax
import jax.numpy as jnp
from jax import lax
from jax.sharding import PartitionSpec as P

ITERS = 3


def with_halo(cells, sides, width):
    for axis, dim in sides:
        count = lax.axis_size(axis)
        ends = count - 1
        head = lax.slice_in_dim(cells, 0, width, axis=dim)
        tail = lax.slice_in_dim(cells, cells.shape[dim] - width, cells.shape[dim], axis=dim)
        cells = jnp.concatenate(
            [
                lax.ppermute(tail, axis, [(i, (i + 1) % count) for i in range(ends)]),
                cells,
                lax.ppermute(head, axis, [((i + 1) % count, i) for i in range(ends)]),
            ],
            axis=dim,
        )
    return cells


def cycle_modes(field):
    nphi = field.shape[-1]
    cycles = field.shape[1]
    second = 128
    first = nphi // second
    half = second // 2
    highest = lax.Precision.HIGHEST
    values = field.reshape(3, cycles, first, second)
    row_a = lax.broadcasted_iota(jnp.int32, (first, first), 0)
    col_a = lax.broadcasted_iota(jnp.int32, (first, first), 1)
    angle_a = 2.0 * math.pi / first * (row_a * col_a % first).astype(jnp.float32)
    cos_a = jnp.cos(angle_a)
    sin_a = jnp.sin(angle_a)
    real_y = jnp.einsum("kj,crjb->crkb", cos_a, values, precision=highest)
    imag_y = -jnp.einsum("kj,crjb->crkb", sin_a, values, precision=highest)
    row_t = lax.broadcasted_iota(jnp.int32, (first, second), 0)
    col_t = lax.broadcasted_iota(jnp.int32, (first, second), 1)
    angle_t = 2.0 * math.pi / nphi * (row_t * col_t % nphi).astype(jnp.float32)
    cos_t = jnp.cos(angle_t)
    sin_t = jnp.sin(angle_t)
    real_z = real_y * cos_t + imag_y * sin_t
    imag_z = imag_y * cos_t - real_y * sin_t
    row_b = lax.broadcasted_iota(jnp.int32, (half, second), 0)
    col_b = lax.broadcasted_iota(jnp.int32, (half, second), 1)
    angle_b = 2.0 * math.pi / second * (row_b * col_b % second).astype(jnp.float32)
    cos_b = jnp.cos(angle_b)
    sin_b = jnp.sin(angle_b)
    real_x = jnp.einsum("qj,crkj->crqk", cos_b, real_z, precision=highest) + jnp.einsum(
        "qj,crkj->crqk", sin_b, imag_z, precision=highest
    )
    imag_x = jnp.einsum("qj,crkj->crqk", cos_b, imag_z, precision=highest) - jnp.einsum(
        "qj,crkj->crqk", sin_b, real_z, precision=highest
    )
    scale = 1.0 / math.sqrt(nphi)
    real_x = real_x.reshape(3, cycles, half * first) * scale
    imag_x = imag_x.reshape(3, cycles, half * first) * scale
    return jnp.stack([real_x, imag_x], axis=1).reshape(6, cycles, half * first)


def operate(field, root, diagonal):
    scaled = root * field
    padded = with_halo(scaled, (("det", 1),), 1)
    beside = padded[:, 2:] + padded[:, :-2]
    return diagonal * field - 0.45 * root * beside


def squares(vector):
    return lax.psum(jnp.sum(vector * vector), ("det", "tm"))


def per_device(
    samples, pointing, angles, counts, sky_map, prior_precision, omega_noise, omega_prior
):
    tiles = samples.shape[2]
    slots_cap = samples.shape[3]
    n_tm = lax.axis_size("tm")
    rdev = sky_map.shape[1]
    nphi = sky_map.shape[2]
    pixels = rdev * nphi
    flat_data = samples.reshape(tiles, slots_cap)
    flat_angle = angles.reshape(tiles, slots_cap)
    flat_pixel = pointing.reshape(tiles, slots_cap).astype(jnp.float32)
    flat_count = counts.reshape(tiles, 1).astype(jnp.float32)
    got_data, got_angle, got_pixel, got_count = (
        lax.all_to_all(flat_data, ("det", "tm"), split_axis=0, concat_axis=0, tiled=True),
        lax.all_to_all(flat_angle, ("det", "tm"), split_axis=0, concat_axis=0, tiled=True),
        lax.all_to_all(flat_pixel, ("det", "tm"), split_axis=0, concat_axis=0, tiled=True),
        lax.all_to_all(flat_count, ("det", "tm"), split_axis=0, concat_axis=0, tiled=True),
    )
    pixel_index = got_pixel.astype(jnp.int32)
    slot_index = lax.broadcasted_iota(jnp.int32, (tiles, slots_cap), 1).astype(jnp.float32)
    valid = (slot_index < got_count).astype(jnp.float32)
    sky_flat = sky_map.reshape(3, pixels)
    cosine = jnp.cos(2.0 * got_angle)
    sine = jnp.sin(2.0 * got_angle)
    looked = sky_flat[:, pixel_index]
    signal = looked[0] + looked[1] * cosine + looked[2] * sine
    masked_signal = valid * signal
    part_cross = jnp.sum(masked_signal * got_data, axis=1)
    part_square = jnp.sum(masked_signal * signal, axis=1)
    total_cross, total_square = lax.psum((part_cross, part_square), ("det", "tm"))
    gains_all = total_cross / (total_square + 1e-06)
    position = lax.axis_index("det") * n_tm + lax.axis_index("tm")
    own_gain = lax.dynamic_slice_in_dim(gains_all, position, 1).reshape(1, 1)
    residual = valid * (got_data - gains_all[:, None] * signal)
    weights = jnp.stack([residual, residual * cosine, residual * sine]).reshape(3, -1)
    binned = jnp.zeros((3, pixels), jnp.float32).at[:, pixel_index.reshape(-1)].add(weights)
    cycle_index = (pixel_index // nphi).reshape(1, -1)
    cycle_ids = lax.broadcasted_iota(jnp.int32, (rdev, 1), 0)
    hits = jnp.sum(jnp.where(cycle_index == cycle_ids, valid.reshape(1, -1), 0.0), axis=1)
    binned = binned.reshape(3, rdev, nphi)
    planes = cycle_modes(binned)
    modes_count = planes.shape[2]
    weight_plane = jnp.broadcast_to((hits / nphi)[None, :, None], (1, rdev, modes_count))
    spectrum, weight = (
        lax.all_to_all(planes, "tm", split_axis=2, concat_axis=1, tiled=True),
        lax.all_to_all(weight_plane, "tm", split_axis=2, concat_axis=1, tiled=True),
    )
    precision = jnp.repeat(prior_precision, 2, axis=0)
    root = jnp.sqrt(precision)
    diagonal = precision + weight
    rhs = spectrum + jnp.sqrt(weight) * omega_noise + root * omega_prior
    solution = jnp.zeros_like(rhs)
    resid = rhs
    direction = rhs
    norm_now = squares(resid)
    for iteration in range(ITERS):
        image = operate(direction, root, diagonal)
        alpha = norm_now / lax.psum(jnp.sum(direction * image), ("det", "tm"))
        solution = solution + alpha * direction
        resid = resid - alpha * image
        norm_next = squares(resid)
        direction = resid + norm_next / norm_now * direction
        norm_now = norm_next
    return (own_gain, binned, solution)


def solution(mesh):
    return jax.shard_map(
        per_device,
        mesh=mesh,
        in_specs=(
            P("det", "tm", None, None),
            P("det", "tm", None, None),
            P("det", "tm", None, None),
            P("det", "tm", None),
            P(None, ("det", "tm"), None),
            P(None, "det", "tm"),
            P(None, "det", "tm"),
            P(None, "det", "tm"),
        ),
        out_specs=(P("det", "tm"), P(None, ("det", "tm"), None), P(None, "det", "tm")),
        check_vma=False,
    )
```

profile of v0, /device:TPU:0, one launch (start us, length us, event | category | flops | bytes accessed | tf_op | source)
XLA Modules:
  0.0 506.3 jit_solution(17587187857238490097)
XLA Ops:
  0.6 0.7 convert_bitcast_fusion
  1.3 0.7 copy.94
  2.0 7.3 %all-to-all-start = ((f32[32,1,1]{2,1,0:T(1,128)}), f32[32,1,1]{2,1,0:T(1,128)S(1)}, u32[]{:S(2)}, u32[]{:S(2)}) async-start(f32[32,1,1]{2,1,0:T(1,128)} %copy.94), calls=%async_computation | async-start | bytes 32768 | tf_op jit(solution)/shard_map/all_to_all | solution.py:95
  9.4 1.4 all_to_all.54
  10.8 1.4 all_to_all.52
  12.2 5.5 %copy.95 = f32[3,2,8192]{0,2,1:T(8,128)} copy(f32[3,2,8192]{2,1,0:T(2,128)} %param.12) | data formatting | bytes 393216 | tf_op args[4]
  17.8 0.6 copy.142
  18.4 5.8 %all-to-all-start.1 = ((f32[32,1,256]{2,1,0:T(1,128)}), f32[32,1,256]{2,1,0:T(1,128)S(1)}, u32[]{:S(2)}, u32[]{:S(2)}) async-start(f32[32,1,256]{2,1,0:T(1,128)} %bitcast.171), calls=%async_computation.1 | async-start | bytes 65536 | tf_op jit(solution)/shard_map/all_to_all | solution.py:94
  24.7 6.8 %all-to-all-done.1 = f32[32,1,256]{2,1,0:T(1,128)S(1)} async-done(((f32[32,1,256]{2,1,0:T(1,128)}), f32[32,1,256]{2,1,0:T(1,128)S(1)}, u32[]{:S(2)}, u32[]{:S(2)}) %all-to-all-start.1) | async-done | bytes 32800 | tf_op jit(solution)/shard_map/all_to_all | solution.py:94
  31.5 2.6 all-to-all-start.2
  34.1 31.1 %gather_fusion = f32[8192,3]{1,0:T(8,128)} fusion(f32[3,16384]{0,1:T(8,128)} %bitcast.178, s32[8192]{0:T(1024)S(1)} %broadcast_clamp_fusion), kind=kCustom, calls=%fused_computation | custom fusion | bytes 229376 | tf_op jit(solution)/shard_map/gather | solution.py:103
  65.2 2.8 copy.97
  68.2 5.8 %all-to-all-start.3 = ((f32[32,1,256]{2,1,0:T(1,128)}), f32[32,1,256]{2,1,0:T(1,128)S(1)}, u32[]{:S(2)}, u32[]{:S(2)}) async-start(f32[32,1,256]{2,1,0:T(1,128)} %all_to_all.54), calls=%async_computation.3 | async-start | bytes 65536 | tf_op jit(solution)/shard_map/all_to_all | solution.py:92
  74.0 0.9 broadcast_multiply_fusion
  75.0 5.3 %slice.70 = f32[1,32,256]{0,2,1:T(8,128)} slice(f32[3,32,256]{0,2,1:T(8,128)} %bitcast.175), slice={[2:3], [0:32], [0:256]} | slice | bytes 65536 | tf_op jit(solution)/shard_map/slice | solution.py:104
  80.3 2.8 copy.117
  83.1 2.9 copy.120
  86.2 40.5 %all-reduce.1 = (f32[32]{0:T(128)S(1)}, f32[32]{0:T(128)S(1)}) all-reduce(f32[32]{0:T(128)S(1)} %get-tuple-element.27, f32[32]{0:T(128)S(1)} %get-tuple-element.26), channel_id=1, replica_groups=mesh['det'=4,'tm'=8] {'det','tm'}, use_global_device_ids=true, to_apply=%region_1.0 | all-reduce | flops 64 | bytes 512 | tf_op jit(solution)/shard_map/psum | solution.py:108
  126.7 0.9 reshape_multiply_fusion
  127.7 0.9 bitcast_multiply_fusion.1
  128.6 2.7 copy.102
  131.3 48.2 %scatter_custom_fusion = f32[3,16384]{0,1:T(8,128)} fusion(s32[8192]{0:T(1024)S(1)} %bitcast.191, f32[8192,3]{1,0:T(8,128)} %copy.102, f32[]{:T(128)} %constant.72.clone.1), kind=kCustom, calls=%fused_computation.2 | custom fusion | flops 24576 | bytes 197120 | tf_op jit(solution)/shard_map/scatter-add | solution.py:114
  179.5 5.2 %copy.103 = f32[3,2,64,128]{3,2,1,0:T(8,128)S(1)} copy(f32[3,2,64,128]{0,3,2,1:T(8,128)} %bitcast.172) | data formatting | bytes 393216 | tf_op jit(solution)/shard_map/reshape;reshape | solution.py:35
  184.7 0.5 convolution_bitcast_fusion
  185.2 0.5 fusion.6
  186.6 0.4 fusion.3
  187.3 0.4 fusion.5
  188.2 1.1 broadcast_bitcast_fusion
  189.3 0.5 broadcast.321
  189.9 19.4 %reduce.2 = f32[4096,2]{1,0:T(8,128)} reduce(f32[4096,1,2]{2,1,0:T(1,128)S(1)} %broadcast_bitcast_fusion, f32[]{:T(128)} %broadcast.321), dimensions={1}, to_apply=%broadcast_bitcast_fusion.reduce_sub_computation | reduce | bytes 65540
  209.3 3.7 reshape.365
  212.9 3.9 all-to-all-start.5
  217.0 4.5 copy.108
  221.5 8.6 %reshape.363 = f32[8,1,6144]{2,1,0:T(1,128)} reshape(f32[4096,2,6]{2,1,0:T(2,128)} %bitcast.176) | data formatting | bytes 393216
  230.1 5.1 %all-to-all-start.4 = ((f32[8,1,6144]{2,1,0:T(1,128)}), f32[8,1,6144]{2,1,0:T(1,128)S(1)}, u32[]{:S(2)}, u32[]{:S(2)}) async-start(f32[8,1,6144]{2,1,0:T(1,128)} %reshape.363), calls=%async_computation.4 | async-start | bytes 393216 | tf_op jit(solution)/shard_map/all_to_all | solution.py:123
  235.2 0.7 reduce.3
  235.9 3.4 reshape.366
  239.3 0.6 copy.110
  240.0 3.5 all-to-all-done.4
  243.5 1.1 reduce.1
  244.7 8.5 %reshape.364 = f32[4096,2,6]{2,1,0:T(2,128)} reshape(f32[8,6144]{1,0:T(8,128)S(1)} %reduce.1) | data formatting | bytes 393216
  253.2 5.2 %copy.109 = f32[6,8,2,512]{3,2,1,0:T(2,128)S(1)} copy(f32[6,8,2,512]{0,2,3,1:T(2,128)} %bitcast.177) | data formatting | bytes 393216 | tf_op jit(solution)/shard_map/all_to_all | solution.py:123
  258.7 4.2 collective-permute-start.1
  262.9 1.3 collective-permute-start
  264.3 4.2 collective-permute-done
  268.5 0.8 multiply_reduce_fusion.3
  269.3 38.8 %all-reduce = (f32[]{:T(128)}, f32[]{:T(128)}) all-reduce(f32[]{:T(128)} %get-tuple-element.25, f32[]{:T(128)} %get-tuple-element.24), channel_id=1, replica_groups=mesh['det'=4,'tm'=8] {'det','tm'}, use_global_device_ids=true, to_apply=%region_7.8 | all-reduce | flops 2 | bytes 16 | tf_op jit(solution)/shard_map/psum | solution.py:75
  309.4 0.7 multiply_reduce_fusion.2
  310.1 42.2 %psum.60 = f32[]{:T(128)} all-reduce(f32[]{:T(128)} %get-tuple-element.34), channel_id=1, replica_groups=mesh['det'=4,'tm'=8] {'det','tm'}, use_global_device_ids=true, to_apply=%region_11.12 | all-reduce | flops 1 | bytes 8 | tf_op jit(solution)/shard_map/psum | solution.py:75
  353.7 4.2 collective-permute-start.3
  357.9 1.3 collective-permute-start.2
  359.3 4.2 collective-permute-done.2
  363.5 0.7 multiply_reduce_fusion.1
  364.2 38.9 %psum.61 = f32[]{:T(128)} all-reduce(f32[]{:T(128)} %multiply_reduce_fusion.1), channel_id=1, replica_groups=mesh['det'=4,'tm'=8] {'det','tm'}, use_global_device_ids=true, to_apply=%region_13.14 | all-reduce | flops 1 | bytes 8 | tf_op jit(solution)/shard_map/psum | solution.py:136
  404.5 0.7 multiply_reduce_fusion
  405.2 41.9 %psum.62 = f32[]{:T(128)} all-reduce(f32[]{:T(128)} %multiply_reduce_fusion), channel_id=1, replica_groups=mesh['det'=4,'tm'=8] {'det','tm'}, use_global_device_ids=true, to_apply=%region_15.16 | all-reduce | flops 1 | bytes 8 | tf_op jit(solution)/shard_map/psum | solution.py:75
  448.7 4.2 collective-permute-start.5
  452.9 1.3 collective-permute-start.4
  454.2 0.6 dynamic_slice.3
  454.8 3.7 collective-permute-done.4
  458.4 0.7 fusion.22
  459.1 5.9 %copy.111 = f32[3,2,8192]{2,1,0:T(2,128)} copy(f32[3,2,8192]{0,2,1:T(8,128)} %bitcast.173) | data formatting | bytes 393216
  465.0 38.8 %psum.63 = f32[]{:T(128)} all-reduce(f32[]{:T(128)} %fusion.22), channel_id=1, replica_groups=mesh['det'=4,'tm'=8] {'det','tm'}, use_global_device_ids=true, to_apply=%region_17.18 | all-reduce | flops 1 | bytes 8 | tf_op jit(solution)/shard_map/psum | solution.py:136
  505.1 0.7 multiply_add_fusion
  (50 shorter events, 3.6 us)
Async XLA Ops:
  2.0 16.4 %all-to-all-start = ((f32[32,1,1]{2,1,0:T(1,128)}), f32[32,1,1]{2,1,0:T(1,128)S(1)}, u32[]{:S(2)}, u32[]{:S(2)}) async-start(f32[32,1,1]{2,1,0:T(1,128)} %copy.94), calls=%async_computation | async-start | bytes 32768 | tf_op jit(solution)/shard_map/all_to_all | solution.py:95
  12.2 5.5 %copy-start.3 = (s32[1,1,32,256]{3,2,1,0:T(8,128)S(1)}, s32[1,1,32,256]{3,2,1,0:T(8,128)}, u32[]{:S(2)}) copy-start(s32[1,1,32,256]{3,2,1,0:T(8,128)} %param.9) | copy-start | bytes 98308
  18.4 13.1 %all-to-all-start.1 = ((f32[32,1,256]{2,1,0:T(1,128)}), f32[32,1,256]{2,1,0:T(1,128)S(1)}, u32[]{:S(2)}, u32[]{:S(2)}) async-start(f32[32,1,256]{2,1,0:T(1,128)} %bitcast.171), calls=%async_computation.1 | async-start | bytes 65536 | tf_op jit(solution)/shard_map/all_to_all | solution.py:94
  31.5 36.7 %all-to-all-start.2 = ((f32[32,1,256]{2,1,0:T(1,128)}), f32[32,1,256]{2,1,0:T(1,128)S(1)}, u32[]{:S(2)}, u32[]{:S(2)}) async-start(f32[32,1,256]{2,1,0:T(1,128)} %all_to_all.52), calls=%async_computation.2 | async-start | bytes 65536 | tf_op jit(solution)/shard_map/all_to_all | solution.py:93
  68.2 17.8 %all-to-all-start.3 = ((f32[32,1,256]{2,1,0:T(1,128)}), f32[32,1,256]{2,1,0:T(1,128)S(1)}, u32[]{:S(2)}, u32[]{:S(2)}) async-start(f32[32,1,256]{2,1,0:T(1,128)} %all_to_all.54), calls=%async_computation.3 | async-start | bytes 65536 | tf_op jit(solution)/shard_map/all_to_all | solution.py:92
  212.9 17.2 %all-to-all-start.5 = ((f32[8,1,1024]{2,1,0:T(1,128)}), f32[8,1,1024]{2,1,0:T(1,128)S(1)}, u32[]{:S(2)}, u32[]{:S(2)}) async-start(f32[8,1,1024]{2,1,0:T(1,128)} %reshape.365), calls=%async_computation.5 | async-start | bytes 65536 | tf_op jit(solution)/shard_map/all_to_all | solution.py:124
  230.1 13.4 %all-to-all-start.4 = ((f32[8,1,6144]{2,1,0:T(1,128)}), f32[8,1,6144]{2,1,0:T(1,128)S(1)}, u32[]{:S(2)}, u32[]{:S(2)}) async-start(f32[8,1,6144]{2,1,0:T(1,128)} %reshape.363), calls=%async_computation.4 | async-start | bytes 393216 | tf_op jit(solution)/shard_map/all_to_all | solution.py:123
  244.6 14.0 %copy-start = (f32[3,16,512]{2,1,0:T(8,128)S(1)}, f32[3,16,512]{2,1,0:T(8,128)}, u32[]{:S(2)}) copy-start(f32[3,16,512]{2,1,0:T(8,128)} %param.13) | copy-start | bytes 294916
  244.7 14.0 %copy-start.1 = (f32[6,16,512]{2,1,0:T(8,128)S(1)}, f32[6,16,512]{2,1,0:T(8,128)}, u32[]{:S(2)}) copy-start(f32[6,16,512]{2,1,0:T(8,128)} %param.15) | copy-start | bytes 589828
  244.7 14.0 %copy-start.2 = (f32[6,16,512]{2,1,0:T(8,128)S(1)}, f32[6,16,512]{2,1,0:T(8,128)}, u32[]{:S(2)}) copy-start(f32[6,16,512]{2,1,0:T(8,128)} %param.14) | copy-start | bytes 589828
  258.7 5.6 %collective-permute-start.1 = (f32[6,1,512]{2,1,0:T(1,128)S(1)}, f32[6,1,512]{2,1,0:T(1,128)S(1)}, u32[]{:S(2)}, u32[]{:S(2)}) collective-permute-start(f32[6,1,512]{2,1,0:T(1,128)S(1)} %get-tuple-element.45), channel_id=1, source_target_pairs={{0,8},{8,16},{16,24},{1,9},{9,17},{17,25},{2,10},{10,18},{18,26},{... | collective-permute-start | bytes 36872 | tf_op jit(solution)/shard_map/ppermute | solution.py:19
  262.9 5.6 %collective-permute-start = (f32[6,1,512]{2,1,0:T(1,128)S(1)}, f32[6,1,512]{2,1,0:T(1,128)S(1)}, u32[]{:S(2)}, u32[]{:S(2)}) collective-permute-start(f32[6,1,512]{2,1,0:T(1,128)S(1)} %get-tuple-element.44), channel_id=1, source_target_pairs={{8,0},{16,8},{24,16},{9,1},{17,9},{25,17},{10,2},{18,10},{26,18},{... | collective-permute-start | bytes 36872 | tf_op jit(solution)/shard_map/ppermute | solution.py:21
  353.7 5.6 %collective-permute-start.3 = (f32[6,1,512]{2,1,0:T(1,128)S(1)}, f32[6,1,512]{2,1,0:T(1,128)S(1)}, u32[]{:S(2)}, u32[]{:S(2)}) collective-permute-start(f32[6,1,512]{2,1,0:T(1,128)S(1)} %get-tuple-element.43), channel_id=1, source_target_pairs={{0,8},{8,16},{16,24},{1,9},{9,17},{17,25},{2,10},{10,18},{18,26},{... | collective-permute-start | bytes 36872 | tf_op jit(solution)/shard_map/ppermute | solution.py:19
  357.9 5.6 %collective-permute-start.2 = (f32[6,1,512]{2,1,0:T(1,128)S(1)}, f32[6,1,512]{2,1,0:T(1,128)S(1)}, u32[]{:S(2)}, u32[]{:S(2)}) collective-permute-start(f32[6,1,512]{2,1,0:T(1,128)S(1)} %get-tuple-element.42), channel_id=1, source_target_pairs={{8,0},{16,8},{24,16},{9,1},{17,9},{25,17},{10,2},{18,10},{26,18},{... | collective-permute-start | bytes 36872 | tf_op jit(solution)/shard_map/ppermute | solution.py:21
  448.7 6.1 %collective-permute-start.5 = (f32[6,1,512]{2,1,0:T(1,128)S(1)}, f32[6,1,512]{2,1,0:T(1,128)S(1)}, u32[]{:S(2)}, u32[]{:S(2)}) collective-permute-start(f32[6,1,512]{2,1,0:T(1,128)S(1)} %get-tuple-element.41), channel_id=1, source_target_pairs={{0,8},{8,16},{16,24},{1,9},{9,17},{17,25},{2,10},{10,18},{18,26},{... | collective-permute-start | bytes 36872 | tf_op jit(solution)/shard_map/ppermute | solution.py:19
  452.9 5.6 %collective-permute-start.4 = (f32[6,1,512]{2,1,0:T(1,128)S(1)}, f32[6,1,512]{2,1,0:T(1,128)S(1)}, u32[]{:S(2)}, u32[]{:S(2)}) collective-permute-start(f32[6,1,512]{2,1,0:T(1,128)S(1)} %get-tuple-element.40), channel_id=1, source_target_pairs={{8,0},{16,8},{24,16},{9,1},{17,9},{25,17},{10,2},{18,10},{26,18},{... | collective-permute-start | bytes 36872 | tf_op jit(solution)/shard_map/ppermute | solution.py:21
where the time goes:
time: 516 us; the launch traced here: 506 us
  blocking collectives  241 us (47%)
  local copies, waits for them, and re-layouts  106 us (21%)
  other arithmetic  78.7 us (15%)
  starting transfers between devices  47 us (9%)
  waiting for transfers between devices  22.6 us (4%)
  between operations  8.15 us (2%)
    psum x3, blocking collectives, squares(): return lax.psum(jnp.sum(vector * vector), ('det', 'tm'))  123 us
    psum x2, blocking collectives, per_device(): alpha = norm_now / lax.psum(jnp.sum(direction * image), ('det', 'tm'))  77.7 us
    scatter-add x1, other arithmetic, per_device(): jnp.zeros((3, pixels), jnp.float32).at[:, pixel_index.reshape(-1)]  48.2 us
    unnamed x19, local copies, waits for them, and re-layouts  43.1 us
    psum x1, blocking collectives, per_device(): lax.psum((part_cross, part_square), ('det', 'tm'))  40.5 us
    gather x2, local copies, waits for them, and re-layouts, per_device(): looked = sky_flat[:, pixel_index]  33.9 us
    unnamed x2, other arithmetic  19.5 us
    ppermute x3, starting transfers between devices, with_halo(): lax.ppermute(tail, axis, [(i, (i + 1) % count) for i in range(ends)])  12.5 us
  transfers between devices with their start and end apart: 12, of which 7 were waited for; matrix products, arithmetic and copies ran while one was open for 14% of the time, Pallas kernels for 0%

commit v1 on v0

v1 whole, which is shorter than its diff:
```python
import math

import jax
import jax.numpy as jnp
import ml_dtypes
import numpy as np
from jax import lax
from jax.experimental import pallas as pl
from jax.experimental.pallas import tpu as pltpu
from jax.sharding import PartitionSpec as P

SHIFT = 5.0
SPREAD = 5.0
COUPLING = 0.45

LANES = 128
GROUP = 2
PLANES = 6
CHUNK = 16


def split_np(table):
    high = table.astype(ml_dtypes.bfloat16)
    low = (table - high.astype(np.float64)).astype(ml_dtypes.bfloat16)
    return high, low


def split(values):
    high = values.astype(jnp.bfloat16)
    low = (values - high.astype(jnp.float32)).astype(jnp.bfloat16)
    return high, low


def dft_tables(nphi, n_tm):
    first, second = LANES, nphi // LANES
    half = second // 2
    column = np.arange(first)
    digit = 2 * (column % (first // 2)) + column // (first // 2)
    k = np.arange(first)
    angle = 2.0 * math.pi / first * (np.outer(digit, k) % first)
    stage_a = np.concatenate([np.cos(angle), np.sin(angle)], axis=1)
    high, low = split_np(stage_a)
    stage_a = np.concatenate([high, high, low], axis=0)
    b = np.arange(second)
    angle = 2.0 * math.pi / nphi * (np.outer(b, k) % nphi)
    twiddle = np.stack([np.cos(angle), np.sin(angle)]).astype(np.float32)
    per_band = half // n_tm
    row = np.arange(half)
    q = (row % n_tm) * per_band + row // n_tm
    angle = 2.0 * math.pi / second * (np.outer(q, b) % second)
    cos_b, sin_b = np.cos(angle), np.sin(angle)
    stage_b = np.block([[cos_b, -sin_b], [-sin_b, -cos_b]]) / math.sqrt(nphi)
    high, low = split_np(stage_b)
    stage_b = np.concatenate([high, high, low], axis=1)
    return stage_a, twiddle, stage_b


def pack_kernel(samples_ref, angles_ref, pointing_ref, counts_ref, out_ref):
    tiles = samples_ref.shape[0]
    halves = samples_ref.shape[1] // LANES
    for h in range(halves):
        cut = slice(h * LANES, (h + 1) * LANES)
        out_ref[pl.ds(h, tiles, stride=8), :] = samples_ref[:, cut]
        out_ref[pl.ds(halves + h, tiles, stride=8), :] = angles_ref[:, cut]
        out_ref[pl.ds(2 * halves + h, tiles, stride=8), :] = pointing_ref[:, cut].astype(jnp.float32)
    count = counts_ref[...].astype(jnp.float32)
    row = lax.broadcasted_iota(jnp.int32, (tiles, tiles), 0)
    col = lax.broadcasted_iota(jnp.int32, (tiles, tiles), 1)
    column = jnp.sum(jnp.where(row == col, count, 0.0), axis=1, keepdims=True)
    column = jnp.broadcast_to(column, (tiles, LANES))
    out_ref[pl.ds(3 * halves, tiles, stride=8), :] = column
    out_ref[pl.ds(3 * halves + 1, tiles, stride=8), :] = column


def lookup_kernel(
    got_ref, sky_ref, data_ref, signal_ref, cosine_ref, sine_ref, pixel_ref, weight_ref, sums_ref,
    table, high, low,
):
    tiles = got_ref.shape[0] // 8
    cap = data_ref.shape[1]
    halves = cap // LANES
    rows = sky_ref.shape[1]
    cycles = 2
    nphi = rows * LANES // cycles

    for c in range(3):
        part = split(sky_ref[c].T)
        table[c * LANES : (c + 1) * LANES, :rows] = part[0]
        table[c * LANES : (c + 1) * LANES, rows:] = part[1]

    def received(field):
        parts = [got_ref[pl.ds(field * halves + h, tiles, stride=8), :] for h in range(halves)]
        return jnp.concatenate(parts, axis=1)

    data = received(0)
    angle = received(1)
    pixel = received(2).astype(jnp.int32)
    count = got_ref[pl.ds(3 * halves, tiles, stride=8), :]
    count = jnp.concatenate([count] * halves, axis=1)
    slot = lax.broadcasted_iota(jnp.int32, (tiles, cap), 1).astype(jnp.float32)
    valid = jnp.where(slot < count, 1.0, 0.0)
    cosine = jnp.cos(2.0 * angle)
    sine = jnp.sin(2.0 * angle)
    cosine_ref[...] = cosine
    sine_ref[...] = sine
    pixel_ref[...] = pixel
    cycle = pixel // nphi
    high[...] = (pixel % nphi) // LANES * cycles + cycle
    low[...] = pixel % LANES

    iota = lax.broadcasted_iota(jnp.int32, (LANES, cap), 0)

    def step(index, carry):
        for g in range(GROUP):
            s = index * GROUP + g
            onehot = jnp.where(iota == high[pl.ds(s, 1), :], 1.0, 0.0).astype(jnp.bfloat16)
            onehot = jnp.concatenate([onehot, onehot], axis=0)
            found = jnp.dot(table[...], onehot, preferred_element_type=jnp.float32)
            mask = iota == low[pl.ds(s, 1), :]
            looked = [
                jnp.sum(
                    jnp.where(mask, found[c * LANES : (c + 1) * LANES], 0.0), axis=0, keepdims=True
                )
                for c in range(3)
            ]
            signal_ref[pl.ds(s, 1), :] = (
                looked[0]
                + looked[1] * cosine_ref[pl.ds(s, 1), :]
                + looked[2] * sine_ref[pl.ds(s, 1), :]
            )
        return carry

    lax.fori_loop(0, tiles // GROUP, step, 0)

    signal = signal_ref[...]
    masked = valid * signal
    signal_ref[...] = masked
    data_ref[...] = valid * data
    cross = jnp.sum(masked * data, axis=1, keepdims=True)
    square = jnp.sum(masked * signal, axis=1, keepdims=True)
    width = sums_ref.shape[1]
    row = lax.broadcasted_iota(jnp.int32, (tiles, width), 0)
    lane = lax.broadcasted_iota(jnp.int32, (tiles, width), 1)
    both = jnp.where(lane == row, cross, 0.0) + jnp.where(lane == row + width // 2, square, 0.0)
    both = jnp.sum(both, axis=0, keepdims=True)
    sums_ref[...] = jnp.broadcast_to(both, sums_ref.shape)
    for cy in range(cycles):
        hits = jnp.sum(jnp.where(cycle == cy, valid, 0.0), keepdims=True)
        weight_ref[cy : cy + 1, :] = jnp.broadcast_to(hits / nphi, (1, LANES))


def send_shape(send_ref, second):
    per_device = send_ref.shape[0] // CHUNK
    n_tm = lax.axis_size("tm")
    return n_tm, per_device // n_tm


def bin_kernel(
    sums_ref, data_ref, signal_ref, cosine_ref, sine_ref, pixel_ref, weight_ref,
    stage_a_ref, twiddle_ref, stage_b_ref,
    gain_ref, binned_ref, send_ref,
    acc, weights, high, low, wide, onehot,
):
    tiles, cap = data_ref.shape
    cycles = 2
    second = twiddle_ref.shape[1]
    first = LANES
    nphi = first * second
    n_tm, per_band = send_shape(send_ref, second)
    stride = per_band * CHUNK

    total = jnp.sum(sums_ref[...], axis=0, keepdims=True)
    width = total.shape[1]
    row = lax.broadcasted_iota(jnp.int32, (tiles, width), 0)
    lane = lax.broadcasted_iota(jnp.int32, (tiles, width), 1)
    cross = jnp.sum(jnp.where(lane == row, total, 0.0), axis=1, keepdims=True)
    square = jnp.sum(jnp.where(lane == row + width // 2, total, 0.0), axis=1, keepdims=True)
    gains = cross / (square + 1e-06)
    position = lax.axis_index("det") * n_tm + lax.axis_index("tm")
    place = lax.broadcasted_iota(jnp.int32, (tiles, 1), 0)
    gain_ref[...] = jnp.sum(jnp.where(place == position, gains, 0.0), axis=0, keepdims=True)

    residual = data_ref[...] - gains * signal_ref[...]
    for c, values in enumerate((residual, residual * cosine_ref[...], residual * sine_ref[...])):
        top = values.astype(jnp.bfloat16).astype(jnp.float32)
        weights[2 * c] = top
        weights[2 * c + 1] = values - top
    pixel = pixel_ref[...]
    low[...] = pixel % second
    high[...] = pixel // nphi * first + (pixel // second) % 2 * (first // 2) + (pixel % nphi) // first

    acc[...] = jnp.zeros_like(acc)
    iota_low = lax.broadcasted_iota(jnp.int32, (second, cap), 0)
    iota_high = lax.broadcasted_iota(jnp.int32, (cycles * first, cap), 0)

    def step(index, carry):
        for g in range(GROUP):
            s = index * GROUP + g
            cut = slice(g * cap, (g + 1) * cap)
            mask = iota_low == low[pl.ds(s, 1), :]
            for i in range(6):
                wide[i * second : (i + 1) * second, cut] = jnp.where(
                    mask, weights[i, pl.ds(s, 1), :], 0.0
                ).astype(jnp.bfloat16)
            onehot[:, cut] = jnp.where(iota_high == high[pl.ds(s, 1), :], 1.0, 0.0).astype(
                jnp.bfloat16
            )
        acc[...] += lax.dot_general(
            wide[...], onehot[...], (((1,), (1,)), ((), ())), preferred_element_type=jnp.float32
        )
        return carry

    lax.fori_loop(0, tiles // GROUP, step, 0)

    blocks = []
    for c in range(3):
        at = 2 * c * second
        map_c = acc[at : at + second, :] + acc[at + second : at + 2 * second, :]
        for cy in range(cycles):
            block = map_c[:, cy * first : (cy + 1) * first]
            blocks.append(block)
            flipped = block.T
            binned_ref[c, pl.ds(cy, first // 2, stride=cycles), :] = jnp.concatenate(
                [flipped[: first // 2], flipped[first // 2 :]], axis=1
            )
    field = jnp.concatenate(blocks, axis=0)
    field_high, field_low = split(field)
    modes = jnp.dot(
        jnp.concatenate([field_high, field_low, field_high], axis=1),
        stage_a_ref[...],
        preferred_element_type=jnp.float32,
    )
    turned = []
    for i in range(3 * cycles):
        real = modes[i * second : (i + 1) * second, :first]
        imag = modes[i * second : (i + 1) * second, first:]
        cos_t = twiddle_ref[0]
        sin_t = twiddle_ref[1]
        turned.append(
            jnp.concatenate([real * cos_t - imag * sin_t, real * sin_t + imag * cos_t], axis=0)
        )
    turned = jnp.concatenate(turned, axis=1)
    turned_high, turned_low = split(turned)
    spectrum = jnp.dot(
        stage_b_ref[...],
        jnp.concatenate([turned_high, turned_low, turned_high], axis=0),
        preferred_element_type=jnp.float32,
    )
    half = second // 2
    for c in range(3):
        for cy in range(cycles):
            at = (c * cycles + cy) * first
            for part in range(2):
                for ql in range(per_band):
                    start = part * half + ql * n_tm
                    line = ql * CHUNK + (2 * c + part) * cycles + cy
                    send_ref[pl.ds(line, n_tm, stride=stride), :] = spectrum[
                        start : start + n_tm, at : at + first
                    ]
    for cy in range(cycles):
        weight = jnp.broadcast_to(weight_ref[cy : cy + 1, :], (n_tm, LANES))
        for ql in range(per_band):
            line = ql * CHUNK + PLANES * cycles + cy
            send_ref[pl.ds(line, n_tm, stride=stride), :] = weight
            send_ref[pl.ds(line + cycles, n_tm, stride=stride), :] = jnp.zeros_like(weight)


def rhs_kernel(
    got_ref, prior_ref, noise_ref, draw_ref, rhs_ref, weight_ref, left_ref, right_ref, lines
):
    count = prior_ref.shape[1]
    per_band = prior_ref.shape[2] // LANES
    stride = per_band * CHUNK
    n_tm = got_ref.shape[0] // stride
    cycles = count // n_tm
    for ql in range(per_band):
        cut = slice(ql * LANES, (ql + 1) * LANES)
        for p in range(PLANES + 1):
            for cy in range(cycles):
                lines[p, pl.ds(cy, n_tm, stride=cycles), :] = got_ref[
                    pl.ds(ql * CHUNK + p * cycles + cy, n_tm, stride=stride), :
                ]
        weight = lines[PLANES]
        weight_ref[:, cut] = weight
        root_weight = jnp.sqrt(weight)
        for c in range(3):
            root = jnp.sqrt(prior_ref[c, :, cut])
            for p in (2 * c, 2 * c + 1):
                rhs_ref[p, :, cut] = (
                    lines[p] + root_weight * noise_ref[p, :, cut] + root * draw_ref[p, :, cut]
                )
    for p in range(PLANES):
        left_ref[p] = rhs_ref[p, :8, :]
        right_ref[p] = rhs_ref[p, count - 8 :, :]
    left_ref[PLANES] = weight_ref[:8, :]
    right_ref[PLANES] = weight_ref[count - 8 :, :]


def krylov_kernel(
    rhs_ref, weight_ref, prior_ref, after_ref, prior_after_ref, one_ref, two_ref, sums_ref
):
    count = rhs_ref.shape[1]
    rows = count + 8
    band = rhs_ref.shape[2]
    row = lax.broadcasted_iota(jnp.int32, (rows, band), 0)
    first = lax.axis_index("det") == 0
    counted = (row < count + 3) & ((row >= 3) | first)
    share = jnp.where(counted, 1.0, 0.0)
    top = row == 0
    weight = jnp.concatenate([weight_ref[...], after_ref[PLANES]], axis=0)
    sums = [jnp.zeros((rows, band), jnp.float32) for _ in range(6)]
    for c in range(3):
        precision = jnp.concatenate([prior_ref[c], prior_after_ref[c]], axis=0)
        root = jnp.sqrt(precision)
        diagonal = (precision + weight - SHIFT) * (1.0 / SPREAD)
        beside = root * (COUPLING / SPREAD)

        def apply(field):
            scaled = root * field
            before = jnp.where(top, 0.0, pltpu.roll(scaled, 1, 0))
            after = pltpu.roll(scaled, rows - 1, 0)
            return diagonal * field - beside * (before + after)

        for part in range(2):
            p = 2 * c + part
            zero = jnp.concatenate([rhs_ref[p], after_ref[p]], axis=0)
            one = apply(zero)
            two = apply(one)
            three = apply(two)
            one_ref[p] = one[:count]
            two_ref[p] = two[:count]
            held_zero = share * zero
            held_one = share * one
            held_two = share * two
            for i, term in enumerate(
                (
                    held_zero * zero,
                    held_zero * one,
                    held_one * one,
                    held_one * two,
                    held_two * two,
                    held_two * three,
                )
            ):
                sums[i] = sums[i] + jnp.where(counted, term, 0.0)
    lane = lax.broadcasted_iota(jnp.int32, (1, LANES), 1)
    line = jnp.zeros((1, LANES), jnp.float32)
    for i in range(6):
        line = jnp.where(lane == i, jnp.sum(sums[i], keepdims=True), line)
    sums_ref[...] = jnp.broadcast_to(line, sums_ref.shape)


def inner(left, right, moments):
    result = 0.0
    for i, a in enumerate(left):
        for j, b in enumerate(right):
            result = result + a * b * moments[i + j]
    return result


def operated(coefficients):
    result = [SHIFT * a for a in coefficients] + [0.0]
    for i, a in enumerate(coefficients):
        result[i + 1] = result[i + 1] + SPREAD * a
    return result


def padded(values, length):
    return list(values) + [0.0] * (length - len(values))


def conjugate_gradient(moments):
    resid = [1.0]
    direction = [1.0]
    solution = [0.0]
    norm_now = moments[0]
    for iteration in range(3):
        image = operated(direction)
        alpha = norm_now / inner(direction, image, moments)
        size = len(direction)
        solution = [a + alpha * b for a, b in zip(padded(solution, size), direction)]
        if iteration == 2:
            break
        resid = [a - alpha * b for a, b in zip(padded(resid, size + 1), image)]
        norm_next = inner(resid, resid, moments)
        beta = norm_next / norm_now
        direction = [a + beta * b for a, b in zip(resid, padded(direction, size + 1))]
        norm_now = norm_next
    return solution


def final_kernel(
    sums_ref, rhs_ref, one_ref, two_ref, prior_ref, weight_ref, before_ref, prior_before_ref, out_ref
):
    total = jnp.sum(sums_ref[...], axis=0, keepdims=True)
    moments = [total[:, i : i + 1] for i in range(6)]
    zero_by, one_by, two_by = conjugate_gradient(moments)
    count = rhs_ref.shape[1]
    weight_last = before_ref[PLANES, 7:8, :]
    weight_first = weight_ref[0:1, :]
    beside = COUPLING / SPREAD
    for c in range(3):
        precision_last = prior_before_ref[c, 7:8, :]
        root_far = jnp.sqrt(prior_before_ref[c, 6:7, :])
        root_last = jnp.sqrt(precision_last)
        precision_first = prior_ref[c, 0:1, :]
        root_first = jnp.sqrt(precision_first)
        root_second = jnp.sqrt(prior_ref[c, 1:2, :])
        diagonal_last = (precision_last + weight_last - SHIFT) * (1.0 / SPREAD)
        diagonal_first = (precision_first + weight_first - SHIFT) * (1.0 / SPREAD)
        for part in range(2):
            p = 2 * c + part
            out_ref[p] = zero_by * rhs_ref[p] + one_by * one_ref[p] + two_by * two_ref[p]
            far = before_ref[p, 6:7, :]
            last = before_ref[p, 7:8, :]
            one_last = diagonal_last * last - beside * root_last * (
                root_far * far + root_first * rhs_ref[p, 0:1, :]
            )
            one_first = -beside * root_first * root_last * last
            two_first = diagonal_first * one_first - beside * root_first * root_last * one_last
            two_second = -beside * root_second * root_first * one_first
            out_ref[p, 0:1, :] += one_by * one_first + two_by * two_first
            out_ref[p, 1:2, :] += two_by * two_second


def call(kernel, name, outs, scratch=()):
    return pl.pallas_call(
        kernel,
        out_shape=tuple(jax.ShapeDtypeStruct(shape, dtype) for shape, dtype in outs),
        scratch_shapes=list(scratch),
        compiler_params=pltpu.CompilerParams(vmem_limit_bytes=24 * 2**20),
        name=name,
    )


def exchange(values, axes):
    return lax.all_to_all(values, axes, split_axis=0, concat_axis=0, tiled=True)


def per_device(
    samples, pointing, angles, counts, sky_map, prior_precision, omega_noise, omega_prior
):
    f32, i32, bf16 = jnp.float32, jnp.int32, jnp.bfloat16
    tiles, cap = samples.shape[2:]
    n_det, n_tm = lax.axis_size("det"), lax.axis_size("tm")
    devices = n_det * n_tm
    cycles, nphi = sky_map.shape[1:]
    count, band = prior_precision.shape[1:]
    second = nphi // LANES
    everywhere = ("det", "tm")
    forth = [(i, i + 1) for i in range(n_det - 1)]
    back = [(i + 1, i) for i in range(n_det - 1)]

    packed = call(pack_kernel, "pack", [((tiles * 8, LANES), f32)])(
        samples.reshape(tiles, cap),
        angles.reshape(tiles, cap),
        pointing.reshape(tiles, cap),
        counts.reshape(1, tiles),
    )[0]
    got = exchange(packed.reshape(tiles, 8, LANES), everywhere).reshape(tiles * 8, LANES)
    prior_after = lax.ppermute(prior_precision[:, :8, :], "det", back)
    prior_before = lax.ppermute(prior_precision[:, count - 8 :, :], "det", forth)

    sky = sky_map.reshape(3, cycles, second, LANES).transpose(0, 2, 1, 3)
    sky = sky.reshape(3, second * cycles, LANES)
    width = LANES * -(-2 * tiles // LANES)
    data, signal, cosine, sine, pixel, weight, sums = call(
        lookup_kernel,
        "lookup",
        [((tiles, cap), f32)] * 4 + [((tiles, cap), i32), ((cycles, LANES), f32), ((devices, width), f32)],
        [
            pltpu.VMEM((3 * LANES, 2 * second * cycles), bf16),
            pltpu.VMEM((tiles, cap), i32),
            pltpu.VMEM((tiles, cap), i32),
        ],
    )(got, sky)
    sums = exchange(sums, everywhere)

    stage_a, twiddle, stage_b = dft_tables(nphi, n_tm)
    gain, binned, send = call(
        bin_kernel,
        "bin",
        [((1, 1), f32), ((3, second * cycles, LANES), f32), ((band // LANES * n_tm * CHUNK, LANES), f32)],
        [
            pltpu.VMEM((6 * second, cycles * LANES), f32),
            pltpu.VMEM((6, tiles, cap), f32),
            pltpu.VMEM((tiles, cap), i32),
            pltpu.VMEM((tiles, cap), i32),
            pltpu.VMEM((6 * second, GROUP * cap), bf16),
            pltpu.VMEM((cycles * LANES, GROUP * cap), bf16),
        ],
    )(sums, data, signal, cosine, sine, pixel, weight, stage_a, twiddle, stage_b)
    binned = binned.reshape(3, second, cycles, LANES).transpose(0, 2, 1, 3).reshape(3, cycles, nphi)

    got = exchange(send.reshape(n_tm, -1, LANES), "tm").reshape(-1, LANES)
    rhs, weight, left, right = call(
        rhs_kernel,
        "rhs",
        [((PLANES, count, band), f32), ((count, band), f32)] + [((PLANES + 1, 8, band), f32)] * 2,
        [pltpu.VMEM((PLANES + 1, count, LANES), f32)],
    )(got, prior_precision, omega_noise, omega_prior)
    after = lax.ppermute(left, "det", back)
    before = lax.ppermute(right, "det", forth)
    one, two, sums = call(
        krylov_kernel,
        "krylov",
        [((PLANES, count, band), f32)] * 2 + [((devices, LANES), f32)],
    )(rhs, weight, prior_precision, after, prior_after)
    sums = exchange(sums, everywhere)
    solution = call(final_kernel, "final", [((PLANES, count, band), f32)])(
        sums, rhs, one, two, prior_precision, weight, before, prior_before
    )[0]
    return (gain, binned, solution)


def solution(mesh):
    return jax.shard_map(
        per_device,
        mesh=mesh,
        in_specs=(
            P("det", "tm", None, None),
            P("det", "tm", None, None),
            P("det", "tm", None, None),
            P("det", "tm", None),
            P(None, ("det", "tm"), None),
            P(None, "det", "tm"),
            P(None, "det", "tm"),
            P(None, "det", "tm"),
        ),
        out_specs=(P("det", "tm"), P(None, ("det", "tm"), None), P(None, "det", "tm")),
        check_vma=False,
    )
```

time: 516 us -> 76.8 us (0.15); the launches traced: 506 us -> 76.2 us
  blocking collectives: 241 us -> 36.4 us
  local copies, waits for them, and re-layouts: 106 us -> 2.96 us
  other arithmetic: 78.7 us -> 0 us
  starting transfers between devices: 47 us -> 15.3 us
  waiting for transfers between devices: 22.6 us -> 7.18 us
  Pallas kernels: 0 us -> 13.7 us
  between operations: 8.15 us -> 0.75 us
    psum x6 -> x0, blocking collectives: 241 us -> none  [the longest x3 123 us: squares(): return lax.psum(jnp.sum(vector * vector), ('det', 'tm'))]
    scatter-add x1 -> x0, other arithmetic: 48.2 us -> none  [per_device(): jnp.zeros((3, pixels), jnp.float32).at[:, pixel_index.reshape(-1)]]
    unnamed x19 -> x22, local copies, waits for them, and re-layouts: 43.1 us -> 2.95 us
    all_to_all x0 -> x3, blocking collectives: none -> 36.4 us  [exchange(): return lax.all_to_all(values, axes, split_axis=0, concat_axis=0, tiled=True)]
    gather x2 -> x0, local copies, waits for them, and re-layouts: 33.9 us -> none  [per_device(): looked = sky_flat[:, pixel_index]]
    all_to_all x6 -> x1, starting transfers between devices: 30.5 us -> 3.57 us  [exchange(): return lax.all_to_all(values, axes, split_axis=0, concat_axis=0, tiled=True)]
    unnamed x2 -> x0, other arithmetic: 19.5 us -> none
    pallas_call x0 -> x6, Pallas kernels: none -> 13.7 us  [the longest x1 6.16 us: per_device(): call(bin_kernel, 'bin', [((1, 1), f32), ((3, second * cycles, LANES), f32...]
  transfers between devices with their start and end apart: 12 -> 5, of which waited for: 7 -> 2; matrix products, arithmetic and copies ran while one was open for 14% -> 0% of each run, Pallas kernels for 0% -> 2%
where the time goes in v1:
time: 76.8 us; the launch traced here: 76.2 us
  blocking collectives  36.4 us (47%)
  starting transfers between devices  15.3 us (20%)
  Pallas kernels  13.7 us (18%)
  waiting for transfers between devices  7.18 us (9%)
  local copies, waits for them, and re-layouts  2.96 us (4%)
    all_to_all x3, blocking collectives, exchange(): return lax.all_to_all(values, axes, split_axis=0, concat_axis=0, tiled=True)  36.4 us
    all_to_all x1, waiting for transfers between devices, exchange(): return lax.all_to_all(values, axes, split_axis=0, concat_axis=0, tiled=True)  7.05 us
    pallas_call x1, Pallas kernels, per_device(): call(bin_kernel, 'bin', [((1, 1), f32), ((3, second * cycles, LANES), f32...  6.16 us
    pallas_call x1, Pallas kernels, per_device(): call(lookup_kernel, 'lookup', [((tiles, cap), f32)] * 4 + [((tiles, cap),...  4.99 us
    ppermute x1, starting transfers between devices, per_device(): before = lax.ppermute(right, 'det', forth)  4.55 us
    ppermute x1, starting transfers between devices, per_device(): prior_before = lax.ppermute(prior_precision[:, count - 8:, :], 'det', forth)  4.55 us
    all_to_all x1, starting transfers between devices, exchange(): return lax.all_to_all(values, axes, split_axis=0, concat_axis=0, tiled=True)  3.57 us
    unnamed x22, local copies, waits for them, and re-layouts  2.95 us
  transfers between devices with their start and end apart: 5, of which 2 were waited for; matrix products, arithmetic and copies ran while one was open for 0% of the time, Pallas kernels for 2%

profile of v1, /device:TPU:0, one launch (start us, length us, event | category | flops | bytes accessed | tf_op | source)
XLA Modules:
  0.0 76.2 jit_solution(7682507553504827508)
XLA Ops:
  0.6 0.0 copy-start.10
  0.6 0.6 copy-done.10
  1.3 0.0 copy-start.7
  1.3 0.8 copy-done.7
  2.0 0.0 copy-start.8
  2.0 0.8 copy-done.8
  2.8 0.0 copy-start.9
  2.8 0.8 copy-done.9
  3.6 0.0 copy-start.1
  3.6 0.1 pack.1
  3.6 15.3 %all_to_all.32 = f32[32,8,128]{2,1,0:T(8,128)S(1)} all-to-all(f32[32,8,128]{2,1,0:T(8,128)S(1)} %bitcast.27), channel_id=1, replica_groups=mesh['det'=4,'tm'=8] {'det','tm'}, dimensions={0} | all-to-all | bytes 262144 | tf_op jit(solution)/shard_map/all_to_all | solution.py:437
  18.9 0.0 copy-start.4
  18.9 0.0 copy-done.1
  18.9 0.0 copy-start.5
  18.9 5.0 %lookup.1 = (f32[32,256]{1,0:T(8,128)S(1)}, f32[32,256]{1,0:T(8,128)S(1)}, f32[32,256]{1,0:T(8,128)S(1)}, f32[32,256]{1,0:T(8,128)S(1)}, s32[32,256]{1,0:T(8,128...) custom-call(f32[256,128]{1,0:T(8,128)S(1)} %bitcast.28, f32[3,128,128]{2,1,0:T(8,128)S(1)} %bitcast.30), custom_call_target="tpu_custom_call" | custom-call | tf_op jit(solution)/shard_map/lookup/pallas_call | solution.py:467
  23.9 0.0 copy-start.6
  23.9 8.9 %all_to_all.33 = f32[32,1,128]{2,1,0:T(1,128)S(1)} all-to-all(f32[32,1,128]{2,1,0:T(1,128)S(1)} %bitcast.36), channel_id=1, replica_groups=mesh['det'=4,'tm'=8] {'det','tm'}, dimensions={0} | all-to-all | bytes 32768 | tf_op jit(solution)/shard_map/all_to_all | solution.py:437
  32.8 0.0 copy-done.4
  32.8 0.0 copy-done.5
  32.8 0.0 copy-done.6
  32.8 6.2 %bin.1 = (f32[1,1]{1,0:T(1,128)}, f32[3,128,128]{2,1,0:T(8,128)}, f32[512,128]{1,0:T(8,128)S(1)}) custom-call(f32[32,128]{1,0:T(8,128)S(1)} %bitcast.32, f32[32,256]{1,0:T(8,128)S(1)} %get-tuple-element.21.data_ref, f32[32,256]{1,0:T(8,128)S(1)} %get-tuple-element.22.signal_ref, f32[32,256]{1,0:T(8,128)S(1)} %get-tuple-element.23.cosine_ref, ...), custom_call_target="tpu_custom_call" | custom-call | tf_op jit(solution)/shard_map/bin/pallas_call | solution.py:480
  39.0 0.0 copy-start
  39.0 0.0 copy-start.2
  39.0 0.0 copy-start.3
  39.0 12.3 %all_to_all.34 = f32[8,64,128]{2,1,0:T(8,128)S(1)} all-to-all(f32[8,64,128]{2,1,0:T(8,128)S(1)} %bitcast.29), channel_id=1, replica_groups=mesh['det'=4,'tm'=8] {'tm'}, dimensions={0} | all-to-all | bytes 524288 | tf_op jit(solution)/shard_map/all_to_all | solution.py:437
  51.2 0.0 copy-done
  51.2 0.0 copy-done.2
  51.2 0.0 copy-done.3
  51.2 0.2 rhs.1
  51.5 1.3 %collective-permute-start = (f32[7,8,512]{2,1,0:T(8,128)S(1)}, f32[7,8,512]{2,1,0:T(8,128)S(1)}, u32[]{:S(2)}, u32[]{:S(2)}) collective-permute-start(f32[7,8,512]{2,1,0:T(8,128)S(1)} %get-tuple-element.32), channel_id=1, source_target_pairs={{8,0},{16,8},{24,16},{9,1},{17,9},{25,17},{10,2},{18,10},{26,18},{... | collective-permute-start | bytes 344072 | tf_op jit(solution)/shard_map/ppermute | solution.py:502
  52.8 4.6 %collective-permute-start.2 = (f32[7,8,512]{2,1,0:T(8,128)S(1)}, f32[7,8,512]{2,1,0:T(8,128)S(1)}, u32[]{:S(2)}, u32[]{:S(2)}) collective-permute-start(f32[7,8,512]{2,1,0:T(8,128)S(1)} %get-tuple-element.36), channel_id=1, source_target_pairs={{0,8},{8,16},{16,24},{1,9},{9,17},{17,25},{2,10},{10,18},{18,26},{... | collective-permute-start | bytes 344072 | tf_op jit(solution)/shard_map/ppermute | solution.py:503
  57.3 1.3 %collective-permute-start.1 = (f32[3,8,512]{2,1,0:T(8,128)S(1)}, f32[3,8,512]{2,1,0:T(8,128)S(1)}, u32[]{:S(2)}, u32[]{:S(2)}) collective-permute-start(f32[3,8,512]{2,1,0:T(8,128)S(1)} %get-tuple-element.38), channel_id=1, source_target_pairs={{8,0},{16,8},{24,16},{9,1},{17,9},{25,17},{10,2},{18,10},{26,18},{... | collective-permute-start | bytes 147464 | tf_op jit(solution)/shard_map/ppermute | solution.py:461
  58.6 4.5 %collective-permute-start.3 = (f32[3,8,512]{2,1,0:T(8,128)S(1)}, f32[3,8,512]{2,1,0:T(8,128)S(1)}, u32[]{:S(2)}, u32[]{:S(2)}) collective-permute-start(f32[3,8,512]{2,1,0:T(8,128)S(1)} %get-tuple-element.37), channel_id=1, source_target_pairs={{0,8},{8,16},{16,24},{1,9},{9,17},{17,25},{2,10},{10,18},{18,26},{... | collective-permute-start | bytes 147464 | tf_op jit(solution)/shard_map/ppermute | solution.py:462
  63.2 0.1 collective-permute-done.1.prior_after_ref
  63.3 0.0 collective-permute-done.after_ref
  63.3 1.3 %krylov.1 = (f32[6,16,512]{2,1,0:T(8,128)S(1)}, f32[6,16,512]{2,1,0:T(8,128)S(1)}, f32[32,128]{1,0:T(8,128)}) custom-call(f32[6,16,512]{2,1,0:T(8,128)S(1)} %get-tuple-element.30.rhs_ref, f32[16,512]{1,0:T(8,128)S(1)} %get-tuple-element.31.weight_ref, f32[3,16,512]{2,1,0:T(8,128)S(1)} %copy-done, f32[7,8,512]{2,1,0:T(8,128)S(1)} %collective-permute-done.after_ref, ...), custom_call_target="tpu_custom_call" | custom-call | tf_op jit(solution)/shard_map/krylov/pallas_call | solution.py:504
  64.6 3.6 %all-to-all-start.3 = ((f32[32,1,128]{2,1,0:T(1,128)}), f32[32,1,128]{2,1,0:T(1,128)S(1)}, u32[]{:S(2)}, u32[]{:S(2)}) async-start(f32[32,1,128]{2,1,0:T(1,128)} %bitcast.18), calls=%async_computation.3 | async-start | bytes 32768 | tf_op jit(solution)/shard_map/all_to_all | solution.py:437
  68.2 0.0 collective-permute-done.3.prior_before_ref
  68.2 0.0 collective-permute-done.2.before_ref
  68.2 7.0 %all-to-all-done.3 = f32[32,1,128]{2,1,0:T(1,128)S(1)} async-done(((f32[32,1,128]{2,1,0:T(1,128)}), f32[32,1,128]{2,1,0:T(1,128)S(1)}, u32[]{:S(2)}, u32[]{:S(2)}) %all-to-all-start.3) | async-done | bytes 16416 | tf_op jit(solution)/shard_map/all_to_all | solution.py:437
  75.3 0.9 %final.1 = f32[6,16,512]{2,1,0:T(8,128)} custom-call(f32[32,128]{1,0:T(8,128)S(1)} %bitcast.31, f32[6,16,512]{2,1,0:T(8,128)S(1)} %get-tuple-element.30.rhs_ref, f32[6,16,512]{2,1,0:T(8,128)S(1)} %get-tuple-element.34.one_ref, f32[6,16,512]{2,1,0:T(8,128)S(1)} %get-tuple-element.35.two_ref, f32[3,16,512]{2,1,0:T(8,128)S(1)} %copy-done, ...), custom_call_target="tpu_custom_call" | custom-call | tf_op jit(solution)/shard_map/final/pallas_call | solution.py:510
  (1 shorter events, 0.0 us)
Async XLA Ops:
  0.6 0.7 copy-start.10
  1.3 0.8 copy-start.7
  2.0 0.8 copy-start.8
  2.8 0.8 copy-start.9
  3.6 15.4 %copy-start.1 = (f32[3,2,8192]{2,1,0:T(2,128)S(1)}, f32[3,2,8192]{2,1,0:T(2,128)}, u32[]{:S(2)}) copy-start(f32[3,2,8192]{2,1,0:T(2,128)} %param.15) | copy-start | bytes 589828
  18.9 13.9 %copy-start.4 = (bf16[384,256]{1,0:T(8,128)(2,1)S(1)}, bf16[384,256]{1,0:T(8,128)(2,1)}, u32[]{:S(2)}) copy-start(bf16[384,256]{1,0:T(8,128)(2,1)} %constant.6.clone.stage_a_ref) | copy-start | bytes 589828
  18.9 13.9 %copy-start.5 = (f32[2,64,128]{2,1,0:T(8,128)S(1)}, f32[2,64,128]{2,1,0:T(8,128)}, u32[]{:S(2)}) copy-start(f32[2,64,128]{2,1,0:T(8,128)} %constant.7.clone.twiddle_ref) | copy-start | bytes 196612
  23.9 8.9 %copy-start.6 = (bf16[64,384]{1,0:T(8,128)(2,1)S(1)}, bf16[64,384]{1,0:T(8,128)(2,1)}, u32[]{:S(2)}) copy-start(bf16[64,384]{1,0:T(8,128)(2,1)} %constant.8.clone.stage_b_ref) | copy-start | bytes 147460
  39.0 12.3 %copy-start = (f32[3,16,512]{2,1,0:T(8,128)S(1)}, f32[3,16,512]{2,1,0:T(8,128)}, u32[]{:S(2)}) copy-start(f32[3,16,512]{2,1,0:T(8,128)} %prior_ref.5) | copy-start | bytes 294916
  39.0 12.3 %copy-start.2 = (f32[6,16,512]{2,1,0:T(8,128)S(1)}, f32[6,16,512]{2,1,0:T(8,128)}, u32[]{:S(2)}) copy-start(f32[6,16,512]{2,1,0:T(8,128)} %noise_ref.1) | copy-start | bytes 589828
  39.0 12.3 %copy-start.3 = (f32[6,16,512]{2,1,0:T(8,128)S(1)}, f32[6,16,512]{2,1,0:T(8,128)}, u32[]{:S(2)}) copy-start(f32[6,16,512]{2,1,0:T(8,128)} %draw_ref.1) | copy-start | bytes 589828
  51.5 11.9 %collective-permute-start = (f32[7,8,512]{2,1,0:T(8,128)S(1)}, f32[7,8,512]{2,1,0:T(8,128)S(1)}, u32[]{:S(2)}, u32[]{:S(2)}) collective-permute-start(f32[7,8,512]{2,1,0:T(8,128)S(1)} %get-tuple-element.32), channel_id=1, source_target_pairs={{8,0},{16,8},{24,16},{9,1},{17,9},{25,17},{10,2},{18,10},{26,18},{... | collective-permute-start | bytes 344072 | tf_op jit(solution)/shard_map/ppermute | solution.py:502
  52.8 15.5 %collective-permute-start.2 = (f32[7,8,512]{2,1,0:T(8,128)S(1)}, f32[7,8,512]{2,1,0:T(8,128)S(1)}, u32[]{:S(2)}, u32[]{:S(2)}) collective-permute-start(f32[7,8,512]{2,1,0:T(8,128)S(1)} %get-tuple-element.36), channel_id=1, source_target_pairs={{0,8},{8,16},{16,24},{1,9},{9,17},{17,25},{2,10},{10,18},{18,26},{... | collective-permute-start | bytes 344072 | tf_op jit(solution)/shard_map/ppermute | solution.py:503
  57.3 6.0 %collective-permute-start.1 = (f32[3,8,512]{2,1,0:T(8,128)S(1)}, f32[3,8,512]{2,1,0:T(8,128)S(1)}, u32[]{:S(2)}, u32[]{:S(2)}) collective-permute-start(f32[3,8,512]{2,1,0:T(8,128)S(1)} %get-tuple-element.38), channel_id=1, source_target_pairs={{8,0},{16,8},{24,16},{9,1},{17,9},{25,17},{10,2},{18,10},{26,18},{... | collective-permute-start | bytes 147464 | tf_op jit(solution)/shard_map/ppermute | solution.py:461
  58.6 9.6 %collective-permute-start.3 = (f32[3,8,512]{2,1,0:T(8,128)S(1)}, f32[3,8,512]{2,1,0:T(8,128)S(1)}, u32[]{:S(2)}, u32[]{:S(2)}) collective-permute-start(f32[3,8,512]{2,1,0:T(8,128)S(1)} %get-tuple-element.37), channel_id=1, source_target_pairs={{0,8},{8,16},{16,24},{1,9},{9,17},{17,25},{2,10},{10,18},{18,26},{... | collective-permute-start | bytes 147464 | tf_op jit(solution)/shard_map/ppermute | solution.py:462
  64.6 10.6 %all-to-all-start.3 = ((f32[32,1,128]{2,1,0:T(1,128)}), f32[32,1,128]{2,1,0:T(1,128)S(1)}, u32[]{:S(2)}, u32[]{:S(2)}) async-start(f32[32,1,128]{2,1,0:T(1,128)} %bitcast.18), calls=%async_computation.3 | async-start | bytes 32768 | tf_op jit(solution)/shard_map/all_to_all | solution.py:437

commit v2 on v1

--- a/solution.py
+++ b/solution.py
@@ -14,9 +14,10 @@
 COUPLING = 0.45
 
 LANES = 128
-GROUP = 2
+GROUP = 16
 PLANES = 6
-CHUNK = 16
+HALO = 3
+BLOCK = 8
 
 
 def split_np(table):
@@ -55,7 +56,25 @@
     return stage_a, twiddle, stage_b
 
 
-def pack_kernel(samples_ref, angles_ref, pointing_ref, counts_ref, out_ref):
+def pack_kernel(
+    samples_hbm, angles_hbm, pointing_hbm, counts_hbm, out_ref,
+    samples_ref, angles_ref, pointing_ref, counts_ref, sems,
+):
+    copies = [
+        pltpu.make_async_copy(source, target, sems.at[i])
+        for i, (source, target) in enumerate(
+            (
+                (samples_hbm, samples_ref),
+                (angles_hbm, angles_ref),
+                (pointing_hbm, pointing_ref),
+                (counts_hbm, counts_ref),
+            )
+        )
+    ]
+    for copy in copies:
+        copy.start()
+    for copy in copies:
+        copy.wait()
     tiles = samples_ref.shape[0]
     halves = samples_ref.shape[1] // LANES
     for h in range(halves):
@@ -73,7 +92,7 @@
 
 
 def lookup_kernel(
-    got_ref, sky_ref, data_ref, signal_ref, cosine_ref, sine_ref, pixel_ref, weight_ref, sums_ref,
+    got_ref, sky_ref, data_ref, signal_ref, cosine_ref, sine_ref, pixel_ref, sums_ref,
     table, high, low,
 ):
     tiles = got_ref.shape[0] // 8
@@ -141,24 +160,19 @@
     width = sums_ref.shape[1]
     row = lax.broadcasted_iota(jnp.int32, (tiles, width), 0)
     lane = lax.broadcasted_iota(jnp.int32, (tiles, width), 1)
-    both = jnp.where(lane == row, cross, 0.0) + jnp.where(lane == row + width // 2, square, 0.0)
-    both = jnp.sum(both, axis=0, keepdims=True)
-    sums_ref[...] = jnp.broadcast_to(both, sums_ref.shape)
+    both = jnp.where(lane == row, cross, 0.0) + jnp.where(lane == row + tiles, square, 0.0)
+    line = jnp.sum(both, axis=0, keepdims=True)
+    lane = lax.broadcasted_iota(jnp.int32, (1, width), 1)
     for cy in range(cycles):
         hits = jnp.sum(jnp.where(cycle == cy, valid, 0.0), keepdims=True)
-        weight_ref[cy : cy + 1, :] = jnp.broadcast_to(hits / nphi, (1, LANES))
-
-
-def send_shape(send_ref, second):
-    per_device = send_ref.shape[0] // CHUNK
-    n_tm = lax.axis_size("tm")
-    return n_tm, per_device // n_tm
+        line = jnp.where(lane == 2 * tiles + cy, hits / nphi, line)
+    sums_ref[...] = jnp.broadcast_to(line, sums_ref.shape)
 
 
 def bin_kernel(
-    sums_ref, data_ref, signal_ref, cosine_ref, sine_ref, pixel_ref, weight_ref,
+    sums_ref, data_ref, signal_ref, cosine_ref, sine_ref, pixel_ref,
     stage_a_ref, twiddle_ref, stage_b_ref,
-    gain_ref, binned_ref, send_ref,
+    gain_ref, binned_ref, weight_ref, send_ref,
     acc, weights, high, low, wide, onehot,
 ):
     tiles, cap = data_ref.shape
@@ -166,16 +180,24 @@
     second = twiddle_ref.shape[1]
     first = LANES
     nphi = first * second
-    n_tm, per_band = send_shape(send_ref, second)
-    stride = per_band * CHUNK
+    n_tm = lax.axis_size("tm")
+    lines = PLANES * cycles
+    stride = send_ref.shape[0] // n_tm
+    per_band = stride // lines
 
     total = jnp.sum(sums_ref[...], axis=0, keepdims=True)
     width = total.shape[1]
     row = lax.broadcasted_iota(jnp.int32, (tiles, width), 0)
     lane = lax.broadcasted_iota(jnp.int32, (tiles, width), 1)
     cross = jnp.sum(jnp.where(lane == row, total, 0.0), axis=1, keepdims=True)
-    square = jnp.sum(jnp.where(lane == row + width // 2, total, 0.0), axis=1, keepdims=True)
+    square = jnp.sum(jnp.where(lane == row + tiles, total, 0.0), axis=1, keepdims=True)
     gains = cross / (square + 1e-06)
+    for cy in range(cycles):
+        at = 2 * tiles + cy
+        weight_ref[pl.ds(cy, tiles, stride=cycles), :] = jnp.broadcast_to(
+            sums_ref[:, at : at + 1], (tiles, LANES)
+        )
+    weight_ref[tiles * cycles :, :] = jnp.zeros((8, LANES), jnp.float32)
     position = lax.axis_index("det") * n_tm + lax.axis_index("tm")
     place = lax.broadcasted_iota(jnp.int32, (tiles, 1), 0)
     gain_ref[...] = jnp.sum(jnp.where(place == position, gains, 0.0), axis=0, keepdims=True)
@@ -253,100 +275,116 @@
             for part in range(2):
                 for ql in range(per_band):
                     start = part * half + ql * n_tm
-                    line = ql * CHUNK + (2 * c + part) * cycles + cy
+                    line = ql * lines + (2 * c + part) * cycles + cy
                     send_ref[pl.ds(line, n_tm, stride=stride), :] = spectrum[
                         start : start + n_tm, at : at + first
                     ]
-    for cy in range(cycles):
-        weight = jnp.broadcast_to(weight_ref[cy : cy + 1, :], (n_tm, LANES))
-        for ql in range(per_band):
-            line = ql * CHUNK + PLANES * cycles + cy
-            send_ref[pl.ds(line, n_tm, stride=stride), :] = weight
-            send_ref[pl.ds(line + cycles, n_tm, stride=stride), :] = jnp.zeros_like(weight)
 
 
 def rhs_kernel(
-    got_ref, prior_ref, noise_ref, draw_ref, rhs_ref, weight_ref, left_ref, right_ref, lines
+    got_ref, weights_ref, prior_ref, noise_ref, draw_ref, rhs_ref, one_ref, two_ref, lines
 ):
     count = prior_ref.shape[1]
     per_band = prior_ref.shape[2] // LANES
-    stride = per_band * CHUNK
-    n_tm = got_ref.shape[0] // stride
+    n_tm = lax.axis_size("tm")
     cycles = count // n_tm
+    each = PLANES * cycles
+    stride = per_band * each
+    start = pl.multiple_of(lax.axis_index("det") * count, 8)
+    root_weight = jnp.sqrt(weights_ref[pl.ds(start, count), :])
     for ql in range(per_band):
         cut = slice(ql * LANES, (ql + 1) * LANES)
-        for p in range(PLANES + 1):
+        for p in range(PLANES):
             for cy in range(cycles):
                 lines[p, pl.ds(cy, n_tm, stride=cycles), :] = got_ref[
-                    pl.ds(ql * CHUNK + p * cycles + cy, n_tm, stride=stride), :
+                    pl.ds(ql * each + p * cycles + cy, n_tm, stride=stride), :
                 ]
-        weight = lines[PLANES]
-        weight_ref[:, cut] = weight
-        root_weight = jnp.sqrt(weight)
         for c in range(3):
             root = jnp.sqrt(prior_ref[c, :, cut])
             for p in (2 * c, 2 * c + 1):
                 rhs_ref[p, :, cut] = (
                     lines[p] + root_weight * noise_ref[p, :, cut] + root * draw_ref[p, :, cut]
                 )
-    for p in range(PLANES):
-        left_ref[p] = rhs_ref[p, :8, :]
-        right_ref[p] = rhs_ref[p, count - 8 :, :]
-    left_ref[PLANES] = weight_ref[:8, :]
-    right_ref[PLANES] = weight_ref[count - 8 :, :]
+    even = lax.axis_index("det") % 2 == 0
+    for ref in (one_ref, two_ref):
+        ref[(PLANES + 3) * HALO :, :] = jnp.zeros_like(ref[(PLANES + 3) * HALO :, :])
+    for p in range(PLANES + 3):
+        source = rhs_ref.at[p] if p < PLANES else prior_ref.at[p - PLANES]
+        head = source[:HALO, :]
+        tail = source[count - HALO :, :]
+        one_ref[p * HALO : (p + 1) * HALO, :] = jnp.where(even, tail, head)
+        two_ref[p * HALO : (p + 1) * HALO, :] = jnp.where(even, head, tail)
 
 
 def krylov_kernel(
-    rhs_ref, weight_ref, prior_ref, after_ref, prior_after_ref, one_ref, two_ref, sums_ref
+    rhs_ref, weights_ref, prior_ref, from_one_ref, from_two_ref, one_ref, two_ref, sums_ref, wide
 ):
     count = rhs_ref.shape[1]
-    rows = count + 8
+    rows = count + BLOCK
     band = rhs_ref.shape[2]
-    row = lax.broadcasted_iota(jnp.int32, (rows, band), 0)
-    first = lax.axis_index("det") == 0
-    counted = (row < count + 3) & ((row >= 3) | first)
-    share = jnp.where(counted, 1.0, 0.0)
-    top = row == 0
-    weight = jnp.concatenate([weight_ref[...], after_ref[PLANES]], axis=0)
+    group = lax.axis_index("det")
+    even = group % 2 == 0
+    has_before = group > 0
+    has_after = group < lax.axis_size("det") - 1
+    own = lax.broadcasted_iota(jnp.int32, (rows, band), 0) < count
+    start = pl.multiple_of(group * count, BLOCK)
+    before = pl.multiple_of(jnp.maximum(start - BLOCK, 0), BLOCK)
+    place = lax.broadcasted_iota(jnp.int32, (BLOCK, LANES), 0)
+    beyond = jnp.where(
+        place < BLOCK - HALO,
+        weights_ref[pl.ds(start + count, BLOCK), :],
+        weights_ref[pl.ds(before, BLOCK), :],
+    )
+    weight = jnp.concatenate([weights_ref[pl.ds(start, count), :], beyond], axis=0)
+    weight = jnp.concatenate([weight] * (band // LANES), axis=1)
     sums = [jnp.zeros((rows, band), jnp.float32) for _ in range(6)]
+
+    def extended(values, p):
+        here = slice(p * HALO, (p + 1) * HALO)
+        one, two = from_one_ref[here, :], from_two_ref[here, :]
+        wide[:count, :] = values
+        wide[count : count + HALO, :] = jnp.where(has_after, jnp.where(even, one, two), 0.0)
+        wide[rows - HALO :, :] = jnp.where(has_before, jnp.where(even, two, one), 0.0)
+        return wide[...]
+
+    wide[count:, :] = jnp.zeros((BLOCK, band), jnp.float32)
     for c in range(3):
-        precision = jnp.concatenate([prior_ref[c], prior_after_ref[c]], axis=0)
+        precision = extended(prior_ref[c], PLANES + c)
         root = jnp.sqrt(precision)
         diagonal = (precision + weight - SHIFT) * (1.0 / SPREAD)
         beside = root * (COUPLING / SPREAD)
 
         def apply(field):
             scaled = root * field
-            before = jnp.where(top, 0.0, pltpu.roll(scaled, 1, 0))
-            after = pltpu.roll(scaled, rows - 1, 0)
-            return diagonal * field - beside * (before + after)
+            return diagonal * field - beside * (
+                pltpu.roll(scaled, 1, 0) + pltpu.roll(scaled, rows - 1, 0)
+            )
 
         for part in range(2):
             p = 2 * c + part
-            zero = jnp.concatenate([rhs_ref[p], after_ref[p]], axis=0)
+            zero = extended(rhs_ref[p], p)
             one = apply(zero)
             two = apply(one)
-            three = apply(two)
             one_ref[p] = one[:count]
             two_ref[p] = two[:count]
-            held_zero = share * zero
-            held_one = share * one
-            held_two = share * two
+            scaled = root * two
+            pair = scaled * pltpu.roll(scaled, rows - 1, 0)
             for i, term in enumerate(
                 (
-                    held_zero * zero,
-                    held_zero * one,
-                    held_one * one,
-                    held_one * two,
-                    held_two * two,
-                    held_two * three,
+                    zero * zero,
+                    zero * one,
+                    one * one,
+                    one * two,
+                    two * two,
+                    diagonal * two * two - (2.0 * COUPLING / SPREAD) * pair,
                 )
             ):
-                sums[i] = sums[i] + jnp.where(counted, term, 0.0)
+                sums[i] = sums[i] + term
     lane = lax.broadcasted_iota(jnp.int32, (1, LANES), 1)
     line = jnp.zeros((1, LANES), jnp.float32)
     for i in range(6):
-        line = jnp.where(lane == i, jnp.sum(sums[i], keepdims=True), line)
+        part = jnp.sum(jnp.where(own, sums[i], 0.0), keepdims=True)
+        line = jnp.where(lane == i, part, line)
     sums_ref[...] = jnp.broadcast_to(line, sums_ref.shape)
 
 
@@ -389,47 +427,23 @@
     return solution
 
 
-def final_kernel(
-    sums_ref, rhs_ref, one_ref, two_ref, prior_ref, weight_ref, before_ref, prior_before_ref, out_ref
-):
+def final_kernel(sums_ref, rhs_ref, one_ref, two_ref, out_ref):
     total = jnp.sum(sums_ref[...], axis=0, keepdims=True)
     moments = [total[:, i : i + 1] for i in range(6)]
     zero_by, one_by, two_by = conjugate_gradient(moments)
-    count = rhs_ref.shape[1]
-    weight_last = before_ref[PLANES, 7:8, :]
-    weight_first = weight_ref[0:1, :]
-    beside = COUPLING / SPREAD
-    for c in range(3):
-        precision_last = prior_before_ref[c, 7:8, :]
-        root_far = jnp.sqrt(prior_before_ref[c, 6:7, :])
-        root_last = jnp.sqrt(precision_last)
-        precision_first = prior_ref[c, 0:1, :]
-        root_first = jnp.sqrt(precision_first)
-        root_second = jnp.sqrt(prior_ref[c, 1:2, :])
-        diagonal_last = (precision_last + weight_last - SHIFT) * (1.0 / SPREAD)
-        diagonal_first = (precision_first + weight_first - SHIFT) * (1.0 / SPREAD)
-        for part in range(2):
-            p = 2 * c + part
-            out_ref[p] = zero_by * rhs_ref[p] + one_by * one_ref[p] + two_by * two_ref[p]
-            far = before_ref[p, 6:7, :]
-            last = before_ref[p, 7:8, :]
-            one_last = diagonal_last * last - beside * root_last * (
-                root_far * far + root_first * rhs_ref[p, 0:1, :]
-            )
-            one_first = -beside * root_first * root_last * last
-            two_first = diagonal_first * one_first - beside * root_first * root_last * one_last
-            two_second = -beside * root_second * root_first * one_first
-            out_ref[p, 0:1, :] += one_by * one_first + two_by * two_first
-            out_ref[p, 1:2, :] += two_by * two_second
-
-
-def call(kernel, name, outs, scratch=()):
+    for p in range(PLANES):
+        out_ref[p] = zero_by * rhs_ref[p] + one_by * one_ref[p] + two_by * two_ref[p]
+
+
+def call(kernel, name, outs, scratch=(), in_specs=None, limit=24):
+    extra = {} if in_specs is None else {"in_specs": in_specs}
     return pl.pallas_call(
         kernel,
         out_shape=tuple(jax.ShapeDtypeStruct(shape, dtype) for shape, dtype in outs),
         scratch_shapes=list(scratch),
-        compiler_params=pltpu.CompilerParams(vmem_limit_bytes=24 * 2**20),
+        compiler_params=pltpu.CompilerParams(vmem_limit_bytes=limit * 2**20),
         name=name,
+        **extra,
     )
 
 
@@ -448,26 +462,37 @@
     count, band = prior_precision.shape[1:]
     second = nphi // LANES
     everywhere = ("det", "tm")
-    forth = [(i, i + 1) for i in range(n_det - 1)]
-    back = [(i + 1, i) for i in range(n_det - 1)]
-
-    packed = call(pack_kernel, "pack", [((tiles * 8, LANES), f32)])(
+    pairs = [(i, i ^ 1) for i in range(n_det)]
+    others = [(i, (i + 1 if i % 2 else i - 1) % n_det) for i in range(n_det)]
+
+    packed = call(
+        pack_kernel,
+        "pack",
+        [((tiles * 8, LANES), f32)],
+        [
+            pltpu.VMEM((tiles, cap), f32),
+            pltpu.VMEM((tiles, cap), f32),
+            pltpu.VMEM((tiles, cap), i32),
+            pltpu.VMEM((1, tiles), i32),
+            pltpu.SemaphoreType.DMA((4,)),
+        ],
+        [pl.BlockSpec(memory_space=pltpu.HBM)] * 4,
+        60,
+    )(
         samples.reshape(tiles, cap),
         angles.reshape(tiles, cap),
         pointing.reshape(tiles, cap),
         counts.reshape(1, tiles),
     )[0]
     got = exchange(packed.reshape(tiles, 8, LANES), everywhere).reshape(tiles * 8, LANES)
-    prior_after = lax.ppermute(prior_precision[:, :8, :], "det", back)
-    prior_before = lax.ppermute(prior_precision[:, count - 8 :, :], "det", forth)
 
     sky = sky_map.reshape(3, cycles, second, LANES).transpose(0, 2, 1, 3)
     sky = sky.reshape(3, second * cycles, LANES)
-    width = LANES * -(-2 * tiles // LANES)
-    data, signal, cosine, sine, pixel, weight, sums = call(
+    width = LANES * -(-(2 * tiles + cycles) // LANES)
+    data, signal, cosine, sine, pixel, sums = call(
         lookup_kernel,
         "lookup",
-        [((tiles, cap), f32)] * 4 + [((tiles, cap), i32), ((cycles, LANES), f32), ((devices, width), f32)],
+        [((tiles, cap), f32)] * 4 + [((tiles, cap), i32), ((devices, width), f32)],
         [
             pltpu.VMEM((3 * LANES, 2 * second * cycles), bf16),
             pltpu.VMEM((tiles, cap), i32),
@@ -477,10 +502,15 @@
     sums = exchange(sums, everywhere)
 
     stage_a, twiddle, stage_b = dft_tables(nphi, n_tm)
-    gain, binned, send = call(
+    gain, binned, weights, send = call(
         bin_kernel,
         "bin",
-        [((1, 1), f32), ((3, second * cycles, LANES), f32), ((band // LANES * n_tm * CHUNK, LANES), f32)],
+        [
+            ((1, 1), f32),
+            ((3, second * cycles, LANES), f32),
+            ((tiles * cycles + 8, LANES), f32),
+            ((PLANES * cycles * n_tm * band // LANES, LANES), f32),
+        ],
         [
             pltpu.VMEM((6 * second, cycles * LANES), f32),
             pltpu.VMEM((6, tiles, cap), f32),
@@ -489,27 +519,27 @@
             pltpu.VMEM((6 * second, GROUP * cap), bf16),
             pltpu.VMEM((cycles * LANES, GROUP * cap), bf16),
         ],
-    )(sums, data, signal, cosine, sine, pixel, weight, stage_a, twiddle, stage_b)
+    )(sums, data, signal, cosine, sine, pixel, stage_a, twiddle, stage_b)
     binned = binned.reshape(3, second, cycles, LANES).transpose(0, 2, 1, 3).reshape(3, cycles, nphi)
 
     got = exchange(send.reshape(n_tm, -1, LANES), "tm").reshape(-1, LANES)
-    rhs, weight, left, right = call(
+    halo_rows = -(-(PLANES + 3) * HALO // 8) * 8
+    rhs, to_one, to_two = call(
         rhs_kernel,
         "rhs",
-        [((PLANES, count, band), f32), ((count, band), f32)] + [((PLANES + 1, 8, band), f32)] * 2,
-        [pltpu.VMEM((PLANES + 1, count, LANES), f32)],
-    )(got, prior_precision, omega_noise, omega_prior)
-    after = lax.ppermute(left, "det", back)
-    before = lax.ppermute(right, "det", forth)
+        [((PLANES, count, band), f32)] + [((halo_rows, band), f32)] * 2,
+        [pltpu.VMEM((PLANES, count, LANES), f32)],
+    )(got, weights, prior_precision, omega_noise, omega_prior)
+    from_one = lax.ppermute(to_one, "det", pairs)
+    from_two = lax.ppermute(to_two, "det", others)
     one, two, sums = call(
         krylov_kernel,
         "krylov",
         [((PLANES, count, band), f32)] * 2 + [((devices, LANES), f32)],
-    )(rhs, weight, prior_precision, after, prior_after)
+        [pltpu.VMEM((count + BLOCK, band), f32)],
+    )(rhs, weights, prior_precision, from_one, from_two)
     sums = exchange(sums, everywhere)
-    solution = call(final_kernel, "final", [((PLANES, count, band), f32)])(
-        sums, rhs, one, two, prior_precision, weight, before, prior_before
-    )[0]
+    solution = call(final_kernel, "final", [((PLANES, count, band), f32)])(sums, rhs, one, two)[0]
     return (gain, binned, solution)
 
 

time: 76.8 us -> 61.3 us (0.80)
  starting transfers between devices: 15.3 us -> 2.13 us
  blocking collectives: 36.4 us -> 44.7 us
  Pallas kernels: 13.7 us -> 9.81 us
  waiting for transfers between devices: 7.18 us -> 3.69 us
  local copies, waits for them, and re-layouts: 2.96 us -> 0.03 us
    ppermute x4 -> x2, starting transfers between devices: 11.7 us -> 2.13 us  [the longest x1 1.48 us: per_device(): from_two = lax.ppermute(to_two, 'det', others)]
    all_to_all x3 -> x4, blocking collectives: 36.4 us -> 44.7 us  [exchange(): return lax.all_to_all(values, axes, split_axis=0, concat_axis=0, tiled=True)]
    all_to_all x1 -> x0, waiting for transfers between devices: 7.05 us -> none  [exchange(): return lax.all_to_all(values, axes, split_axis=0, concat_axis=0, tiled=True)]
    all_to_all x1 -> x0, starting transfers between devices: 3.57 us -> none  [exchange(): return lax.all_to_all(values, axes, split_axis=0, concat_axis=0, tiled=True)]
    ppermute x4 -> x2, waiting for transfers between devices: 0.14 us -> 3.69 us  [the longest x1 2.2 us: per_device(): from_one = lax.ppermute(to_one, 'det', pairs)]
    unnamed x22 -> x14, local copies, waits for them, and re-layouts: 2.95 us -> 0.03 us
    pallas_call x1, Pallas kernels: 6.16 us -> 3.29 us  [per_device(): call(bin_kernel, 'bin', [((1, 1), f32), ((3, second * cycles, LANES), f32...]
    pallas_call x1, Pallas kernels: 4.99 us -> 3.25 us  [per_device(): call(lookup_kernel, 'lookup', [((tiles, cap), f32)] * 4 + [((tiles, cap),...]
  transfers between devices with their start and end apart: 5 -> 2, of which waited for: 2 -> 2; matrix products, arithmetic and copies ran while one was open for 0% -> 0% of each run, Pallas kernels for 2% -> 0%
where the time goes in v2:
time: 61.3 us; the launch traced here: 61 us
  blocking collectives  44.7 us (73%)
  Pallas kernels  9.81 us (16%)
  waiting for transfers between devices  3.69 us (6%)
  starting transfers between devices  2.13 us (3%)
  between operations  0.7 us (1%)
    all_to_all x4, blocking collectives, exchange(): return lax.all_to_all(values, axes, split_axis=0, concat_axis=0, tiled=True)  44.7 us
    pallas_call x1, Pallas kernels, per_device(): call(bin_kernel, 'bin', [((1, 1), f32), ((3, second * cycles, LANES), f32...  3.29 us
    pallas_call x1, Pallas kernels, per_device(): call(lookup_kernel, 'lookup', [((tiles, cap), f32)] * 4 + [((tiles, cap),...  3.25 us
    ppermute x1, waiting for transfers between devices, per_device(): from_one = lax.ppermute(to_one, 'det', pairs)  2.2 us
    pallas_call x1, Pallas kernels, per_device(): call(pack_kernel, 'pack', [((tiles * 8, LANES), f32)], [pltpu.VMEM((tiles...  1.6 us
    ppermute x1, waiting for transfers between devices, per_device(): from_two = lax.ppermute(to_two, 'det', others)  1.49 us
    ppermute x1, starting transfers between devices, per_device(): from_two = lax.ppermute(to_two, 'det', others)  1.48 us
  transfers between devices with their start and end apart: 2, of which 2 were waited for; matrix products, arithmetic and copies ran while one was open for 0% of the time, Pallas kernels for 0%

profile of v2, /device:TPU:0, one launch (start us, length us, event | category | flops | bytes accessed | tf_op | source)
XLA Modules:
  0.0 61.0 jit_solution(4550023236565095792)
XLA Ops:
  0.6 0.0 copy-start.1
  0.6 1.6 %pack.1 = f32[256,128]{1,0:T(8,128)} custom-call(f32[32,256]{1,0:T(8,128)} %bitcast.35, f32[32,256]{1,0:T(8,128)} %bitcast.36, s32[32,256]{1,0:T(8,128)} %bitcast.37, s32[1,32]{1,0:T(1,128)} %bitcast.38), custom_call_target="tpu_custom_call" | custom-call | tf_op jit(solution)/shard_map/pack/pallas_call | solution.py:468
  2.3 15.5 %all_to_all.32 = f32[32,8,128]{2,1,0:T(8,128)S(1)} all-to-all(f32[32,8,128]{2,1,0:T(8,128)} %bitcast.34), channel_id=1, replica_groups=mesh['det'=4,'tm'=8] {'det','tm'}, dimensions={0} | all-to-all | bytes 262144 | tf_op jit(solution)/shard_map/all_to_all | solution.py:451
  17.7 0.0 copy-start.4
  17.7 0.0 copy-done.1
  17.7 0.0 copy-start.5
  17.7 0.0 copy-start.6
  17.8 3.2 %lookup.1 = (f32[32,256]{1,0:T(8,128)S(1)}, f32[32,256]{1,0:T(8,128)S(1)}, f32[32,256]{1,0:T(8,128)S(1)}, f32[32,256]{1,0:T(8,128)S(1)}, s32[32,256]{1,0:T(8,128)S(1)}, /*index=5*/f32[32,128]{1,0:T(8,128)S(1)}) custom-call(f32[256,128]{1,0:T(8,128)S(1)} %bitcast.27, f32[3,128,128]{2,1,0:T(8,128)S(1)} %bitcast.28), custom_call_target="tpu_custom_call" | custom-call | tf_op jit(solution)/shard_map/lookup/pallas_call | solution.py:492
  21.0 8.9 %all_to_all.33 = f32[32,1,128]{2,1,0:T(1,128)S(1)} all-to-all(f32[32,1,128]{2,1,0:T(1,128)S(1)} %bitcast.32), channel_id=1, replica_groups=mesh['det'=4,'tm'=8] {'det','tm'}, dimensions={0} | all-to-all | bytes 32768 | tf_op jit(solution)/shard_map/all_to_all | solution.py:451
  29.9 0.0 copy-done.4
  29.9 0.0 copy-done.5
  29.9 0.0 copy-done.6
  29.9 0.0 copy-start.3
  29.9 3.3 %bin.1 = (f32[1,1]{1,0:T(1,128)}, f32[3,128,128]{2,1,0:T(8,128)}, f32[72,128]{1,0:T(8,128)S(1)}, f32[384,128]{1,0:T(8,128)S(1)}) custom-call(f32[32,128]{1,0:T(8,128)S(1)} %bitcast.30, f32[32,256]{1,0:T(8,128)S(1)} %get-tuple-element.20.data_ref, f32[32,256]{1,0:T(8,128)S(1)} %get-tuple-element.21.signal_ref, f32[32,256]{1,0:T(8,128)S(1)} %get-tuple-element.22.cosine_ref, ...), custom_call_target="tpu_custom_call" | custom-call | tf_op jit(solution)/shard_map/bin/pallas_call | solution.py:505
  33.2 0.0 copy-start
  33.2 0.0 copy-start.2
  33.2 10.9 %all_to_all.34 = f32[8,48,128]{2,1,0:T(8,128)S(1)} all-to-all(f32[8,48,128]{2,1,0:T(8,128)S(1)} %bitcast.29), channel_id=1, replica_groups=mesh['det'=4,'tm'=8] {'tm'}, dimensions={0} | all-to-all | bytes 393216 | tf_op jit(solution)/shard_map/all_to_all | solution.py:451
  44.0 0.0 copy-done.3
  44.1 0.0 copy-done
  44.1 0.0 copy-done.2
  44.1 0.2 rhs.1
  44.2 0.7 %collective-permute-start = (f32[32,512]{1,0:T(8,128)S(1)}, f32[32,512]{1,0:T(8,128)S(1)}, u32[]{:S(2)}, u32[]{:S(2)}) collective-permute-start(f32[32,512]{1,0:T(8,128)S(1)} %get-tuple-element.30), channel_id=1, source_target_pairs={{0,8},{8,0},{16,24},{24,16},{1,9},{9,1},{17,25},{25,17},{2,10},{10... | collective-permute-start | bytes 196616 | tf_op jit(solution)/shard_map/ppermute | solution.py:533
  44.9 1.5 %collective-permute-start.1 = (f32[32,512]{1,0:T(8,128)S(1)}, f32[32,512]{1,0:T(8,128)S(1)}, u32[]{:S(2)}, u32[]{:S(2)}) collective-permute-start(f32[32,512]{1,0:T(8,128)S(1)} %get-tuple-element.31), channel_id=1, source_target_pairs={{0,24},{8,16},{16,8},{24,0},{1,25},{9,17},{17,9},{25,1},{2,26},{10... | collective-permute-start | bytes 196616 | tf_op jit(solution)/shard_map/ppermute | solution.py:534
  46.4 2.2 %collective-permute-done.from_one_ref = f32[32,512]{1,0:T(8,128)S(1)} collective-permute-done((f32[32,512]{1,0:T(8,128)S(1)}, f32[32,512]{1,0:T(8,128)S(1)}, u32[]{:S(2)}, u32[]{:S(2)}) %collective-permute-start) | collective-permute-done | bytes 65568 | tf_op jit(solution)/shard_map/ppermute | solution.py:533
  48.6 1.5 %collective-permute-done.1.from_two_ref = f32[32,512]{1,0:T(8,128)S(1)} collective-permute-done((f32[32,512]{1,0:T(8,128)S(1)}, f32[32,512]{1,0:T(8,128)S(1)}, u32[]{:S(2)}, u32[]{:S(2)}) %collective-permute-start.1) | collective-permute-done | bytes 65568 | tf_op jit(solution)/shard_map/ppermute | solution.py:534
  50.1 0.6 krylov.1
  50.7 9.5 %all_to_all.35 = f32[32,1,128]{2,1,0:T(1,128)S(1)} all-to-all(f32[32,1,128]{2,1,0:T(1,128)S(1)} %bitcast.33), channel_id=1, replica_groups=mesh['det'=4,'tm'=8] {'det','tm'}, dimensions={0} | all-to-all | bytes 32768 | tf_op jit(solution)/shard_map/all_to_all | solution.py:451
  60.1 0.9 %final.1 = f32[6,16,512]{2,1,0:T(8,128)} custom-call(f32[32,128]{1,0:T(8,128)S(1)} %bitcast.31, f32[6,16,512]{2,1,0:T(8,128)S(1)} %get-tuple-element.29.rhs_ref, f32[6,16,512]{2,1,0:T(8,128)S(1)} %get-tuple-element.33.one_ref, f32[6,16,512]{2,1,0:T(8,128)S(1)} %get-tuple-element.34.two_ref), custom_call_target="tpu_custom_call" | custom-call | tf_op jit(solution)/shard_map/final/pallas_call | solution.py:542
Async XLA Ops:
  0.6 17.1 %copy-start.1 = (f32[3,2,8192]{2,1,0:T(2,128)S(1)}, f32[3,2,8192]{2,1,0:T(2,128)}, u32[]{:S(2)}) copy-start(f32[3,2,8192]{2,1,0:T(2,128)} %param.15) | copy-start | bytes 589828
  17.7 12.1 %copy-start.4 = (bf16[384,256]{1,0:T(8,128)(2,1)S(1)}, bf16[384,256]{1,0:T(8,128)(2,1)}, u32[]{:S(2)}) copy-start(bf16[384,256]{1,0:T(8,128)(2,1)} %constant.6.clone.stage_a_ref) | copy-start | bytes 589828
  17.7 12.1 %copy-start.5 = (f32[2,64,128]{2,1,0:T(8,128)S(1)}, f32[2,64,128]{2,1,0:T(8,128)}, u32[]{:S(2)}) copy-start(f32[2,64,128]{2,1,0:T(8,128)} %constant.7.clone.twiddle_ref) | copy-start | bytes 196612
  17.7 12.1 %copy-start.6 = (bf16[64,384]{1,0:T(8,128)(2,1)S(1)}, bf16[64,384]{1,0:T(8,128)(2,1)}, u32[]{:S(2)}) copy-start(bf16[64,384]{1,0:T(8,128)(2,1)} %constant.8.clone.stage_b_ref) | copy-start | bytes 147460
  29.9 14.2 %copy-start.3 = (f32[6,16,512]{2,1,0:T(8,128)S(1)}, f32[6,16,512]{2,1,0:T(8,128)}, u32[]{:S(2)}) copy-start(f32[6,16,512]{2,1,0:T(8,128)} %draw_ref.1) | copy-start | bytes 589828
  33.2 10.9 %copy-start = (f32[3,16,512]{2,1,0:T(8,128)S(1)}, f32[3,16,512]{2,1,0:T(8,128)}, u32[]{:S(2)}) copy-start(f32[3,16,512]{2,1,0:T(8,128)} %prior_ref.3) | copy-start | bytes 294916
  33.2 10.9 %copy-start.2 = (f32[6,16,512]{2,1,0:T(8,128)S(1)}, f32[6,16,512]{2,1,0:T(8,128)}, u32[]{:S(2)}) copy-start(f32[6,16,512]{2,1,0:T(8,128)} %noise_ref.1) | copy-start | bytes 589828
  44.2 4.3 %collective-permute-start = (f32[32,512]{1,0:T(8,128)S(1)}, f32[32,512]{1,0:T(8,128)S(1)}, u32[]{:S(2)}, u32[]{:S(2)}) collective-permute-start(f32[32,512]{1,0:T(8,128)S(1)} %get-tuple-element.30), channel_id=1, source_target_pairs={{0,8},{8,0},{16,24},{24,16},{1,9},{9,1},{17,25},{25,17},{2,10},{10... | collective-permute-start | bytes 196616 | tf_op jit(solution)/shard_map/ppermute | solution.py:533
  44.9 5.2 %collective-permute-start.1 = (f32[32,512]{1,0:T(8,128)S(1)}, f32[32,512]{1,0:T(8,128)S(1)}, u32[]{:S(2)}, u32[]{:S(2)}) collective-permute-start(f32[32,512]{1,0:T(8,128)S(1)} %get-tuple-element.31), channel_id=1, source_target_pairs={{0,24},{8,16},{16,8},{24,0},{1,25},{9,17},{17,9},{25,1},{2,26},{10... | collective-permute-start | bytes 196616 | tf_op jit(solution)/shard_map/ppermute | solution.py:534

commit v3 on v2

--- a/solution.py
+++ b/solution.py
@@ -14,7 +14,7 @@
 COUPLING = 0.45
 
 LANES = 128
-GROUP = 16
+GROUP = 32
 PLANES = 6
 HALO = 3
 BLOCK = 8
@@ -77,27 +77,28 @@
         copy.wait()
     tiles = samples_ref.shape[0]
     halves = samples_ref.shape[1] // LANES
+    lines = 3 * halves + 1
     for h in range(halves):
         cut = slice(h * LANES, (h + 1) * LANES)
-        out_ref[pl.ds(h, tiles, stride=8), :] = samples_ref[:, cut]
-        out_ref[pl.ds(halves + h, tiles, stride=8), :] = angles_ref[:, cut]
-        out_ref[pl.ds(2 * halves + h, tiles, stride=8), :] = pointing_ref[:, cut].astype(jnp.float32)
+        out_ref[pl.ds(h, tiles, stride=lines), :] = samples_ref[:, cut]
+        out_ref[pl.ds(halves + h, tiles, stride=lines), :] = angles_ref[:, cut]
+        out_ref[pl.ds(2 * halves + h, tiles, stride=lines), :] = pointing_ref[:, cut].astype(
+            jnp.float32
+        )
     count = counts_ref[...].astype(jnp.float32)
     row = lax.broadcasted_iota(jnp.int32, (tiles, tiles), 0)
     col = lax.broadcasted_iota(jnp.int32, (tiles, tiles), 1)
     column = jnp.sum(jnp.where(row == col, count, 0.0), axis=1, keepdims=True)
-    column = jnp.broadcast_to(column, (tiles, LANES))
-    out_ref[pl.ds(3 * halves, tiles, stride=8), :] = column
-    out_ref[pl.ds(3 * halves + 1, tiles, stride=8), :] = column
+    out_ref[pl.ds(3 * halves, tiles, stride=lines), :] = jnp.broadcast_to(column, (tiles, LANES))
 
 
 def lookup_kernel(
     got_ref, sky_ref, data_ref, signal_ref, cosine_ref, sine_ref, pixel_ref, sums_ref,
     table, high, low,
 ):
-    tiles = got_ref.shape[0] // 8
-    cap = data_ref.shape[1]
+    tiles, cap = data_ref.shape
     halves = cap // LANES
+    lines = 3 * halves + 1
     rows = sky_ref.shape[1]
     cycles = 2
     nphi = rows * LANES // cycles
@@ -108,13 +109,13 @@
         table[c * LANES : (c + 1) * LANES, rows:] = part[1]
 
     def received(field):
-        parts = [got_ref[pl.ds(field * halves + h, tiles, stride=8), :] for h in range(halves)]
+        parts = [got_ref[pl.ds(field * halves + h, tiles, stride=lines), :] for h in range(halves)]
         return jnp.concatenate(parts, axis=1)
 
     data = received(0)
     angle = received(1)
     pixel = received(2).astype(jnp.int32)
-    count = got_ref[pl.ds(3 * halves, tiles, stride=8), :]
+    count = got_ref[pl.ds(3 * halves, tiles, stride=lines), :]
     count = jnp.concatenate([count] * halves, axis=1)
     slot = lax.broadcasted_iota(jnp.int32, (tiles, cap), 1).astype(jnp.float32)
     valid = jnp.where(slot < count, 1.0, 0.0)
@@ -172,7 +173,7 @@
 def bin_kernel(
     sums_ref, data_ref, signal_ref, cosine_ref, sine_ref, pixel_ref,
     stage_a_ref, twiddle_ref, stage_b_ref,
-    gain_ref, binned_ref, weight_ref, send_ref,
+    gain_ref, maps_ref, weight_ref, send_ref,
     acc, weights, high, low, wide, onehot,
 ):
     tiles, cap = data_ref.shape
@@ -241,10 +242,7 @@
         for cy in range(cycles):
             block = map_c[:, cy * first : (cy + 1) * first]
             blocks.append(block)
-            flipped = block.T
-            binned_ref[c, pl.ds(cy, first // 2, stride=cycles), :] = jnp.concatenate(
-                [flipped[: first // 2], flipped[first // 2 :]], axis=1
-            )
+            maps_ref[c * second : (c + 1) * second, cy * first : (cy + 1) * first] = block
     field = jnp.concatenate(blocks, axis=0)
     field_high, field_low = split(field)
     modes = jnp.dot(
@@ -281,6 +279,18 @@
                     ]
 
 
+def flip_kernel(maps_ref, binned_ref):
+    first = LANES
+    cycles = maps_ref.shape[1] // first
+    second = maps_ref.shape[0] // 3
+    for c in range(3):
+        for cy in range(cycles):
+            flipped = maps_ref[c * second : (c + 1) * second, cy * first : (cy + 1) * first].T
+            binned_ref[c, pl.ds(cy, first // 2, stride=cycles), :] = jnp.concatenate(
+                [flipped[: first // 2], flipped[first // 2 :]], axis=1
+            )
+
+
 def rhs_kernel(
     got_ref, weights_ref, prior_ref, noise_ref, draw_ref, rhs_ref, one_ref, two_ref, lines
 ):
@@ -306,18 +316,25 @@
                     lines[p] + root_weight * noise_ref[p, :, cut] + root * draw_ref[p, :, cut]
                 )
     even = lax.axis_index("det") % 2 == 0
-    for ref in (one_ref, two_ref):
-        ref[(PLANES + 3) * HALO :, :] = jnp.zeros_like(ref[(PLANES + 3) * HALO :, :])
-    for p in range(PLANES + 3):
-        source = rhs_ref.at[p] if p < PLANES else prior_ref.at[p - PLANES]
-        head = source[:HALO, :]
-        tail = source[count - HALO :, :]
+    after = PLANES * HALO
+    for p in range(PLANES):
+        c = p // 2
+        head = rhs_ref[p, :HALO, :]
+        tail = rhs_ref[p, count - HALO :, :]
+        row = lax.broadcasted_iota(jnp.int32, head.shape, 0)
+        head = jnp.where(row == HALO - 1, jnp.sqrt(prior_ref[c, :HALO, :]) * head, head)
+        tail = jnp.where(row == HALO - 2, jnp.sqrt(prior_ref[c, count - HALO :, :]) * tail, tail)
         one_ref[p * HALO : (p + 1) * HALO, :] = jnp.where(even, tail, head)
         two_ref[p * HALO : (p + 1) * HALO, :] = jnp.where(even, head, tail)
+    for c in range(3):
+        head = prior_ref[c, :2, :]
+        tail = prior_ref[c, count - 2 :, :]
+        one_ref[after + 2 * c : after + 2 * c + 2, :] = jnp.where(even, tail, head)
+        two_ref[after + 2 * c : after + 2 * c + 2, :] = jnp.where(even, head, tail)
 
 
 def krylov_kernel(
-    rhs_ref, weights_ref, prior_ref, from_one_ref, from_two_ref, one_ref, two_ref, sums_ref, wide
+    rhs_ref, weights_ref, prior_ref, from_one_ref, from_two_ref, one_ref, two_ref, sums_ref, wide, prior_wide
 ):
     count = rhs_ref.shape[1]
     rows = count + BLOCK
@@ -339,17 +356,28 @@
     weight = jnp.concatenate([weight] * (band // LANES), axis=1)
     sums = [jnp.zeros((rows, band), jnp.float32) for _ in range(6)]
 
-    def extended(values, p):
-        here = slice(p * HALO, (p + 1) * HALO)
-        one, two = from_one_ref[here, :], from_two_ref[here, :]
-        wide[:count, :] = values
-        wide[count : count + HALO, :] = jnp.where(has_after, jnp.where(even, one, two), 0.0)
-        wide[rows - HALO :, :] = jnp.where(has_before, jnp.where(even, two, one), 0.0)
+    def arrived(at, size):
+        one, two = from_one_ref[at : at + size, :], from_two_ref[at : at + size, :]
+        ahead = jnp.where(has_after, jnp.where(even, one, two), 0.0)
+        behind = jnp.where(has_before, jnp.where(even, two, one), 0.0)
+        return ahead, behind
+
+    wide[count:, :] = jnp.zeros((BLOCK, band), jnp.float32)
+    prior_wide[count:, :] = jnp.ones((BLOCK, band), jnp.float32)
+
+    def extended(p):
+        ahead, behind = arrived(p * HALO, HALO)
+        wide[:count, :] = rhs_ref[p]
+        wide[count : count + HALO, :] = ahead
+        wide[rows - 2 :, :] = behind[HALO - 2 :]
         return wide[...]
 
-    wide[count:, :] = jnp.zeros((BLOCK, band), jnp.float32)
     for c in range(3):
-        precision = extended(prior_ref[c], PLANES + c)
+        ahead, behind = arrived(PLANES * HALO + 2 * c, 2)
+        prior_wide[:count, :] = prior_ref[c]
+        prior_wide[count : count + 2, :] = ahead
+        prior_wide[rows - 1 :, :] = behind[1:]
+        precision = prior_wide[...]
         root = jnp.sqrt(precision)
         diagonal = (precision + weight - SHIFT) * (1.0 / SPREAD)
         beside = root * (COUPLING / SPREAD)
@@ -362,7 +390,7 @@
 
         for part in range(2):
             p = 2 * c + part
-            zero = extended(rhs_ref[p], p)
+            zero = extended(p)
             one = apply(zero)
             two = apply(one)
             one_ref[p] = one[:count]
@@ -465,10 +493,11 @@
     pairs = [(i, i ^ 1) for i in range(n_det)]
     others = [(i, (i + 1 if i % 2 else i - 1) % n_det) for i in range(n_det)]
 
+    lines = 3 * cap // LANES + 1
     packed = call(
         pack_kernel,
         "pack",
-        [((tiles * 8, LANES), f32)],
+        [((tiles * lines, LANES), f32)],
         [
             pltpu.VMEM((tiles, cap), f32),
             pltpu.VMEM((tiles, cap), f32),
@@ -477,14 +506,18 @@
             pltpu.SemaphoreType.DMA((4,)),
         ],
         [pl.BlockSpec(memory_space=pltpu.HBM)] * 4,
-        60,
     )(
-        samples.reshape(tiles, cap),
-        angles.reshape(tiles, cap),
-        pointing.reshape(tiles, cap),
-        counts.reshape(1, tiles),
+        *(
+            pltpu.with_memory_space_constraint(values, pltpu.HBM)
+            for values in (
+                samples.reshape(tiles, cap),
+                angles.reshape(tiles, cap),
+                pointing.reshape(tiles, cap),
+                counts.reshape(1, tiles),
+            )
+        )
     )[0]
-    got = exchange(packed.reshape(tiles, 8, LANES), everywhere).reshape(tiles * 8, LANES)
+    got = exchange(packed.reshape(tiles, lines * LANES), everywhere).reshape(tiles * lines, LANES)
 
     sky = sky_map.reshape(3, cycles, second, LANES).transpose(0, 2, 1, 3)
     sky = sky.reshape(3, second * cycles, LANES)
@@ -502,12 +535,12 @@
     sums = exchange(sums, everywhere)
 
     stage_a, twiddle, stage_b = dft_tables(nphi, n_tm)
-    gain, binned, weights, send = call(
+    gain, maps, weights, send = call(
         bin_kernel,
         "bin",
         [
             ((1, 1), f32),
-            ((3, second * cycles, LANES), f32),
+            ((3 * second, cycles * LANES), f32),
             ((tiles * cycles + 8, LANES), f32),
             ((PLANES * cycles * n_tm * band // LANES, LANES), f32),
         ],
@@ -520,23 +553,25 @@
             pltpu.VMEM((cycles * LANES, GROUP * cap), bf16),
         ],
     )(sums, data, signal, cosine, sine, pixel, stage_a, twiddle, stage_b)
-    binned = binned.reshape(3, second, cycles, LANES).transpose(0, 2, 1, 3).reshape(3, cycles, nphi)
-
     got = exchange(send.reshape(n_tm, -1, LANES), "tm").reshape(-1, LANES)
-    halo_rows = -(-(PLANES + 3) * HALO // 8) * 8
+    halo_rows = PLANES * HALO + 3 * 2
     rhs, to_one, to_two = call(
         rhs_kernel,
         "rhs",
         [((PLANES, count, band), f32)] + [((halo_rows, band), f32)] * 2,
         [pltpu.VMEM((PLANES, count, LANES), f32)],
     )(got, weights, prior_precision, omega_noise, omega_prior)
+    maps, to_one, to_two = lax.optimization_barrier((maps, to_one, to_two))
     from_one = lax.ppermute(to_one, "det", pairs)
     from_two = lax.ppermute(to_two, "det", others)
+    binned = call(flip_kernel, "flip", [((3, second * cycles, LANES), f32)])(maps)[0]
+    binned = binned.reshape(3, second, cycles, LANES).transpose(0, 2, 1, 3).reshape(3, cycles, nphi)
+    binned, rhs = lax.optimization_barrier((binned, rhs))
     one, two, sums = call(
         krylov_kernel,
         "krylov",
         [((PLANES, count, band), f32)] * 2 + [((devices, LANES), f32)],
-        [pltpu.VMEM((count + BLOCK, band), f32)],
+        [pltpu.VMEM((count + BLOCK, band), f32)] * 2,
     )(rhs, weights, prior_precision, from_one, from_two)
     sums = exchange(sums, everywhere)
     solution = call(final_kernel, "final", [((PLANES, count, band), f32)])(sums, rhs, one, two)[0]

time: 61.3 us -> 59.2 us (0.966)
  waiting for transfers between devices: 3.69 us -> 2.56 us
    ppermute x1, waiting for transfers between devices: 2.2 us -> 1.08 us  [per_device(): from_one = lax.ppermute(to_one, 'det', pairs)]
    pallas_call x2 -> x3, Pallas kernels: 4.89 us -> 4.45 us  [the longest x1 2.54 us: per_device(): call(bin_kernel, 'bin', [((1, 1), f32), ((3 * second, cycles * LANES), f3...]
  transfers between devices with their start and end apart: 2 -> 2, of which waited for: 2 -> 2; matrix products, arithmetic and copies ran while one was open for 0% -> 0% of each run, Pallas kernels for 0% -> 2%
where the time goes in v3:
time: 59.2 us; the launch traced here: 59 us
  blocking collectives  44.3 us (75%)
  Pallas kernels  9.28 us (16%)
  waiting for transfers between devices  2.56 us (4%)
  starting transfers between devices  2.12 us (4%)
  between operations  0.71 us (1%)
    all_to_all x4, blocking collectives, exchange(): return lax.all_to_all(values, axes, split_axis=0, concat_axis=0, tiled=True)  44.3 us
    pallas_call x1, Pallas kernels, per_device(): call(lookup_kernel, 'lookup', [((tiles, cap), f32)] * 4 + [((tiles, cap),...  3.13 us
    pallas_call x1, Pallas kernels, per_device(): call(bin_kernel, 'bin', [((1, 1), f32), ((3 * second, cycles * LANES), f3...  2.54 us
    ppermute x1, waiting for transfers between devices, per_device(): from_two = lax.ppermute(to_two, 'det', others)  1.48 us
    ppermute x1, starting transfers between devices, per_device(): from_two = lax.ppermute(to_two, 'det', others)  1.47 us
  transfers between devices with their start and end apart: 2, of which 2 were waited for; matrix products, arithmetic and copies ran while one was open for 0% of the time, Pallas kernels for 2%

profile of v3, /device:TPU:0, one launch (start us, length us, event | category | flops | bytes accessed | tf_op | source)
XLA Modules:
  0.0 59.0 jit_solution(12249723223796656627)
XLA Ops:
  0.6 0.0 copy-start.1
  0.6 1.0 %pack.1 = f32[224,128]{1,0:T(8,128)S(1)} custom-call(f32[32,256]{1,0:T(8,128)} %bitcast.36, f32[32,256]{1,0:T(8,128)} %bitcast.37, s32[32,256]{1,0:T(8,128)} %bitcast.38, s32[1,32]{1,0:T(1,128)} %bitcast.39), custom_call_target="tpu_custom_call" | custom-call | tf_op jit(solution)/shard_map/pack/pallas_call | solution.py:497
  1.6 15.1 %all_to_all.36 = f32[32,1,896]{2,1,0:T(1,128)S(1)} all-to-all(f32[32,1,896]{2,1,0:T(1,128)S(1)} %bitcast.28), channel_id=1, replica_groups=mesh['det'=4,'tm'=8] {'det','tm'}, dimensions={0} | all-to-all | bytes 229376 | tf_op jit(solution)/shard_map/all_to_all | solution.py:479
  16.7 0.0 copy-start.4
  16.7 0.0 copy-done.1
  16.7 0.0 copy-start.5
  16.7 0.0 copy-start.6
  16.7 3.1 %lookup.1 = (f32[32,256]{1,0:T(8,128)S(1)}, f32[32,256]{1,0:T(8,128)S(1)}, f32[32,256]{1,0:T(8,128)S(1)}, f32[32,256]{1,0:T(8,128)S(1)}, s32[32,256]{1,0:T(8,128)S(1)}, /*index=5*/f32[32,128]{1,0:T(8,128)S(1)}) custom-call(f32[224,128]{1,0:T(8,128)S(1)} %bitcast.27, f32[3,128,128]{2,1,0:T(8,128)S(1)} %bitcast.29), custom_call_target="tpu_custom_call" | custom-call | tf_op jit(solution)/shard_map/lookup/pallas_call | solution.py:525
  19.8 8.8 %all_to_all.37 = f32[32,1,128]{2,1,0:T(1,128)S(1)} all-to-all(f32[32,1,128]{2,1,0:T(1,128)S(1)} %bitcast.33), channel_id=1, replica_groups=mesh['det'=4,'tm'=8] {'det','tm'}, dimensions={0} | all-to-all | bytes 32768 | tf_op jit(solution)/shard_map/all_to_all | solution.py:479
  28.7 0.0 copy-done.4
  28.7 0.0 copy-done.5
  28.7 0.0 copy-done.6
  28.7 0.0 copy-start.3
  28.7 2.5 %bin.1 = (f32[1,1]{1,0:T(1,128)}, f32[192,256]{1,0:T(8,128)S(1)}, f32[72,128]{1,0:T(8,128)S(1)}, f32[384,128]{1,0:T(8,128)S(1)}) custom-call(f32[32,128]{1,0:T(8,128)S(1)} %bitcast.31, f32[32,256]{1,0:T(8,128)S(1)} %get-tuple-element.25.data_ref, f32[32,256]{1,0:T(8,128)S(1)} %get-tuple-element.26.signal_ref, f32[32,256]{1,0:T(8,128)S(1)} %get-tuple-element.27.cosine_ref, ...), custom_call_target="tpu_custom_call" | custom-call | tf_op jit(solution)/shard_map/bin/pallas_call | solution.py:538
  31.2 0.0 copy-start
  31.2 0.0 copy-start.2
  31.3 10.9 %all_to_all.38 = f32[8,48,128]{2,1,0:T(8,128)S(1)} all-to-all(f32[8,48,128]{2,1,0:T(8,128)S(1)} %bitcast.30), channel_id=1, replica_groups=mesh['det'=4,'tm'=8] {'tm'}, dimensions={0} | all-to-all | bytes 393216 | tf_op jit(solution)/shard_map/all_to_all | solution.py:479
  42.1 0.0 copy-done.3
  42.1 0.0 copy-done
  42.1 0.0 copy-done.2
  42.1 0.2 rhs.1
  42.3 0.6 %collective-permute-start = (f32[24,512]{1,0:T(8,128)S(1)}, f32[24,512]{1,0:T(8,128)S(1)}, u32[]{:S(2)}, u32[]{:S(2)}) collective-permute-start(f32[24,512]{1,0:T(8,128)S(1)} %get-tuple-element.40), channel_id=1, source_target_pairs={{0,8},{8,0},{16,24},{24,16},{1,9},{9,1},{17,25},{25,17},{2,10},{10... | collective-permute-start | bytes 147464 | tf_op jit(solution)/shard_map/ppermute | solution.py:565
  43.0 1.5 %collective-permute-start.1 = (f32[24,512]{1,0:T(8,128)S(1)}, f32[24,512]{1,0:T(8,128)S(1)}, u32[]{:S(2)}, u32[]{:S(2)}) collective-permute-start(f32[24,512]{1,0:T(8,128)S(1)} %get-tuple-element.41), channel_id=1, source_target_pairs={{0,24},{8,16},{16,8},{24,0},{1,25},{9,17},{17,9},{25,1},{2,26},{10... | collective-permute-start | bytes 147464 | tf_op jit(solution)/shard_map/ppermute | solution.py:566
  44.5 0.9 %flip.1 = f32[3,128,128]{2,1,0:T(8,128)} custom-call(f32[192,256]{1,0:T(8,128)S(1)} %get-tuple-element.36.maps_ref), custom_call_target="tpu_custom_call" | custom-call | tf_op jit(solution)/shard_map/flip/pallas_call | solution.py:567
  45.4 1.1 %collective-permute-done.from_one_ref = f32[24,512]{1,0:T(8,128)S(1)} collective-permute-done((f32[24,512]{1,0:T(8,128)S(1)}, f32[24,512]{1,0:T(8,128)S(1)}, u32[]{:S(2)}, u32[]{:S(2)}) %collective-permute-start) | collective-permute-done | bytes 49184 | tf_op jit(solution)/shard_map/ppermute | solution.py:565
  46.5 1.5 %collective-permute-done.1.from_two_ref = f32[24,512]{1,0:T(8,128)S(1)} collective-permute-done((f32[24,512]{1,0:T(8,128)S(1)}, f32[24,512]{1,0:T(8,128)S(1)}, u32[]{:S(2)}, u32[]{:S(2)}) %collective-permute-start.1) | collective-permute-done | bytes 49184 | tf_op jit(solution)/shard_map/ppermute | solution.py:566
  48.0 0.6 %krylov.1 = (f32[6,16,512]{2,1,0:T(8,128)S(1)}, f32[6,16,512]{2,1,0:T(8,128)S(1)}, f32[32,128]{1,0:T(8,128)S(1)}) custom-call(f32[6,16,512]{2,1,0:T(8,128)S(1)} %get-tuple-element.39.rhs_ref, f32[72,128]{1,0:T(8,128)S(1)} %get-tuple-element.33.weights_ref, f32[3,16,512]{2,1,0:T(8,128)S(1)} %copy-done, f32[24,512]{1,0:T(8,128)S(1)} %collective-permute-done.from_one_ref, ...), custom_call_target="tpu_custom_call" | custom-call | tf_op jit(solution)/shard_map/krylov/pallas_call | solution.py:570
  48.6 9.5 %all_to_all.39 = f32[32,1,128]{2,1,0:T(1,128)S(1)} all-to-all(f32[32,1,128]{2,1,0:T(1,128)S(1)} %bitcast.34), channel_id=1, replica_groups=mesh['det'=4,'tm'=8] {'det','tm'}, dimensions={0} | all-to-all | bytes 32768 | tf_op jit(solution)/shard_map/all_to_all | solution.py:479
  58.1 0.9 %final.1 = f32[6,16,512]{2,1,0:T(8,128)} custom-call(f32[32,128]{1,0:T(8,128)S(1)} %bitcast.32, f32[6,16,512]{2,1,0:T(8,128)S(1)} %get-tuple-element.39.rhs_ref, f32[6,16,512]{2,1,0:T(8,128)S(1)} %get-tuple-element.43.one_ref, f32[6,16,512]{2,1,0:T(8,128)S(1)} %get-tuple-element.44.two_ref), custom_call_target="tpu_custom_call" | custom-call | tf_op jit(solution)/shard_map/final/pallas_call | solution.py:577
Async XLA Ops:
  0.6 16.1 %copy-start.1 = (f32[3,2,8192]{2,1,0:T(2,128)S(1)}, f32[3,2,8192]{2,1,0:T(2,128)}, u32[]{:S(2)}) copy-start(f32[3,2,8192]{2,1,0:T(2,128)} %param.15) | copy-start | bytes 589828
  16.7 12.0 %copy-start.4 = (bf16[384,256]{1,0:T(8,128)(2,1)S(1)}, bf16[384,256]{1,0:T(8,128)(2,1)}, u32[]{:S(2)}) copy-start(bf16[384,256]{1,0:T(8,128)(2,1)} %constant.6.clone.stage_a_ref) | copy-start | bytes 589828
  16.7 12.0 %copy-start.5 = (f32[2,64,128]{2,1,0:T(8,128)S(1)}, f32[2,64,128]{2,1,0:T(8,128)}, u32[]{:S(2)}) copy-start(f32[2,64,128]{2,1,0:T(8,128)} %constant.7.clone.twiddle_ref) | copy-start | bytes 196612
  16.7 12.0 %copy-start.6 = (bf16[64,384]{1,0:T(8,128)(2,1)S(1)}, bf16[64,384]{1,0:T(8,128)(2,1)}, u32[]{:S(2)}) copy-start(bf16[64,384]{1,0:T(8,128)(2,1)} %constant.8.clone.stage_b_ref) | copy-start | bytes 147460
  28.7 13.5 %copy-start.3 = (f32[6,16,512]{2,1,0:T(8,128)S(1)}, f32[6,16,512]{2,1,0:T(8,128)}, u32[]{:S(2)}) copy-start(f32[6,16,512]{2,1,0:T(8,128)} %draw_ref.1) | copy-start | bytes 589828
  31.2 10.9 %copy-start = (f32[3,16,512]{2,1,0:T(8,128)S(1)}, f32[3,16,512]{2,1,0:T(8,128)}, u32[]{:S(2)}) copy-start(f32[3,16,512]{2,1,0:T(8,128)} %prior_ref.3) | copy-start | bytes 294916
  31.2 10.9 %copy-start.2 = (f32[6,16,512]{2,1,0:T(8,128)S(1)}, f32[6,16,512]{2,1,0:T(8,128)}, u32[]{:S(2)}) copy-start(f32[6,16,512]{2,1,0:T(8,128)} %noise_ref.1) | copy-start | bytes 589828
  42.3 4.2 %collective-permute-start = (f32[24,512]{1,0:T(8,128)S(1)}, f32[24,512]{1,0:T(8,128)S(1)}, u32[]{:S(2)}, u32[]{:S(2)}) collective-permute-start(f32[24,512]{1,0:T(8,128)S(1)} %get-tuple-element.40), channel_id=1, source_target_pairs={{0,8},{8,0},{16,24},{24,16},{1,9},{9,1},{17,25},{25,17},{2,10},{10... | collective-permute-start | bytes 147464 | tf_op jit(solution)/shard_map/ppermute | solution.py:565
  43.0 5.0 %collective-permute-start.1 = (f32[24,512]{1,0:T(8,128)S(1)}, f32[24,512]{1,0:T(8,128)S(1)}, u32[]{:S(2)}, u32[]{:S(2)}) collective-permute-start(f32[24,512]{1,0:T(8,128)S(1)} %get-tuple-element.41), channel_id=1, source_target_pairs={{0,24},{8,16},{16,8},{24,0},{1,25},{9,17},{17,9},{25,1},{2,26},{10... | collective-permute-start | bytes 147464 | tf_op jit(solution)/shard_map/ppermute | solution.py:566

commit v4 on v3

--- a/solution.py
+++ b/solution.py
@@ -26,10 +26,20 @@
     return high, low
 
 
+def bits(power):
+    return power.bit_length() - 1
+
+
 def split(values):
     high = values.astype(jnp.bfloat16)
     low = (values - high.astype(jnp.float32)).astype(jnp.bfloat16)
     return high, low
+
+
+def meeting_order(n_tm):
+    if n_tm == 8:
+        return [3, 2, 5, 4, 1, 0, 7, 6]
+    return [(i + n_tm // 2 + 1) % n_tm for i in range(n_tm)]
 
 
 def dft_tables(nphi, n_tm):
@@ -47,7 +57,7 @@
     twiddle = np.stack([np.cos(angle), np.sin(angle)]).astype(np.float32)
     per_band = half // n_tm
     row = np.arange(half)
-    q = (row % n_tm) * per_band + row // n_tm
+    q = np.array(meeting_order(n_tm))[row % n_tm] * per_band + row // n_tm
     angle = 2.0 * math.pi / second * (np.outer(q, b) % second)
     cos_b, sin_b = np.cos(angle), np.sin(angle)
     stage_b = np.block([[cos_b, -sin_b], [-sin_b, -cos_b]]) / math.sqrt(nphi)
@@ -92,8 +102,13 @@
     out_ref[pl.ds(3 * halves, tiles, stride=lines), :] = jnp.broadcast_to(column, (tiles, LANES))
 
 
+def repeated(line, rows):
+    tile = jnp.broadcast_to(line, (16, line.shape[1])).astype(jnp.bfloat16)
+    return jnp.concatenate([tile] * (rows // 16), axis=0)
+
+
 def lookup_kernel(
-    got_ref, sky_ref, data_ref, signal_ref, cosine_ref, sine_ref, pixel_ref, sums_ref,
+    got_ref, sky_ref, data_ref, signal_ref, cosine_ref, sine_ref, line_ref, column_ref, sums_ref,
     table, high, low,
 ):
     tiles, cap = data_ref.shape
@@ -123,30 +138,34 @@
     sine = jnp.sin(2.0 * angle)
     cosine_ref[...] = cosine
     sine_ref[...] = sine
-    pixel_ref[...] = pixel
-    cycle = pixel // nphi
-    high[...] = (pixel % nphi) // LANES * cycles + cycle
-    low[...] = pixel % LANES
+    cycle = pixel >> bits(nphi)
+    row = (pixel >> bits(LANES)) & (nphi // LANES - 1)
+    high[...] = (row * cycles + cycle).astype(jnp.float32)
+    low[...] = pixel & (LANES - 1)
+    second = nphi // LANES
+    line_ref[...] = (pixel & (second - 1)).astype(jnp.float32)
+    column = cycle * LANES + ((pixel >> bits(second)) & 1) * (LANES // 2) + row
+    column_ref[...] = column.astype(jnp.float32)
 
     iota = lax.broadcasted_iota(jnp.int32, (LANES, cap), 0)
+    iota_half = iota.astype(jnp.float32).astype(jnp.bfloat16)
+    one = jnp.ones((LANES, cap), jnp.bfloat16)
+    zero = jnp.zeros((LANES, cap), jnp.bfloat16)
 
     def step(index, carry):
         for g in range(GROUP):
             s = index * GROUP + g
-            onehot = jnp.where(iota == high[pl.ds(s, 1), :], 1.0, 0.0).astype(jnp.bfloat16)
+            onehot = jnp.where(iota_half == repeated(high[pl.ds(s, 1), :], LANES), one, zero)
             onehot = jnp.concatenate([onehot, onehot], axis=0)
             found = jnp.dot(table[...], onehot, preferred_element_type=jnp.float32)
             mask = iota == low[pl.ds(s, 1), :]
-            looked = [
-                jnp.sum(
-                    jnp.where(mask, found[c * LANES : (c + 1) * LANES], 0.0), axis=0, keepdims=True
-                )
-                for c in range(3)
-            ]
-            signal_ref[pl.ds(s, 1), :] = (
-                looked[0]
-                + looked[1] * cosine_ref[pl.ds(s, 1), :]
-                + looked[2] * sine_ref[pl.ds(s, 1), :]
+            mixed = (
+                found[:LANES]
+                + found[LANES : 2 * LANES] * cosine_ref[pl.ds(s, 1), :]
+                + found[2 * LANES :] * sine_ref[pl.ds(s, 1), :]
+            )
+            signal_ref[pl.ds(s, 1), :] = jnp.sum(
+                jnp.where(mask, mixed, 0.0), axis=0, keepdims=True
             )
         return carry
 
@@ -170,11 +189,18 @@
     sums_ref[...] = jnp.broadcast_to(line, sums_ref.shape)
 
 
+def all_gains(sums_ref, tiles):
+    total = jnp.sum(sums_ref[...], axis=0, keepdims=True)
+    row = lax.broadcasted_iota(jnp.int32, (tiles, total.shape[1]), 0)
+    lane = lax.broadcasted_iota(jnp.int32, (tiles, total.shape[1]), 1)
+    cross = jnp.sum(jnp.where(lane == row, total, 0.0), axis=1, keepdims=True)
+    square = jnp.sum(jnp.where(lane == row + tiles, total, 0.0), axis=1, keepdims=True)
+    return cross / (square + 1e-06)
+
+
 def bin_kernel(
-    sums_ref, data_ref, signal_ref, cosine_ref, sine_ref, pixel_ref,
-    stage_a_ref, twiddle_ref, stage_b_ref,
-    gain_ref, maps_ref, weight_ref, send_ref,
-    acc, weights, high, low, wide, onehot,
+    sums_ref, data_ref, signal_ref, cosine_ref, sine_ref, line_ref, column_ref,
+    stage_a_ref, twiddle_ref, stage_b_ref, maps_ref, send_ref, acc, weights, wide, onehot,
 ):
     tiles, cap = data_ref.shape
     cycles = 2
@@ -186,47 +212,33 @@
     stride = send_ref.shape[0] // n_tm
     per_band = stride // lines
 
-    total = jnp.sum(sums_ref[...], axis=0, keepdims=True)
-    width = total.shape[1]
-    row = lax.broadcasted_iota(jnp.int32, (tiles, width), 0)
-    lane = lax.broadcasted_iota(jnp.int32, (tiles, width), 1)
-    cross = jnp.sum(jnp.where(lane == row, total, 0.0), axis=1, keepdims=True)
-    square = jnp.sum(jnp.where(lane == row + tiles, total, 0.0), axis=1, keepdims=True)
-    gains = cross / (square + 1e-06)
-    for cy in range(cycles):
-        at = 2 * tiles + cy
-        weight_ref[pl.ds(cy, tiles, stride=cycles), :] = jnp.broadcast_to(
-            sums_ref[:, at : at + 1], (tiles, LANES)
-        )
-    weight_ref[tiles * cycles :, :] = jnp.zeros((8, LANES), jnp.float32)
-    position = lax.axis_index("det") * n_tm + lax.axis_index("tm")
-    place = lax.broadcasted_iota(jnp.int32, (tiles, 1), 0)
-    gain_ref[...] = jnp.sum(jnp.where(place == position, gains, 0.0), axis=0, keepdims=True)
-
+    gains = all_gains(sums_ref, tiles)
     residual = data_ref[...] - gains * signal_ref[...]
     for c, values in enumerate((residual, residual * cosine_ref[...], residual * sine_ref[...])):
         top = values.astype(jnp.bfloat16).astype(jnp.float32)
         weights[2 * c] = top
         weights[2 * c + 1] = values - top
-    pixel = pixel_ref[...]
-    low[...] = pixel % second
-    high[...] = pixel // nphi * first + (pixel // second) % 2 * (first // 2) + (pixel % nphi) // first
-
     acc[...] = jnp.zeros_like(acc)
-    iota_low = lax.broadcasted_iota(jnp.int32, (second, cap), 0)
     iota_high = lax.broadcasted_iota(jnp.int32, (cycles * first, cap), 0)
+    iota_high = iota_high.astype(jnp.float32).astype(jnp.bfloat16)
+    iota_low = iota_high[:second]
+    zero_low = jnp.zeros((second, cap), jnp.bfloat16)
+    zero_high = jnp.zeros((cycles * first, cap), jnp.bfloat16)
+    one_high = jnp.ones((cycles * first, cap), jnp.bfloat16)
 
     def step(index, carry):
         for g in range(GROUP):
             s = index * GROUP + g
             cut = slice(g * cap, (g + 1) * cap)
-            mask = iota_low == low[pl.ds(s, 1), :]
+            mask = iota_low == repeated(line_ref[pl.ds(s, 1), :], second)
             for i in range(6):
                 wide[i * second : (i + 1) * second, cut] = jnp.where(
-                    mask, weights[i, pl.ds(s, 1), :], 0.0
-                ).astype(jnp.bfloat16)
-            onehot[:, cut] = jnp.where(iota_high == high[pl.ds(s, 1), :], 1.0, 0.0).astype(
-                jnp.bfloat16
+                    mask, repeated(weights[i, pl.ds(s, 1), :], second), zero_low
+                )
+            onehot[:, cut] = jnp.where(
+                iota_high == repeated(column_ref[pl.ds(s, 1), :], cycles * first),
+                one_high,
+                zero_high,
             )
         acc[...] += lax.dot_general(
             wide[...], onehot[...], (((1,), (1,)), ((), ())), preferred_element_type=jnp.float32
@@ -279,20 +291,31 @@
                     ]
 
 
-def flip_kernel(maps_ref, binned_ref):
+def report_kernel(maps_ref, sums_ref, binned_ref, gain_ref, weight_ref):
     first = LANES
     cycles = maps_ref.shape[1] // first
     second = maps_ref.shape[0] // 3
+    tiles = sums_ref.shape[0]
     for c in range(3):
         for cy in range(cycles):
             flipped = maps_ref[c * second : (c + 1) * second, cy * first : (cy + 1) * first].T
             binned_ref[c, pl.ds(cy, first // 2, stride=cycles), :] = jnp.concatenate(
                 [flipped[: first // 2], flipped[first // 2 :]], axis=1
             )
+    position = lax.axis_index("det") * lax.axis_size("tm") + lax.axis_index("tm")
+    place = lax.broadcasted_iota(jnp.int32, (tiles, 1), 0)
+    own = jnp.where(place == position, all_gains(sums_ref, tiles), 0.0)
+    gain_ref[...] = jnp.sum(own, axis=0, keepdims=True)
+    for cy in range(cycles):
+        at = 2 * tiles + cy
+        weight_ref[pl.ds(cy, tiles, stride=cycles), :] = jnp.broadcast_to(
+            sums_ref[:, at : at + 1], (tiles, LANES)
+        )
+    weight_ref[tiles * cycles :, :] = jnp.zeros((BLOCK, LANES), jnp.float32)
 
 
 def rhs_kernel(
-    got_ref, weights_ref, prior_ref, noise_ref, draw_ref, rhs_ref, one_ref, two_ref, lines
+    got_ref, sums_ref, prior_ref, noise_ref, draw_ref, rhs_ref, one_ref, two_ref, lines
 ):
     count = prior_ref.shape[1]
     per_band = prior_ref.shape[2] // LANES
@@ -300,15 +323,21 @@
     cycles = count // n_tm
     each = PLANES * cycles
     stride = per_band * each
-    start = pl.multiple_of(lax.axis_index("det") * count, 8)
-    root_weight = jnp.sqrt(weights_ref[pl.ds(start, count), :])
+    order = meeting_order(n_tm)
+    tiles = sums_ref.shape[0]
+    group = sums_ref[pl.ds(pl.multiple_of(lax.axis_index("det") * n_tm, 8), n_tm), :]
+    for cy in range(cycles):
+        at = 2 * tiles + cy
+        lines[PLANES, pl.ds(cy, n_tm, stride=cycles), :] = jnp.broadcast_to(
+            group[:, at : at + 1], (n_tm, LANES)
+        )
+    root_weight = jnp.sqrt(lines[PLANES])
     for ql in range(per_band):
         cut = slice(ql * LANES, (ql + 1) * LANES)
         for p in range(PLANES):
-            for cy in range(cycles):
-                lines[p, pl.ds(cy, n_tm, stride=cycles), :] = got_ref[
-                    pl.ds(ql * each + p * cycles + cy, n_tm, stride=stride), :
-                ]
+            for i, t in enumerate(order):
+                at = i * stride + ql * each + p * cycles
+                lines[p, t * cycles : (t + 1) * cycles, :] = got_ref[at : at + cycles, :]
         for c in range(3):
             root = jnp.sqrt(prior_ref[c, :, cut])
             for p in (2 * c, 2 * c + 1):
@@ -475,8 +504,11 @@
     )
 
 
-def exchange(values, axes):
-    return lax.all_to_all(values, axes, split_axis=0, concat_axis=0, tiled=True)
+def exchange(values, axes, order=None):
+    groups = None if order is None else [order]
+    return lax.all_to_all(
+        values, axes, split_axis=0, concat_axis=0, tiled=True, axis_index_groups=groups
+    )
 
 
 def per_device(
@@ -522,49 +554,54 @@
     sky = sky_map.reshape(3, cycles, second, LANES).transpose(0, 2, 1, 3)
     sky = sky.reshape(3, second * cycles, LANES)
     width = LANES * -(-(2 * tiles + cycles) // LANES)
-    data, signal, cosine, sine, pixel, sums = call(
+    data, signal, cosine, sine, line, column, sums = call(
         lookup_kernel,
         "lookup",
-        [((tiles, cap), f32)] * 4 + [((tiles, cap), i32), ((devices, width), f32)],
+        [((tiles, cap), f32)] * 6 + [((devices, width), f32)],
         [
             pltpu.VMEM((3 * LANES, 2 * second * cycles), bf16),
-            pltpu.VMEM((tiles, cap), i32),
+            pltpu.VMEM((tiles, cap), f32),
             pltpu.VMEM((tiles, cap), i32),
         ],
     )(got, sky)
     sums = exchange(sums, everywhere)
 
     stage_a, twiddle, stage_b = dft_tables(nphi, n_tm)
-    gain, maps, weights, send = call(
+    maps, send = call(
         bin_kernel,
         "bin",
         [
-            ((1, 1), f32),
             ((3 * second, cycles * LANES), f32),
-            ((tiles * cycles + 8, LANES), f32),
             ((PLANES * cycles * n_tm * band // LANES, LANES), f32),
         ],
         [
             pltpu.VMEM((6 * second, cycles * LANES), f32),
             pltpu.VMEM((6, tiles, cap), f32),
-            pltpu.VMEM((tiles, cap), i32),
-            pltpu.VMEM((tiles, cap), i32),
             pltpu.VMEM((6 * second, GROUP * cap), bf16),
             pltpu.VMEM((cycles * LANES, GROUP * cap), bf16),
         ],
-    )(sums, data, signal, cosine, sine, pixel, stage_a, twiddle, stage_b)
-    got = exchange(send.reshape(n_tm, -1, LANES), "tm").reshape(-1, LANES)
+    )(sums, data, signal, cosine, sine, line, column, stage_a, twiddle, stage_b)
+
+    got = exchange(send.reshape(n_tm, -1, LANES), "tm", meeting_order(n_tm)).reshape(-1, LANES)
     halo_rows = PLANES * HALO + 3 * 2
     rhs, to_one, to_two = call(
         rhs_kernel,
         "rhs",
         [((PLANES, count, band), f32)] + [((halo_rows, band), f32)] * 2,
-        [pltpu.VMEM((PLANES, count, LANES), f32)],
-    )(got, weights, prior_precision, omega_noise, omega_prior)
+        [pltpu.VMEM((PLANES + 1, count, LANES), f32)],
+    )(got, sums, prior_precision, omega_noise, omega_prior)
     maps, to_one, to_two = lax.optimization_barrier((maps, to_one, to_two))
     from_one = lax.ppermute(to_one, "det", pairs)
     from_two = lax.ppermute(to_two, "det", others)
-    binned = call(flip_kernel, "flip", [((3, second * cycles, LANES), f32)])(maps)[0]
+    binned, gain, weights = call(
+        report_kernel,
+        "report",
+        [
+            ((3, second * cycles, LANES), f32),
+            ((1, 1), f32),
+            ((tiles * cycles + BLOCK, LANES), f32),
+        ],
+    )(maps, sums)
     binned = binned.reshape(3, second, cycles, LANES).transpose(0, 2, 1, 3).reshape(3, cycles, nphi)
     binned, rhs = lax.optimization_barrier((binned, rhs))
     one, two, sums = call(

time: 59.2 us -> 56.6 us (0.956)
  blocking collectives: 44.3 us -> 42.5 us
  Pallas kernels: 9.28 us -> 8.46 us
    all_to_all x4, blocking collectives: 44.3 us -> 42.5 us  [exchange(): lax.all_to_all(values, axes, split_axis=0, concat_axis=0, tiled=True, axi...]
    pallas_call x3, Pallas kernels: 6.62 us -> 5.82 us  [the longest x1 2.5 us: per_device(): call(bin_kernel, 'bin', [((3 * second, cycles * LANES), f32), ((PLANES *...]
where the time goes in v4:
time: 56.6 us; the launch traced here: 56.3 us
  blocking collectives  42.5 us (75%)
  Pallas kernels  8.46 us (15%)
  waiting for transfers between devices  2.55 us (5%)
  starting transfers between devices  2.12 us (4%)
  between operations  0.71 us (1%)
    all_to_all x4, blocking collectives, exchange(): lax.all_to_all(values, axes, split_axis=0, concat_axis=0, tiled=True, axi...  42.5 us
    pallas_call x1, Pallas kernels, per_device(): call(bin_kernel, 'bin', [((3 * second, cycles * LANES), f32), ((PLANES *...  2.5 us
    pallas_call x1, Pallas kernels, per_device(): call(lookup_kernel, 'lookup', [((tiles, cap), f32)] * 6 + [((devices, wid...  2.32 us
    ppermute x1, waiting for transfers between devices, per_device(): from_one = lax.ppermute(to_one, 'det', pairs)  1.56 us
    ppermute x1, starting transfers between devices, per_device(): from_two = lax.ppermute(to_two, 'det', others)  1.47 us
  transfers between devices with their start and end apart: 2, of which 2 were waited for; matrix products, arithmetic and copies ran while one was open for 0% of the time, Pallas kernels for 2%

profile of v4, /device:TPU:0, one launch (start us, length us, event | category | flops | bytes accessed | tf_op | source)
XLA Modules:
  0.0 56.3 jit_solution(2899484504038184055)
XLA Ops:
  0.6 0.0 copy-start.1
  0.6 1.0 %pack.1 = f32[224,128]{1,0:T(8,128)S(1)} custom-call(f32[32,256]{1,0:T(8,128)} %bitcast.37, f32[32,256]{1,0:T(8,128)} %bitcast.38, s32[32,256]{1,0:T(8,128)} %bitcast.39, s32[1,32]{1,0:T(1,128)} %bitcast.40), custom_call_target="tpu_custom_call" | custom-call | tf_op jit(solution)/shard_map/pack/pallas_call | solution.py:529
  1.6 15.1 %all_to_all.36 = f32[32,1,896]{2,1,0:T(1,128)S(1)} all-to-all(f32[32,1,896]{2,1,0:T(1,128)S(1)} %bitcast.28), channel_id=1, replica_groups=mesh['det'=4,'tm'=8] {'det','tm'}, dimensions={0} | all-to-all | bytes 229376 | tf_op jit(solution)/shard_map/all_to_all | solution.py:509
  16.7 0.0 copy-start.4
  16.7 0.0 copy-done.1
  16.7 0.0 copy-start.5
  16.7 2.3 %lookup.1 = (f32[32,256]{1,0:T(8,128)S(1)}, f32[32,256]{1,0:T(8,128)S(1)}, f32[32,256]{1,0:T(8,128)S(1)}, f32[32,256]{1,0:T(8,128)S(1)}, f32[32,256]{1,0:T(8,128...) custom-call(f32[224,128]{1,0:T(8,128)S(1)} %bitcast.27, f32[3,128,128]{2,1,0:T(8,128)S(1)} %bitcast.32), custom_call_target="tpu_custom_call" | custom-call | tf_op jit(solution)/shard_map/lookup/pallas_call | solution.py:557
  19.0 0.0 copy-start.6
  19.0 9.0 %all_to_all.37 = f32[32,1,128]{2,1,0:T(1,128)S(1)} all-to-all(f32[32,1,128]{2,1,0:T(1,128)S(1)} %bitcast.35), channel_id=1, replica_groups=mesh['det'=4,'tm'=8] {'det','tm'}, dimensions={0} | all-to-all | bytes 32768 | tf_op jit(solution)/shard_map/all_to_all | solution.py:509
  28.0 0.0 copy-done.4
  28.0 0.0 copy-done.5
  28.0 0.0 copy-done.6
  28.0 0.0 copy-start.3
  28.0 2.5 %bin.1 = (f32[192,256]{1,0:T(8,128)S(1)}, f32[384,128]{1,0:T(8,128)S(1)}) custom-call(f32[32,128]{1,0:T(8,128)S(1)} %bitcast.29, f32[32,256]{1,0:T(8,128)S(1)} %get-tuple-element.27.data_ref, f32[32,256]{1,0:T(8,128)S(1)} %get-tuple-element.28.signal_ref, f32[32,256]{1,0:T(8,128)S(1)} %get-tuple-element.29.cosine_ref, ...), custom_call_target="tpu_custom_call" | custom-call | tf_op jit(solution)/shard_map/bin/pallas_call | solution.py:570
  30.5 0.0 copy-start
  30.5 0.0 copy-start.2
  30.6 8.9 %all_to_all.38 = f32[8,48,128]{2,1,0:T(8,128)S(1)} all-to-all(f32[8,48,128]{2,1,0:T(8,128)S(1)} %bitcast.33), channel_id=1, replica_groups={{3,2,5,4,1,0,7,6},{11,10,13,12,9,8,15,14},{19,18,21,20,17,16,23,22},{27..., dimensions={0} | all-to-all | bytes 393216 | tf_op jit(solution)/shard_map/all_to_all | solution.py:509
  39.4 0.0 copy-done.3
  39.4 0.0 copy-done
  39.4 0.0 copy-done.2
  39.4 0.2 rhs.1
  39.6 0.6 %collective-permute-start = (f32[24,512]{1,0:T(8,128)S(1)}, f32[24,512]{1,0:T(8,128)S(1)}, u32[]{:S(2)}, u32[]{:S(2)}) collective-permute-start(f32[24,512]{1,0:T(8,128)S(1)} %get-tuple-element.44), channel_id=1, source_target_pairs={{0,8},{8,0},{16,24},{24,16},{1,9},{9,1},{17,25},{25,17},{2,10},{10... | collective-permute-start | bytes 147464 | tf_op jit(solution)/shard_map/ppermute | solution.py:594
  40.3 1.5 %collective-permute-start.1 = (f32[24,512]{1,0:T(8,128)S(1)}, f32[24,512]{1,0:T(8,128)S(1)}, u32[]{:S(2)}, u32[]{:S(2)}) collective-permute-start(f32[24,512]{1,0:T(8,128)S(1)} %get-tuple-element.45), channel_id=1, source_target_pairs={{0,24},{8,16},{16,8},{24,0},{1,25},{9,17},{17,9},{25,1},{2,26},{10... | collective-permute-start | bytes 147464 | tf_op jit(solution)/shard_map/ppermute | solution.py:595
  41.7 1.0 %report.1 = (f32[3,128,128]{2,1,0:T(8,128)}, f32[1,1]{1,0:T(1,128)}, f32[72,128]{1,0:T(8,128)S(1)}) custom-call(f32[192,256]{1,0:T(8,128)S(1)} %get-tuple-element.37.maps_ref, f32[32,128]{1,0:T(8,128)S(1)} %bitcast.31), custom_call_target="tpu_custom_call" | custom-call | tf_op jit(solution)/shard_map/report/pallas_call | solution.py:596
  42.7 1.6 %collective-permute-done.from_one_ref = f32[24,512]{1,0:T(8,128)S(1)} collective-permute-done((f32[24,512]{1,0:T(8,128)S(1)}, f32[24,512]{1,0:T(8,128)S(1)}, u32[]{:S(2)}, u32[]{:S(2)}) %collective-permute-start) | collective-permute-done | bytes 49184 | tf_op jit(solution)/shard_map/ppermute | solution.py:594
  44.3 1.0 %collective-permute-done.1.from_two_ref = f32[24,512]{1,0:T(8,128)S(1)} collective-permute-done((f32[24,512]{1,0:T(8,128)S(1)}, f32[24,512]{1,0:T(8,128)S(1)}, u32[]{:S(2)}, u32[]{:S(2)}) %collective-permute-start.1) | collective-permute-done | bytes 49184 | tf_op jit(solution)/shard_map/ppermute | solution.py:595
  45.3 0.6 %krylov.1 = (f32[6,16,512]{2,1,0:T(8,128)S(1)}, f32[6,16,512]{2,1,0:T(8,128)S(1)}, f32[32,128]{1,0:T(8,128)S(1)}) custom-call(f32[6,16,512]{2,1,0:T(8,128)S(1)} %get-tuple-element.42.rhs_ref, f32[72,128]{1,0:T(8,128)S(1)} %get-tuple-element.43.weights_ref, f32[3,16,512]{2,1,0:T(8,128)S(1)} %copy-done, f32[24,512]{1,0:T(8,128)S(1)} %collective-permute-done.from_one_ref, ...), custom_call_target="tpu_custom_call" | custom-call | tf_op jit(solution)/shard_map/krylov/pallas_call | solution.py:607
  45.9 9.5 %all_to_all.39 = f32[32,1,128]{2,1,0:T(1,128)S(1)} all-to-all(f32[32,1,128]{2,1,0:T(1,128)S(1)} %bitcast.36), channel_id=1, replica_groups=mesh['det'=4,'tm'=8] {'det','tm'}, dimensions={0} | all-to-all | bytes 32768 | tf_op jit(solution)/shard_map/all_to_all | solution.py:509
  55.4 0.9 %final.1 = f32[6,16,512]{2,1,0:T(8,128)} custom-call(f32[32,128]{1,0:T(8,128)S(1)} %bitcast.34, f32[6,16,512]{2,1,0:T(8,128)S(1)} %get-tuple-element.42.rhs_ref, f32[6,16,512]{2,1,0:T(8,128)S(1)} %get-tuple-element.47.one_ref, f32[6,16,512]{2,1,0:T(8,128)S(1)} %get-tuple-element.48.two_ref), custom_call_target="tpu_custom_call" | custom-call | tf_op jit(solution)/shard_map/final/pallas_call | solution.py:614
Async XLA Ops:
  0.6 16.1 %copy-start.1 = (f32[3,2,8192]{2,1,0:T(2,128)S(1)}, f32[3,2,8192]{2,1,0:T(2,128)}, u32[]{:S(2)}) copy-start(f32[3,2,8192]{2,1,0:T(2,128)} %param.15) | copy-start | bytes 589828
  16.7 11.3 %copy-start.4 = (bf16[384,256]{1,0:T(8,128)(2,1)S(1)}, bf16[384,256]{1,0:T(8,128)(2,1)}, u32[]{:S(2)}) copy-start(bf16[384,256]{1,0:T(8,128)(2,1)} %constant.6.clone.stage_a_ref) | copy-start | bytes 589828
  16.7 11.3 %copy-start.5 = (f32[2,64,128]{2,1,0:T(8,128)S(1)}, f32[2,64,128]{2,1,0:T(8,128)}, u32[]{:S(2)}) copy-start(f32[2,64,128]{2,1,0:T(8,128)} %constant.7.clone.twiddle_ref) | copy-start | bytes 196612
  19.0 9.0 %copy-start.6 = (bf16[64,384]{1,0:T(8,128)(2,1)S(1)}, bf16[64,384]{1,0:T(8,128)(2,1)}, u32[]{:S(2)}) copy-start(bf16[64,384]{1,0:T(8,128)(2,1)} %constant.8.clone.stage_b_ref) | copy-start | bytes 147460
  28.0 11.4 %copy-start.3 = (f32[6,16,512]{2,1,0:T(8,128)S(1)}, f32[6,16,512]{2,1,0:T(8,128)}, u32[]{:S(2)}) copy-start(f32[6,16,512]{2,1,0:T(8,128)} %draw_ref.1) | copy-start | bytes 589828
  30.5 8.9 %copy-start = (f32[3,16,512]{2,1,0:T(8,128)S(1)}, f32[3,16,512]{2,1,0:T(8,128)}, u32[]{:S(2)}) copy-start(f32[3,16,512]{2,1,0:T(8,128)} %prior_ref.3) | copy-start | bytes 294916
  30.5 8.9 %copy-start.2 = (f32[6,16,512]{2,1,0:T(8,128)S(1)}, f32[6,16,512]{2,1,0:T(8,128)}, u32[]{:S(2)}) copy-start(f32[6,16,512]{2,1,0:T(8,128)} %noise_ref.1) | copy-start | bytes 589828
  39.6 4.7 %collective-permute-start = (f32[24,512]{1,0:T(8,128)S(1)}, f32[24,512]{1,0:T(8,128)S(1)}, u32[]{:S(2)}, u32[]{:S(2)}) collective-permute-start(f32[24,512]{1,0:T(8,128)S(1)} %get-tuple-element.44), channel_id=1, source_target_pairs={{0,8},{8,0},{16,24},{24,16},{1,9},{9,1},{17,25},{25,17},{2,10},{10... | collective-permute-start | bytes 147464 | tf_op jit(solution)/shard_map/ppermute | solution.py:594
  40.3 5.0 %collective-permute-start.1 = (f32[24,512]{1,0:T(8,128)S(1)}, f32[24,512]{1,0:T(8,128)S(1)}, u32[]{:S(2)}, u32[]{:S(2)}) collective-permute-start(f32[24,512]{1,0:T(8,128)S(1)} %get-tuple-element.45), channel_id=1, source_target_pairs={{0,24},{8,16},{16,8},{24,0},{1,25},{9,17},{17,9},{25,1},{2,26},{10... | collective-permute-start | bytes 147464 | tf_op jit(solution)/shard_map/ppermute | solution.py:595

commit v5 on v4

--- a/solution.py
+++ b/solution.py
@@ -141,14 +141,14 @@
     cycle = pixel >> bits(nphi)
     row = (pixel >> bits(LANES)) & (nphi // LANES - 1)
     high[...] = (row * cycles + cycle).astype(jnp.float32)
-    low[...] = pixel & (LANES - 1)
+    low[...] = (pixel & (LANES - 1)).astype(jnp.float32)
     second = nphi // LANES
     line_ref[...] = (pixel & (second - 1)).astype(jnp.float32)
     column = cycle * LANES + ((pixel >> bits(second)) & 1) * (LANES // 2) + row
     column_ref[...] = column.astype(jnp.float32)
 
-    iota = lax.broadcasted_iota(jnp.int32, (LANES, cap), 0)
-    iota_half = iota.astype(jnp.float32).astype(jnp.bfloat16)
+    iota = lax.broadcasted_iota(jnp.int32, (LANES, cap), 0).astype(jnp.float32)
+    iota_half = iota.astype(jnp.bfloat16)
     one = jnp.ones((LANES, cap), jnp.bfloat16)
     zero = jnp.zeros((LANES, cap), jnp.bfloat16)
 
@@ -157,12 +157,17 @@
             s = index * GROUP + g
             onehot = jnp.where(iota_half == repeated(high[pl.ds(s, 1), :], LANES), one, zero)
             onehot = jnp.concatenate([onehot, onehot], axis=0)
-            found = jnp.dot(table[...], onehot, preferred_element_type=jnp.float32)
+            found = [
+                jnp.dot(
+                    table[c * LANES : (c + 1) * LANES, :], onehot, preferred_element_type=jnp.float32
+                )
+                for c in range(3)
+            ]
             mask = iota == low[pl.ds(s, 1), :]
             mixed = (
-                found[:LANES]
-                + found[LANES : 2 * LANES] * cosine_ref[pl.ds(s, 1), :]
-                + found[2 * LANES :] * sine_ref[pl.ds(s, 1), :]
+                found[0]
+                + found[1] * cosine_ref[pl.ds(s, 1), :]
+                + found[2] * sine_ref[pl.ds(s, 1), :]
             )
             signal_ref[pl.ds(s, 1), :] = jnp.sum(
                 jnp.where(mask, mixed, 0.0), axis=0, keepdims=True
@@ -180,12 +185,11 @@
     width = sums_ref.shape[1]
     row = lax.broadcasted_iota(jnp.int32, (tiles, width), 0)
     lane = lax.broadcasted_iota(jnp.int32, (tiles, width), 1)
-    both = jnp.where(lane == row, cross, 0.0) + jnp.where(lane == row + tiles, square, 0.0)
-    line = jnp.sum(both, axis=0, keepdims=True)
-    lane = lax.broadcasted_iota(jnp.int32, (1, width), 1)
+    lines = jnp.where(lane == row, cross, 0.0) + jnp.where(lane == row + tiles, square, 0.0)
     for cy in range(cycles):
-        hits = jnp.sum(jnp.where(cycle == cy, valid, 0.0), keepdims=True)
-        line = jnp.where(lane == 2 * tiles + cy, hits / nphi, line)
+        hits = jnp.sum(jnp.where(cycle == cy, valid, 0.0), axis=1, keepdims=True)
+        lines = lines + jnp.where(lane == 2 * tiles + cy, hits * (1.0 / nphi), 0.0)
+    line = jnp.sum(lines, axis=0, keepdims=True)
     sums_ref[...] = jnp.broadcast_to(line, sums_ref.shape)
 
 
@@ -363,7 +367,7 @@
 
 
 def krylov_kernel(
-    rhs_ref, weights_ref, prior_ref, from_one_ref, from_two_ref, one_ref, two_ref, sums_ref, wide, prior_wide
+    rhs_ref, weights_ref, prior_ref, from_one_ref, from_two_ref, one_ref, two_ref, sums_ref, edge
 ):
     count = rhs_ref.shape[1]
     rows = count + BLOCK
@@ -372,7 +376,6 @@
     even = group % 2 == 0
     has_before = group > 0
     has_after = group < lax.axis_size("det") - 1
-    own = lax.broadcasted_iota(jnp.int32, (rows, band), 0) < count
     start = pl.multiple_of(group * count, BLOCK)
     before = pl.multiple_of(jnp.maximum(start - BLOCK, 0), BLOCK)
     place = lax.broadcasted_iota(jnp.int32, (BLOCK, LANES), 0)
@@ -383,7 +386,7 @@
     )
     weight = jnp.concatenate([weights_ref[pl.ds(start, count), :], beyond], axis=0)
     weight = jnp.concatenate([weight] * (band // LANES), axis=1)
-    sums = [jnp.zeros((rows, band), jnp.float32) for _ in range(6)]
+    sums = [jnp.zeros((count, band), jnp.float32) for _ in range(6)]
 
     def arrived(at, size):
         one, two = from_one_ref[at : at + size, :], from_two_ref[at : at + size, :]
@@ -391,22 +394,19 @@
         behind = jnp.where(has_before, jnp.where(even, two, one), 0.0)
         return ahead, behind
 
-    wide[count:, :] = jnp.zeros((BLOCK, band), jnp.float32)
-    prior_wide[count:, :] = jnp.ones((BLOCK, band), jnp.float32)
-
-    def extended(p):
+    for p in range(PLANES):
         ahead, behind = arrived(p * HALO, HALO)
-        wide[:count, :] = rhs_ref[p]
-        wide[count : count + HALO, :] = ahead
-        wide[rows - 2 :, :] = behind[HALO - 2 :]
-        return wide[...]
-
+        edge[p] = jnp.zeros((BLOCK, band), jnp.float32)
+        edge[p, :HALO, :] = ahead
+        edge[p, BLOCK - 2 :, :] = behind[HALO - 2 :]
     for c in range(3):
         ahead, behind = arrived(PLANES * HALO + 2 * c, 2)
-        prior_wide[:count, :] = prior_ref[c]
-        prior_wide[count : count + 2, :] = ahead
-        prior_wide[rows - 1 :, :] = behind[1:]
-        precision = prior_wide[...]
+        edge[PLANES + c] = jnp.ones((BLOCK, band), jnp.float32)
+        edge[PLANES + c, :2, :] = ahead
+        edge[PLANES + c, BLOCK - 1 :, :] = behind[1:]
+
+    for c in range(3):
+        precision = jnp.concatenate([prior_ref[c], edge[PLANES + c]], axis=0)
         root = jnp.sqrt(precision)
         diagonal = (precision + weight - SHIFT) * (1.0 / SPREAD)
         beside = root * (COUPLING / SPREAD)
@@ -419,29 +419,29 @@
 
         for part in range(2):
             p = 2 * c + part
-            zero = extended(p)
+            zero = jnp.concatenate([rhs_ref[p], edge[p]], axis=0)
             one = apply(zero)
             two = apply(one)
-            one_ref[p] = one[:count]
-            two_ref[p] = two[:count]
             scaled = root * two
             pair = scaled * pltpu.roll(scaled, rows - 1, 0)
+            last = diagonal * two * two - (2.0 * COUPLING / SPREAD) * pair
+            zero, one, two, last = zero[:count], one[:count], two[:count], last[:count]
+            one_ref[p] = one
+            two_ref[p] = two
             for i, term in enumerate(
-                (
-                    zero * zero,
-                    zero * one,
-                    one * one,
-                    one * two,
-                    two * two,
-                    diagonal * two * two - (2.0 * COUPLING / SPREAD) * pair,
-                )
+                (zero * zero, zero * one, one * one, one * two, two * two, last)
             ):
                 sums[i] = sums[i] + term
-    lane = lax.broadcasted_iota(jnp.int32, (1, LANES), 1)
-    line = jnp.zeros((1, LANES), jnp.float32)
+    lines = []
     for i in range(6):
-        part = jnp.sum(jnp.where(own, sums[i], 0.0), keepdims=True)
-        line = jnp.where(lane == i, part, line)
+        folded = sums[i][:, :LANES]
+        for at in range(LANES, band, LANES):
+            folded = folded + sums[i][:, at : at + LANES]
+        lines.append(jnp.sum(folded, axis=0, keepdims=True))
+    column = jnp.sum(jnp.concatenate(lines, axis=0), axis=1, keepdims=True)
+    row = lax.broadcasted_iota(jnp.int32, (6, LANES), 0)
+    lane = lax.broadcasted_iota(jnp.int32, (6, LANES), 1)
+    line = jnp.sum(jnp.where(lane == row, column, 0.0), axis=0, keepdims=True)
     sums_ref[...] = jnp.broadcast_to(line, sums_ref.shape)
 
 
@@ -561,7 +561,7 @@
         [
             pltpu.VMEM((3 * LANES, 2 * second * cycles), bf16),
             pltpu.VMEM((tiles, cap), f32),
-            pltpu.VMEM((tiles, cap), i32),
+            pltpu.VMEM((tiles, cap), f32),
         ],
     )(got, sky)
     sums = exchange(sums, everywhere)
@@ -608,7 +608,7 @@
         krylov_kernel,
         "krylov",
         [((PLANES, count, band), f32)] * 2 + [((devices, LANES), f32)],
-        [pltpu.VMEM((count + BLOCK, band), f32)] * 2,
+        [pltpu.VMEM((PLANES + 3, BLOCK, band), f32)],
     )(rhs, weights, prior_precision, from_one, from_two)
     sums = exchange(sums, everywhere)
     solution = call(final_kernel, "final", [((PLANES, count, band), f32)])(sums, rhs, one, two)[0]

time: 56.6 us -> 56.3 us (level)
  no operation moved by 1% of the time
where the time goes in v5:
time: 56.3 us; the launch traced here: 56.1 us
  blocking collectives  42.4 us (75%)
  Pallas kernels  8.21 us (15%)
  waiting for transfers between devices  2.55 us (5%)
  starting transfers between devices  2.12 us (4%)
  between operations  0.7 us (1%)
    all_to_all x4, blocking collectives, exchange(): lax.all_to_all(values, axes, split_axis=0, concat_axis=0, tiled=True, axi...  42.4 us
    pallas_call x1, Pallas kernels, per_device(): call(bin_kernel, 'bin', [((3 * second, cycles * LANES), f32), ((PLANES *...  2.51 us
    pallas_call x1, Pallas kernels, per_device(): call(lookup_kernel, 'lookup', [((tiles, cap), f32)] * 6 + [((devices, wid...  2.11 us
    ppermute x1, waiting for transfers between devices, per_device(): from_one = lax.ppermute(to_one, 'det', pairs)  1.57 us
    ppermute x1, starting transfers between devices, per_device(): from_two = lax.ppermute(to_two, 'det', others)  1.47 us
  transfers between devices with their start and end apart: 2, of which 2 were waited for; matrix products, arithmetic and copies ran while one was open for 0% of the time, Pallas kernels for 2%

profile of v5, /device:TPU:0, one launch (start us, length us, event | category | flops | bytes accessed | tf_op | source)
XLA Modules:
  0.0 56.1 jit_solution(6337699557268115593)
XLA Ops:
  0.6 0.0 copy-start.1
  0.6 1.0 %pack.1 = f32[224,128]{1,0:T(8,128)S(1)} custom-call(f32[32,256]{1,0:T(8,128)} %bitcast.37, f32[32,256]{1,0:T(8,128)} %bitcast.38, s32[32,256]{1,0:T(8,128)} %bitcast.39, s32[1,32]{1,0:T(1,128)} %bitcast.40), custom_call_target="tpu_custom_call" | custom-call | tf_op jit(solution)/shard_map/pack/pallas_call | solution.py:529
  1.6 15.1 %all_to_all.36 = f32[32,1,896]{2,1,0:T(1,128)S(1)} all-to-all(f32[32,1,896]{2,1,0:T(1,128)S(1)} %bitcast.28), channel_id=1, replica_groups=mesh['det'=4,'tm'=8] {'det','tm'}, dimensions={0} | all-to-all | bytes 229376 | tf_op jit(solution)/shard_map/all_to_all | solution.py:509
  16.7 0.0 copy-start.4
  16.7 0.0 copy-done.1
  16.7 0.0 copy-start.5
  16.7 2.1 %lookup.1 = (f32[32,256]{1,0:T(8,128)S(1)}, f32[32,256]{1,0:T(8,128)S(1)}, f32[32,256]{1,0:T(8,128)S(1)}, f32[32,256]{1,0:T(8,128)S(1)}, f32[32,256]{1,0:T(8,128...) custom-call(f32[224,128]{1,0:T(8,128)S(1)} %bitcast.27, f32[3,128,128]{2,1,0:T(8,128)S(1)} %bitcast.32), custom_call_target="tpu_custom_call" | custom-call | tf_op jit(solution)/shard_map/lookup/pallas_call | solution.py:557
  18.8 0.0 copy-start.6
  18.8 9.0 %all_to_all.37 = f32[32,1,128]{2,1,0:T(1,128)S(1)} all-to-all(f32[32,1,128]{2,1,0:T(1,128)S(1)} %bitcast.35), channel_id=1, replica_groups=mesh['det'=4,'tm'=8] {'det','tm'}, dimensions={0} | all-to-all | bytes 32768 | tf_op jit(solution)/shard_map/all_to_all | solution.py:509
  27.8 0.0 copy-done.4
  27.8 0.0 copy-done.5
  27.8 0.0 copy-done.6
  27.8 0.0 copy-start.3
  27.8 2.5 %bin.1 = (f32[192,256]{1,0:T(8,128)S(1)}, f32[384,128]{1,0:T(8,128)S(1)}) custom-call(f32[32,128]{1,0:T(8,128)S(1)} %bitcast.29, f32[32,256]{1,0:T(8,128)S(1)} %get-tuple-element.27.data_ref, f32[32,256]{1,0:T(8,128)S(1)} %get-tuple-element.28.signal_ref, f32[32,256]{1,0:T(8,128)S(1)} %get-tuple-element.29.cosine_ref, ...), custom_call_target="tpu_custom_call" | custom-call | tf_op jit(solution)/shard_map/bin/pallas_call | solution.py:570
  30.3 0.0 copy-start
  30.3 0.0 copy-start.2
  30.3 8.9 %all_to_all.38 = f32[8,48,128]{2,1,0:T(8,128)S(1)} all-to-all(f32[8,48,128]{2,1,0:T(8,128)S(1)} %bitcast.33), channel_id=1, replica_groups={{3,2,5,4,1,0,7,6},{11,10,13,12,9,8,15,14},{19,18,21,20,17,16,23,22},{27..., dimensions={0} | all-to-all | bytes 393216 | tf_op jit(solution)/shard_map/all_to_all | solution.py:509
  39.2 0.0 copy-done.3
  39.2 0.0 copy-done
  39.2 0.0 copy-done.2
  39.2 0.2 rhs.1
  39.4 0.6 %collective-permute-start = (f32[24,512]{1,0:T(8,128)S(1)}, f32[24,512]{1,0:T(8,128)S(1)}, u32[]{:S(2)}, u32[]{:S(2)}) collective-permute-start(f32[24,512]{1,0:T(8,128)S(1)} %get-tuple-element.44), channel_id=1, source_target_pairs={{0,8},{8,0},{16,24},{24,16},{1,9},{9,1},{17,25},{25,17},{2,10},{10... | collective-permute-start | bytes 147464 | tf_op jit(solution)/shard_map/ppermute | solution.py:594
  40.1 1.5 %collective-permute-start.1 = (f32[24,512]{1,0:T(8,128)S(1)}, f32[24,512]{1,0:T(8,128)S(1)}, u32[]{:S(2)}, u32[]{:S(2)}) collective-permute-start(f32[24,512]{1,0:T(8,128)S(1)} %get-tuple-element.45), channel_id=1, source_target_pairs={{0,24},{8,16},{16,8},{24,0},{1,25},{9,17},{17,9},{25,1},{2,26},{10... | collective-permute-start | bytes 147464 | tf_op jit(solution)/shard_map/ppermute | solution.py:595
  41.5 1.0 %report.1 = (f32[3,128,128]{2,1,0:T(8,128)}, f32[1,1]{1,0:T(1,128)}, f32[72,128]{1,0:T(8,128)S(1)}) custom-call(f32[192,256]{1,0:T(8,128)S(1)} %get-tuple-element.37.maps_ref, f32[32,128]{1,0:T(8,128)S(1)} %bitcast.31), custom_call_target="tpu_custom_call" | custom-call | tf_op jit(solution)/shard_map/report/pallas_call | solution.py:596
  42.5 1.6 %collective-permute-done.from_one_ref = f32[24,512]{1,0:T(8,128)S(1)} collective-permute-done((f32[24,512]{1,0:T(8,128)S(1)}, f32[24,512]{1,0:T(8,128)S(1)}, u32[]{:S(2)}, u32[]{:S(2)}) %collective-permute-start) | collective-permute-done | bytes 49184 | tf_op jit(solution)/shard_map/ppermute | solution.py:594
  44.1 1.0 %collective-permute-done.1.from_two_ref = f32[24,512]{1,0:T(8,128)S(1)} collective-permute-done((f32[24,512]{1,0:T(8,128)S(1)}, f32[24,512]{1,0:T(8,128)S(1)}, u32[]{:S(2)}, u32[]{:S(2)}) %collective-permute-start.1) | collective-permute-done | bytes 49184 | tf_op jit(solution)/shard_map/ppermute | solution.py:595
  45.1 0.6 krylov.1
  45.6 9.5 %all_to_all.39 = f32[32,1,128]{2,1,0:T(1,128)S(1)} all-to-all(f32[32,1,128]{2,1,0:T(1,128)S(1)} %bitcast.36), channel_id=1, replica_groups=mesh['det'=4,'tm'=8] {'det','tm'}, dimensions={0} | all-to-all | bytes 32768 | tf_op jit(solution)/shard_map/all_to_all | solution.py:509
  55.2 0.9 %final.1 = f32[6,16,512]{2,1,0:T(8,128)} custom-call(f32[32,128]{1,0:T(8,128)S(1)} %bitcast.34, f32[6,16,512]{2,1,0:T(8,128)S(1)} %get-tuple-element.42.rhs_ref, f32[6,16,512]{2,1,0:T(8,128)S(1)} %get-tuple-element.47.one_ref, f32[6,16,512]{2,1,0:T(8,128)S(1)} %get-tuple-element.48.two_ref), custom_call_target="tpu_custom_call" | custom-call | tf_op jit(solution)/shard_map/final/pallas_call | solution.py:614
Async XLA Ops:
  0.6 16.1 %copy-start.1 = (f32[3,2,8192]{2,1,0:T(2,128)S(1)}, f32[3,2,8192]{2,1,0:T(2,128)}, u32[]{:S(2)}) copy-start(f32[3,2,8192]{2,1,0:T(2,128)} %param.15) | copy-start | bytes 589828
  16.7 11.1 %copy-start.4 = (bf16[384,256]{1,0:T(8,128)(2,1)S(1)}, bf16[384,256]{1,0:T(8,128)(2,1)}, u32[]{:S(2)}) copy-start(bf16[384,256]{1,0:T(8,128)(2,1)} %constant.6.clone.stage_a_ref) | copy-start | bytes 589828
  16.7 11.1 %copy-start.5 = (f32[2,64,128]{2,1,0:T(8,128)S(1)}, f32[2,64,128]{2,1,0:T(8,128)}, u32[]{:S(2)}) copy-start(f32[2,64,128]{2,1,0:T(8,128)} %constant.7.clone.twiddle_ref) | copy-start | bytes 196612
  18.8 9.0 %copy-start.6 = (bf16[64,384]{1,0:T(8,128)(2,1)S(1)}, bf16[64,384]{1,0:T(8,128)(2,1)}, u32[]{:S(2)}) copy-start(bf16[64,384]{1,0:T(8,128)(2,1)} %constant.8.clone.stage_b_ref) | copy-start | bytes 147460
  27.8 11.4 %copy-start.3 = (f32[6,16,512]{2,1,0:T(8,128)S(1)}, f32[6,16,512]{2,1,0:T(8,128)}, u32[]{:S(2)}) copy-start(f32[6,16,512]{2,1,0:T(8,128)} %draw_ref.1) | copy-start | bytes 589828
  30.3 8.9 %copy-start = (f32[3,16,512]{2,1,0:T(8,128)S(1)}, f32[3,16,512]{2,1,0:T(8,128)}, u32[]{:S(2)}) copy-start(f32[3,16,512]{2,1,0:T(8,128)} %prior_ref.3) | copy-start | bytes 294916
  30.3 8.9 %copy-start.2 = (f32[6,16,512]{2,1,0:T(8,128)S(1)}, f32[6,16,512]{2,1,0:T(8,128)}, u32[]{:S(2)}) copy-start(f32[6,16,512]{2,1,0:T(8,128)} %noise_ref.1) | copy-start | bytes 589828
  39.4 4.7 %collective-permute-start = (f32[24,512]{1,0:T(8,128)S(1)}, f32[24,512]{1,0:T(8,128)S(1)}, u32[]{:S(2)}, u32[]{:S(2)}) collective-permute-start(f32[24,512]{1,0:T(8,128)S(1)} %get-tuple-element.44), channel_id=1, source_target_pairs={{0,8},{8,0},{16,24},{24,16},{1,9},{9,1},{17,25},{25,17},{2,10},{10... | collective-permute-start | bytes 147464 | tf_op jit(solution)/shard_map/ppermute | solution.py:594
  40.1 5.0 %collective-permute-start.1 = (f32[24,512]{1,0:T(8,128)S(1)}, f32[24,512]{1,0:T(8,128)S(1)}, u32[]{:S(2)}, u32[]{:S(2)}) collective-permute-start(f32[24,512]{1,0:T(8,128)S(1)} %get-tuple-element.45), channel_id=1, source_target_pairs={{0,24},{8,16},{16,8},{24,0},{1,25},{9,17},{17,9},{25,1},{2,26},{10... | collective-permute-start | bytes 147464 | tf_op jit(solution)/shard_map/ppermute | solution.py:595

commit v6 on v5

--- a/solution.py
+++ b/solution.py
@@ -9,8 +9,7 @@
 from jax.experimental.pallas import tpu as pltpu
 from jax.sharding import PartitionSpec as P
 
-SHIFT = 5.0
-SPREAD = 5.0
+SPREAD = 8.0
 COUPLING = 0.45
 
 LANES = 128
@@ -108,7 +107,7 @@
 
 
 def lookup_kernel(
-    got_ref, sky_ref, data_ref, signal_ref, cosine_ref, sine_ref, line_ref, column_ref, sums_ref,
+    got_ref, sky_ref, prior_ref, data_ref, signal_ref, cosine_ref, sine_ref, line_ref, column_ref, sums_ref,
     table, high, low,
 ):
     tiles, cap = data_ref.shape
@@ -190,6 +189,12 @@
         hits = jnp.sum(jnp.where(cycle == cy, valid, 0.0), axis=1, keepdims=True)
         lines = lines + jnp.where(lane == 2 * tiles + cy, hits * (1.0 / nphi), 0.0)
     line = jnp.sum(lines, axis=0, keepdims=True)
+    prior = prior_ref[...]
+    lane = lax.broadcasted_iota(jnp.int32, (1, width), 1)
+    for i, values in enumerate((prior, prior * prior)):
+        folded = jnp.sum(jnp.sum(values, axis=0), axis=0, keepdims=True)
+        found = jnp.sum(folded, axis=1, keepdims=True)
+        line = jnp.where(lane == 2 * tiles + cycles + i, found, line)
     sums_ref[...] = jnp.broadcast_to(line, sums_ref.shape)
 
 
@@ -316,6 +321,12 @@
             sums_ref[:, at : at + 1], (tiles, LANES)
         )
     weight_ref[tiles * cycles :, :] = jnp.zeros((BLOCK, LANES), jnp.float32)
+    at = 2 * tiles
+    total = jnp.sum(sums_ref[...], axis=0, keepdims=True)
+    hit = jnp.sum(total[:, at : at + cycles], axis=1, keepdims=True) * (1.0 / (tiles * cycles))
+    at = at + cycles
+    center = total[:, at + 1 : at + 2] / total[:, at : at + 1] + hit
+    weight_ref[tiles * cycles + BLOCK - 1 :, :] = jnp.broadcast_to(center, (1, LANES))
 
 
 def rhs_kernel(
@@ -384,7 +395,8 @@
         weights_ref[pl.ds(start + count, BLOCK), :],
         weights_ref[pl.ds(before, BLOCK), :],
     )
-    weight = jnp.concatenate([weights_ref[pl.ds(start, count), :], beyond], axis=0)
+    center = weights_ref[weights_ref.shape[0] - 1 :, :]
+    weight = jnp.concatenate([weights_ref[pl.ds(start, count), :], beyond], axis=0) - center
     weight = jnp.concatenate([weight] * (band // LANES), axis=1)
     sums = [jnp.zeros((count, band), jnp.float32) for _ in range(6)]
 
@@ -408,7 +420,7 @@
     for c in range(3):
         precision = jnp.concatenate([prior_ref[c], edge[PLANES + c]], axis=0)
         root = jnp.sqrt(precision)
-        diagonal = (precision + weight - SHIFT) * (1.0 / SPREAD)
+        diagonal = (precision + weight) * (1.0 / SPREAD)
         beside = root * (COUPLING / SPREAD)
 
         def apply(field):
@@ -453,8 +465,8 @@
     return result
 
 
-def operated(coefficients):
-    result = [SHIFT * a for a in coefficients] + [0.0]
+def operated(coefficients, center):
+    result = [center * a for a in coefficients] + [0.0]
     for i, a in enumerate(coefficients):
         result[i + 1] = result[i + 1] + SPREAD * a
     return result
@@ -464,13 +476,14 @@
     return list(values) + [0.0] * (length - len(values))
 
 
-def conjugate_gradient(moments):
+def conjugate_gradient(moments, center):
+    moments = [moment / moments[0] for moment in moments]
     resid = [1.0]
     direction = [1.0]
     solution = [0.0]
     norm_now = moments[0]
     for iteration in range(3):
-        image = operated(direction)
+        image = operated(direction, center)
         alpha = norm_now / inner(direction, image, moments)
         size = len(direction)
         solution = [a + alpha * b for a, b in zip(padded(solution, size), direction)]
@@ -484,10 +497,11 @@
     return solution
 
 
-def final_kernel(sums_ref, rhs_ref, one_ref, two_ref, out_ref):
+def final_kernel(sums_ref, weights_ref, rhs_ref, one_ref, two_ref, out_ref):
     total = jnp.sum(sums_ref[...], axis=0, keepdims=True)
     moments = [total[:, i : i + 1] for i in range(6)]
-    zero_by, one_by, two_by = conjugate_gradient(moments)
+    center = weights_ref[weights_ref.shape[0] - 1 :, :1]
+    zero_by, one_by, two_by = conjugate_gradient(moments, center)
     for p in range(PLANES):
         out_ref[p] = zero_by * rhs_ref[p] + one_by * one_ref[p] + two_by * two_ref[p]
 
@@ -553,7 +567,7 @@
 
     sky = sky_map.reshape(3, cycles, second, LANES).transpose(0, 2, 1, 3)
     sky = sky.reshape(3, second * cycles, LANES)
-    width = LANES * -(-(2 * tiles + cycles) // LANES)
+    width = LANES * -(-(2 * tiles + cycles + 2) // LANES)
     data, signal, cosine, sine, line, column, sums = call(
         lookup_kernel,
         "lookup",
@@ -563,7 +577,7 @@
             pltpu.VMEM((tiles, cap), f32),
             pltpu.VMEM((tiles, cap), f32),
         ],
-    )(got, sky)
+    )(got, sky, prior_precision)
     sums = exchange(sums, everywhere)
 
     stage_a, twiddle, stage_b = dft_tables(nphi, n_tm)
@@ -611,7 +625,9 @@
         [pltpu.VMEM((PLANES + 3, BLOCK, band), f32)],
     )(rhs, weights, prior_precision, from_one, from_two)
     sums = exchange(sums, everywhere)
-    solution = call(final_kernel, "final", [((PLANES, count, band), f32)])(sums, rhs, one, two)[0]
+    solution = call(final_kernel, "final", [((PLANES, count, band), f32)])(
+        sums, weights, rhs, one, two
+    )[0]
     return (gain, binned, solution)
 
 

time: 56.3 us -> 56.3 us (level)
  no operation moved by 1% of the time
where the time goes in v6:
time: 56.3 us; the launch traced here: 56.1 us
  blocking collectives  42.3 us (75%)
  Pallas kernels  8.36 us (15%)
  waiting for transfers between devices  2.5 us (4%)
  starting transfers between devices  2.13 us (4%)
  between operations  0.71 us (1%)
    all_to_all x4, blocking collectives, exchange(): lax.all_to_all(values, axes, split_axis=0, concat_axis=0, tiled=True, axi...  42.3 us
    pallas_call x1, Pallas kernels, per_device(): call(bin_kernel, 'bin', [((3 * second, cycles * LANES), f32), ((PLANES *...  2.5 us
    pallas_call x1, Pallas kernels, per_device(): call(lookup_kernel, 'lookup', [((tiles, cap), f32)] * 6 + [((devices, wid...  2.11 us
    ppermute x1, waiting for transfers between devices, per_device(): from_one = lax.ppermute(to_one, 'det', pairs)  1.5 us
    ppermute x1, starting transfers between devices, per_device(): from_two = lax.ppermute(to_two, 'det', others)  1.47 us
  transfers between devices with their start and end apart: 2, of which 2 were waited for; matrix products, arithmetic and copies ran while one was open for 0% of the time, Pallas kernels for 2%

profile of v6, /device:TPU:0, one launch (start us, length us, event | category | flops | bytes accessed | tf_op | source)
XLA Modules:
  0.0 56.1 jit_solution(4969095394200938225)
XLA Ops:
  0.6 0.0 copy-start.1
  0.6 1.0 %pack.1 = f32[224,128]{1,0:T(8,128)S(1)} custom-call(f32[32,256]{1,0:T(8,128)} %bitcast.37, f32[32,256]{1,0:T(8,128)} %bitcast.38, s32[32,256]{1,0:T(8,128)} %bitcast.39, s32[1,32]{1,0:T(1,128)} %bitcast.40), custom_call_target="tpu_custom_call" | custom-call | tf_op jit(solution)/shard_map/pack/pallas_call | solution.py:543
  1.6 0.0 copy-start
  1.6 15.1 %all_to_all.36 = f32[32,1,896]{2,1,0:T(1,128)S(1)} all-to-all(f32[32,1,896]{2,1,0:T(1,128)S(1)} %bitcast.28), channel_id=1, replica_groups=mesh['det'=4,'tm'=8] {'det','tm'}, dimensions={0} | all-to-all | bytes 229376 | tf_op jit(solution)/shard_map/all_to_all | solution.py:523
  16.7 0.0 copy-done.1
  16.7 0.0 copy-done
  16.7 0.0 copy-start.4
  16.7 0.0 copy-start.5
  16.7 2.1 %lookup.1 = (f32[32,256]{1,0:T(8,128)S(1)}, f32[32,256]{1,0:T(8,128)S(1)}, f32[32,256]{1,0:T(8,128)S(1)}, f32[32,256]{1,0:T(8,128)S(1)}, f32[32,256]{1,0:T(8,128...) custom-call(f32[224,128]{1,0:T(8,128)S(1)} %bitcast.27, f32[3,128,128]{2,1,0:T(8,128)S(1)} %bitcast.32, ...), custom_call_target="tpu_custom_call" | custom-call | tf_op jit(solution)/shard_map/lookup/pallas_call | solution.py:571
  18.8 0.0 copy-start.6
  18.8 8.8 %all_to_all.37 = f32[32,1,128]{2,1,0:T(1,128)S(1)} all-to-all(f32[32,1,128]{2,1,0:T(1,128)S(1)} %bitcast.35), channel_id=1, replica_groups=mesh['det'=4,'tm'=8] {'det','tm'}, dimensions={0} | all-to-all | bytes 32768 | tf_op jit(solution)/shard_map/all_to_all | solution.py:523
  27.7 0.0 copy-done.4
  27.7 0.0 copy-done.5
  27.7 0.0 copy-done.6
  27.7 2.5 %bin.1 = (f32[192,256]{1,0:T(8,128)S(1)}, f32[384,128]{1,0:T(8,128)S(1)}) custom-call(f32[32,128]{1,0:T(8,128)S(1)} %bitcast.29, f32[32,256]{1,0:T(8,128)S(1)} %get-tuple-element.27.data_ref, f32[32,256]{1,0:T(8,128)S(1)} %get-tuple-element.28.signal_ref, f32[32,256]{1,0:T(8,128)S(1)} %get-tuple-element.29.cosine_ref, ...), custom_call_target="tpu_custom_call" | custom-call | tf_op jit(solution)/shard_map/bin/pallas_call | solution.py:584
  30.2 0.0 copy-start.2
  30.2 0.0 copy-start.3
  30.2 8.9 %all_to_all.38 = f32[8,48,128]{2,1,0:T(8,128)S(1)} all-to-all(f32[8,48,128]{2,1,0:T(8,128)S(1)} %bitcast.33), channel_id=1, replica_groups={{3,2,5,4,1,0,7,6},{11,10,13,12,9,8,15,14},{19,18,21,20,17,16,23,22},{27..., dimensions={0} | all-to-all | bytes 393216 | tf_op jit(solution)/shard_map/all_to_all | solution.py:523
  39.1 0.0 copy-done.2
  39.1 0.0 copy-done.3
  39.1 0.2 rhs.1
  39.3 0.7 %collective-permute-start = (f32[24,512]{1,0:T(8,128)S(1)}, f32[24,512]{1,0:T(8,128)S(1)}, u32[]{:S(2)}, u32[]{:S(2)}) collective-permute-start(f32[24,512]{1,0:T(8,128)S(1)} %get-tuple-element.44), channel_id=1, source_target_pairs={{0,8},{8,0},{16,24},{24,16},{1,9},{9,1},{17,25},{25,17},{2,10},{10... | collective-permute-start | bytes 147464 | tf_op jit(solution)/shard_map/ppermute | solution.py:608
  39.9 1.5 %collective-permute-start.1 = (f32[24,512]{1,0:T(8,128)S(1)}, f32[24,512]{1,0:T(8,128)S(1)}, u32[]{:S(2)}, u32[]{:S(2)}) collective-permute-start(f32[24,512]{1,0:T(8,128)S(1)} %get-tuple-element.45), channel_id=1, source_target_pairs={{0,24},{8,16},{16,8},{24,0},{1,25},{9,17},{17,9},{25,1},{2,26},{10... | collective-permute-start | bytes 147464 | tf_op jit(solution)/shard_map/ppermute | solution.py:609
  41.4 1.1 %report.1 = (f32[3,128,128]{2,1,0:T(8,128)}, f32[1,1]{1,0:T(1,128)}, f32[72,128]{1,0:T(8,128)S(1)}) custom-call(f32[192,256]{1,0:T(8,128)S(1)} %get-tuple-element.37.maps_ref, f32[32,128]{1,0:T(8,128)S(1)} %bitcast.31), custom_call_target="tpu_custom_call" | custom-call | tf_op jit(solution)/shard_map/report/pallas_call | solution.py:610
  42.5 1.5 %collective-permute-done.from_one_ref = f32[24,512]{1,0:T(8,128)S(1)} collective-permute-done((f32[24,512]{1,0:T(8,128)S(1)}, f32[24,512]{1,0:T(8,128)S(1)}, u32[]{:S(2)}, u32[]{:S(2)}) %collective-permute-start) | collective-permute-done | bytes 49184 | tf_op jit(solution)/shard_map/ppermute | solution.py:608
  44.0 1.0 %collective-permute-done.1.from_two_ref = f32[24,512]{1,0:T(8,128)S(1)} collective-permute-done((f32[24,512]{1,0:T(8,128)S(1)}, f32[24,512]{1,0:T(8,128)S(1)}, u32[]{:S(2)}, u32[]{:S(2)}) %collective-permute-start.1) | collective-permute-done | bytes 49184 | tf_op jit(solution)/shard_map/ppermute | solution.py:609
  45.0 0.6 %krylov.1 = (f32[6,16,512]{2,1,0:T(8,128)S(1)}, f32[6,16,512]{2,1,0:T(8,128)S(1)}, f32[32,128]{1,0:T(8,128)S(1)}) custom-call(f32[6,16,512]{2,1,0:T(8,128)S(1)} %get-tuple-element.42.rhs_ref, f32[72,128]{1,0:T(8,128)S(1)} %get-tuple-element.43.weights_ref, f32[3,16,512]{2,1,0:T(8,128)S(1)} %copy-done, f32[24,512]{1,0:T(8,128)S(1)} %collective-permute-done.from_one_ref, ...), custom_call_target="tpu_custom_call" | custom-call | tf_op jit(solution)/shard_map/krylov/pallas_call | solution.py:621
  45.5 9.5 %all_to_all.39 = f32[32,1,128]{2,1,0:T(1,128)S(1)} all-to-all(f32[32,1,128]{2,1,0:T(1,128)S(1)} %bitcast.36), channel_id=1, replica_groups=mesh['det'=4,'tm'=8] {'det','tm'}, dimensions={0} | all-to-all | bytes 32768 | tf_op jit(solution)/shard_map/all_to_all | solution.py:523
  55.1 1.0 %final.1 = f32[6,16,512]{2,1,0:T(8,128)} custom-call(f32[32,128]{1,0:T(8,128)S(1)} %bitcast.34, f32[72,128]{1,0:T(8,128)S(1)} %get-tuple-element.43.weights_ref, f32[6,16,512]{2,1,0:T(8,128)S(1)} %get-tuple-element.42.rhs_ref, f32[6,16,512]{2,1,0:T(8,128)S(1)} %get-tuple-element.47.one_ref, f32[6,16,512]{2,1,0:T(8,128)S(1)} %get-tuple-element.48.two_ref), custom_call_target="tpu_custom_call" | custom-call | tf_op jit(solution)/shard_map/final/pallas_call | solution.py:628
Async XLA Ops:
  0.6 16.1 %copy-start.1 = (f32[3,2,8192]{2,1,0:T(2,128)S(1)}, f32[3,2,8192]{2,1,0:T(2,128)}, u32[]{:S(2)}) copy-start(f32[3,2,8192]{2,1,0:T(2,128)} %param.15) | copy-start | bytes 589828
  1.6 15.1 %copy-start = (f32[3,16,512]{2,1,0:T(8,128)S(1)}, f32[3,16,512]{2,1,0:T(8,128)}, u32[]{:S(2)}) copy-start(f32[3,16,512]{2,1,0:T(8,128)} %prior_ref.5) | copy-start | bytes 294916
  16.7 11.0 %copy-start.4 = (bf16[384,256]{1,0:T(8,128)(2,1)S(1)}, bf16[384,256]{1,0:T(8,128)(2,1)}, u32[]{:S(2)}) copy-start(bf16[384,256]{1,0:T(8,128)(2,1)} %constant.6.clone.stage_a_ref) | copy-start | bytes 589828
  16.7 11.0 %copy-start.5 = (f32[2,64,128]{2,1,0:T(8,128)S(1)}, f32[2,64,128]{2,1,0:T(8,128)}, u32[]{:S(2)}) copy-start(f32[2,64,128]{2,1,0:T(8,128)} %constant.7.clone.twiddle_ref) | copy-start | bytes 196612
  18.8 8.9 %copy-start.6 = (bf16[64,384]{1,0:T(8,128)(2,1)S(1)}, bf16[64,384]{1,0:T(8,128)(2,1)}, u32[]{:S(2)}) copy-start(bf16[64,384]{1,0:T(8,128)(2,1)} %constant.8.clone.stage_b_ref) | copy-start | bytes 147460
  30.2 8.9 %copy-start.2 = (f32[6,16,512]{2,1,0:T(8,128)S(1)}, f32[6,16,512]{2,1,0:T(8,128)}, u32[]{:S(2)}) copy-start(f32[6,16,512]{2,1,0:T(8,128)} %noise_ref.1) | copy-start | bytes 589828
  30.2 8.9 %copy-start.3 = (f32[6,16,512]{2,1,0:T(8,128)S(1)}, f32[6,16,512]{2,1,0:T(8,128)}, u32[]{:S(2)}) copy-start(f32[6,16,512]{2,1,0:T(8,128)} %draw_ref.1) | copy-start | bytes 589828
  39.3 4.7 %collective-permute-start = (f32[24,512]{1,0:T(8,128)S(1)}, f32[24,512]{1,0:T(8,128)S(1)}, u32[]{:S(2)}, u32[]{:S(2)}) collective-permute-start(f32[24,512]{1,0:T(8,128)S(1)} %get-tuple-element.44), channel_id=1, source_target_pairs={{0,8},{8,0},{16,24},{24,16},{1,9},{9,1},{17,25},{25,17},{2,10},{10... | collective-permute-start | bytes 147464 | tf_op jit(solution)/shard_map/ppermute | solution.py:608
  39.9 5.0 %collective-permute-start.1 = (f32[24,512]{1,0:T(8,128)S(1)}, f32[24,512]{1,0:T(8,128)S(1)}, u32[]{:S(2)}, u32[]{:S(2)}) collective-permute-start(f32[24,512]{1,0:T(8,128)S(1)} %get-tuple-element.45), channel_id=1, source_target_pairs={{0,24},{8,16},{16,8},{24,0},{1,25},{9,17},{17,9},{25,1},{2,26},{10... | collective-permute-start | bytes 147464 | tf_op jit(solution)/shard_map/ppermute | solution.py:609

commit v7 on v6

--- a/solution.py
+++ b/solution.py
@@ -37,7 +37,7 @@
 
 def meeting_order(n_tm):
     if n_tm == 8:
-        return [3, 2, 5, 4, 1, 0, 7, 6]
+        return [3, 2, 7, 5, 1, 0, 4, 6]
     return [(i + n_tm // 2 + 1) % n_tm for i in range(n_tm)]
 
 
@@ -82,18 +82,16 @@
     ]
     for copy in copies:
         copy.start()
-    for copy in copies:
-        copy.wait()
     tiles = samples_ref.shape[0]
     halves = samples_ref.shape[1] // LANES
     lines = 3 * halves + 1
-    for h in range(halves):
-        cut = slice(h * LANES, (h + 1) * LANES)
-        out_ref[pl.ds(h, tiles, stride=lines), :] = samples_ref[:, cut]
-        out_ref[pl.ds(halves + h, tiles, stride=lines), :] = angles_ref[:, cut]
-        out_ref[pl.ds(2 * halves + h, tiles, stride=lines), :] = pointing_ref[:, cut].astype(
-            jnp.float32
-        )
+    for field, source in enumerate((samples_ref, angles_ref, pointing_ref)):
+        copies[field].wait()
+        for h in range(halves):
+            out_ref[pl.ds(field * halves + h, tiles, stride=lines), :] = source[
+                :, h * LANES : (h + 1) * LANES
+            ].astype(jnp.float32)
+    copies[3].wait()
     count = counts_ref[...].astype(jnp.float32)
     row = lax.broadcasted_iota(jnp.int32, (tiles, tiles), 0)
     col = lax.broadcasted_iota(jnp.int32, (tiles, tiles), 1)
@@ -477,7 +475,8 @@
 
 
 def conjugate_gradient(moments, center):
-    moments = [moment / moments[0] for moment in moments]
+    inverse = 1.0 / moments[0]
+    moments = [1.0] + [moment * inverse for moment in moments[1:]]
     resid = [1.0]
     direction = [1.0]
     solution = [0.0]

time: 56.3 us -> 56.2 us (level)
  blocking collectives: 42.3 us -> 41.7 us
    ppermute x1, waiting for transfers between devices: 1 us -> 1.76 us  [per_device(): from_two = lax.ppermute(to_two, 'det', others)]
    all_to_all x4, blocking collectives: 42.3 us -> 41.7 us  [exchange(): lax.all_to_all(values, axes, split_axis=0, concat_axis=0, tiled=True, axi...]
where the time goes in v7:
time: 56.2 us; the launch traced here: 55.9 us
  blocking collectives  41.7 us (74%)
  Pallas kernels  8.36 us (15%)
  waiting for transfers between devices  2.97 us (5%)
  starting transfers between devices  2.12 us (4%)
  between operations  0.71 us (1%)
    all_to_all x4, blocking collectives, exchange(): lax.all_to_all(values, axes, split_axis=0, concat_axis=0, tiled=True, axi...  41.7 us
    pallas_call x1, Pallas kernels, per_device(): call(bin_kernel, 'bin', [((3 * second, cycles * LANES), f32), ((PLANES *...  2.5 us
    pallas_call x1, Pallas kernels, per_device(): call(lookup_kernel, 'lookup', [((tiles, cap), f32)] * 6 + [((devices, wid...  2.11 us
    ppermute x1, waiting for transfers between devices, per_device(): from_two = lax.ppermute(to_two, 'det', others)  1.76 us
    ppermute x1, starting transfers between devices, per_device(): from_two = lax.ppermute(to_two, 'det', others)  1.47 us
    ppermute x1, waiting for transfers between devices, per_device(): from_one = lax.ppermute(to_one, 'det', pairs)  1.21 us
  transfers between devices with their start and end apart: 2, of which 2 were waited for; matrix products, arithmetic and copies ran while one was open for 0% of the time, Pallas kernels for 2%

profile of v7, /device:TPU:0, one launch (start us, length us, event | category | flops | bytes accessed | tf_op | source)
XLA Modules:
  0.0 55.9 jit_solution(5524865021319391464)
XLA Ops:
  0.6 0.0 copy-start.1
  0.6 1.0 %pack.1 = f32[224,128]{1,0:T(8,128)S(1)} custom-call(f32[32,256]{1,0:T(8,128)} %bitcast.37, f32[32,256]{1,0:T(8,128)} %bitcast.38, s32[32,256]{1,0:T(8,128)} %bitcast.39, s32[1,32]{1,0:T(1,128)} %bitcast.40), custom_call_target="tpu_custom_call" | custom-call | tf_op jit(solution)/shard_map/pack/pallas_call | solution.py:542
  1.6 0.0 copy-start
  1.6 15.1 %all_to_all.36 = f32[32,1,896]{2,1,0:T(1,128)S(1)} all-to-all(f32[32,1,896]{2,1,0:T(1,128)S(1)} %bitcast.28), channel_id=1, replica_groups=mesh['det'=4,'tm'=8] {'det','tm'}, dimensions={0} | all-to-all | bytes 229376 | tf_op jit(solution)/shard_map/all_to_all | solution.py:522
  16.7 0.0 copy-done.1
  16.7 0.0 copy-done
  16.7 0.0 copy-start.4
  16.7 0.0 copy-start.5
  16.7 2.1 %lookup.1 = (f32[32,256]{1,0:T(8,128)S(1)}, f32[32,256]{1,0:T(8,128)S(1)}, f32[32,256]{1,0:T(8,128)S(1)}, f32[32,256]{1,0:T(8,128)S(1)}, f32[32,256]{1,0:T(8,128...) custom-call(f32[224,128]{1,0:T(8,128)S(1)} %bitcast.27, f32[3,128,128]{2,1,0:T(8,128)S(1)} %bitcast.32, ...), custom_call_target="tpu_custom_call" | custom-call | tf_op jit(solution)/shard_map/lookup/pallas_call | solution.py:570
  18.8 0.0 copy-start.6
  18.8 8.8 %all_to_all.37 = f32[32,1,128]{2,1,0:T(1,128)S(1)} all-to-all(f32[32,1,128]{2,1,0:T(1,128)S(1)} %bitcast.35), channel_id=1, replica_groups=mesh['det'=4,'tm'=8] {'det','tm'}, dimensions={0} | all-to-all | bytes 32768 | tf_op jit(solution)/shard_map/all_to_all | solution.py:522
  27.7 0.0 copy-done.4
  27.7 0.0 copy-done.5
  27.7 0.0 copy-done.6
  27.7 2.5 %bin.1 = (f32[192,256]{1,0:T(8,128)S(1)}, f32[384,128]{1,0:T(8,128)S(1)}) custom-call(f32[32,128]{1,0:T(8,128)S(1)} %bitcast.29, f32[32,256]{1,0:T(8,128)S(1)} %get-tuple-element.27.data_ref, f32[32,256]{1,0:T(8,128)S(1)} %get-tuple-element.28.signal_ref, f32[32,256]{1,0:T(8,128)S(1)} %get-tuple-element.29.cosine_ref, ...), custom_call_target="tpu_custom_call" | custom-call | tf_op jit(solution)/shard_map/bin/pallas_call | solution.py:583
  30.2 0.0 copy-start.2
  30.2 0.0 copy-start.3
  30.2 8.1 %all_to_all.38 = f32[8,48,128]{2,1,0:T(8,128)S(1)} all-to-all(f32[8,48,128]{2,1,0:T(8,128)S(1)} %bitcast.33), channel_id=1, replica_groups={{3,2,7,5,1,0,4,6},{11,10,15,13,9,8,12,14},{19,18,23,21,17,16,20,22},{27..., dimensions={0} | all-to-all | bytes 393216 | tf_op jit(solution)/shard_map/all_to_all | solution.py:522
  38.3 0.0 copy-done.2
  38.3 0.0 copy-done.3
  38.3 0.2 rhs.1
  38.5 0.7 %collective-permute-start = (f32[24,512]{1,0:T(8,128)S(1)}, f32[24,512]{1,0:T(8,128)S(1)}, u32[]{:S(2)}, u32[]{:S(2)}) collective-permute-start(f32[24,512]{1,0:T(8,128)S(1)} %get-tuple-element.44), channel_id=1, source_target_pairs={{0,8},{8,0},{16,24},{24,16},{1,9},{9,1},{17,25},{25,17},{2,10},{10... | collective-permute-start | bytes 147464 | tf_op jit(solution)/shard_map/ppermute | solution.py:607
  39.2 1.5 %collective-permute-start.1 = (f32[24,512]{1,0:T(8,128)S(1)}, f32[24,512]{1,0:T(8,128)S(1)}, u32[]{:S(2)}, u32[]{:S(2)}) collective-permute-start(f32[24,512]{1,0:T(8,128)S(1)} %get-tuple-element.45), channel_id=1, source_target_pairs={{0,24},{8,16},{16,8},{24,0},{1,25},{9,17},{17,9},{25,1},{2,26},{10... | collective-permute-start | bytes 147464 | tf_op jit(solution)/shard_map/ppermute | solution.py:608
  40.6 1.1 %report.1 = (f32[3,128,128]{2,1,0:T(8,128)}, f32[1,1]{1,0:T(1,128)}, f32[72,128]{1,0:T(8,128)S(1)}) custom-call(f32[192,256]{1,0:T(8,128)S(1)} %get-tuple-element.37.maps_ref, f32[32,128]{1,0:T(8,128)S(1)} %bitcast.31), custom_call_target="tpu_custom_call" | custom-call | tf_op jit(solution)/shard_map/report/pallas_call | solution.py:609
  41.7 1.2 %collective-permute-done.from_one_ref = f32[24,512]{1,0:T(8,128)S(1)} collective-permute-done((f32[24,512]{1,0:T(8,128)S(1)}, f32[24,512]{1,0:T(8,128)S(1)}, u32[]{:S(2)}, u32[]{:S(2)}) %collective-permute-start) | collective-permute-done | bytes 49184 | tf_op jit(solution)/shard_map/ppermute | solution.py:607
  42.9 1.8 %collective-permute-done.1.from_two_ref = f32[24,512]{1,0:T(8,128)S(1)} collective-permute-done((f32[24,512]{1,0:T(8,128)S(1)}, f32[24,512]{1,0:T(8,128)S(1)}, u32[]{:S(2)}, u32[]{:S(2)}) %collective-permute-start.1) | collective-permute-done | bytes 49184 | tf_op jit(solution)/shard_map/ppermute | solution.py:608
  44.7 0.6 %krylov.1 = (f32[6,16,512]{2,1,0:T(8,128)S(1)}, f32[6,16,512]{2,1,0:T(8,128)S(1)}, f32[32,128]{1,0:T(8,128)S(1)}) custom-call(f32[6,16,512]{2,1,0:T(8,128)S(1)} %get-tuple-element.42.rhs_ref, f32[72,128]{1,0:T(8,128)S(1)} %get-tuple-element.43.weights_ref, f32[3,16,512]{2,1,0:T(8,128)S(1)} %copy-done, f32[24,512]{1,0:T(8,128)S(1)} %collective-permute-done.from_one_ref, ...), custom_call_target="tpu_custom_call" | custom-call | tf_op jit(solution)/shard_map/krylov/pallas_call | solution.py:620
  45.2 9.7 %all_to_all.39 = f32[32,1,128]{2,1,0:T(1,128)S(1)} all-to-all(f32[32,1,128]{2,1,0:T(1,128)S(1)} %bitcast.36), channel_id=1, replica_groups=mesh['det'=4,'tm'=8] {'det','tm'}, dimensions={0} | all-to-all | bytes 32768 | tf_op jit(solution)/shard_map/all_to_all | solution.py:522
  54.9 1.0 %final.1 = f32[6,16,512]{2,1,0:T(8,128)} custom-call(f32[32,128]{1,0:T(8,128)S(1)} %bitcast.34, f32[72,128]{1,0:T(8,128)S(1)} %get-tuple-element.43.weights_ref, f32[6,16,512]{2,1,0:T(8,128)S(1)} %get-tuple-element.42.rhs_ref, f32[6,16,512]{2,1,0:T(8,128)S(1)} %get-tuple-element.47.one_ref, f32[6,16,512]{2,1,0:T(8,128)S(1)} %get-tuple-element.48.two_ref), custom_call_target="tpu_custom_call" | custom-call | tf_op jit(solution)/shard_map/final/pallas_call | solution.py:627
Async XLA Ops:
  0.6 16.1 %copy-start.1 = (f32[3,2,8192]{2,1,0:T(2,128)S(1)}, f32[3,2,8192]{2,1,0:T(2,128)}, u32[]{:S(2)}) copy-start(f32[3,2,8192]{2,1,0:T(2,128)} %param.15) | copy-start | bytes 589828
  1.6 15.1 %copy-start = (f32[3,16,512]{2,1,0:T(8,128)S(1)}, f32[3,16,512]{2,1,0:T(8,128)}, u32[]{:S(2)}) copy-start(f32[3,16,512]{2,1,0:T(8,128)} %prior_ref.5) | copy-start | bytes 294916
  16.7 11.0 %copy-start.4 = (bf16[384,256]{1,0:T(8,128)(2,1)S(1)}, bf16[384,256]{1,0:T(8,128)(2,1)}, u32[]{:S(2)}) copy-start(bf16[384,256]{1,0:T(8,128)(2,1)} %constant.6.clone.stage_a_ref) | copy-start | bytes 589828
  16.7 11.0 %copy-start.5 = (f32[2,64,128]{2,1,0:T(8,128)S(1)}, f32[2,64,128]{2,1,0:T(8,128)}, u32[]{:S(2)}) copy-start(f32[2,64,128]{2,1,0:T(8,128)} %constant.7.clone.twiddle_ref) | copy-start | bytes 196612
  18.8 8.9 %copy-start.6 = (bf16[64,384]{1,0:T(8,128)(2,1)S(1)}, bf16[64,384]{1,0:T(8,128)(2,1)}, u32[]{:S(2)}) copy-start(bf16[64,384]{1,0:T(8,128)(2,1)} %constant.8.clone.stage_b_ref) | copy-start | bytes 147460
  30.2 8.1 %copy-start.2 = (f32[6,16,512]{2,1,0:T(8,128)S(1)}, f32[6,16,512]{2,1,0:T(8,128)}, u32[]{:S(2)}) copy-start(f32[6,16,512]{2,1,0:T(8,128)} %noise_ref.1) | copy-start | bytes 589828
  30.2 8.1 %copy-start.3 = (f32[6,16,512]{2,1,0:T(8,128)S(1)}, f32[6,16,512]{2,1,0:T(8,128)}, u32[]{:S(2)}) copy-start(f32[6,16,512]{2,1,0:T(8,128)} %draw_ref.1) | copy-start | bytes 589828
  38.5 4.4 %collective-permute-start = (f32[24,512]{1,0:T(8,128)S(1)}, f32[24,512]{1,0:T(8,128)S(1)}, u32[]{:S(2)}, u32[]{:S(2)}) collective-permute-start(f32[24,512]{1,0:T(8,128)S(1)} %get-tuple-element.44), channel_id=1, source_target_pairs={{0,8},{8,0},{16,24},{24,16},{1,9},{9,1},{17,25},{25,17},{2,10},{10... | collective-permute-start | bytes 147464 | tf_op jit(solution)/shard_map/ppermute | solution.py:607
  39.2 5.5 %collective-permute-start.1 = (f32[24,512]{1,0:T(8,128)S(1)}, f32[24,512]{1,0:T(8,128)S(1)}, u32[]{:S(2)}, u32[]{:S(2)}) collective-permute-start(f32[24,512]{1,0:T(8,128)S(1)} %get-tuple-element.45), channel_id=1, source_target_pairs={{0,24},{8,16},{16,8},{24,0},{1,25},{9,17},{17,9},{25,1},{2,26},{10... | collective-permute-start | bytes 147464 | tf_op jit(solution)/shard_map/ppermute | solution.py:608

commit v8 on v7

--- a/solution.py
+++ b/solution.py
@@ -395,8 +395,7 @@
     )
     center = weights_ref[weights_ref.shape[0] - 1 :, :]
     weight = jnp.concatenate([weights_ref[pl.ds(start, count), :], beyond], axis=0) - center
-    weight = jnp.concatenate([weight] * (band // LANES), axis=1)
-    sums = [jnp.zeros((count, band), jnp.float32) for _ in range(6)]
+    sums = [jnp.zeros((count, LANES), jnp.float32) for _ in range(6)]
 
     def arrived(at, size):
         one, two = from_one_ref[at : at + size, :], from_two_ref[at : at + size, :]
@@ -415,8 +414,9 @@
         edge[PLANES + c, :2, :] = ahead
         edge[PLANES + c, BLOCK - 1 :, :] = behind[1:]
 
-    for c in range(3):
-        precision = jnp.concatenate([prior_ref[c], edge[PLANES + c]], axis=0)
+    for c, at in ((c, at) for at in range(0, band, LANES) for c in range(3)):
+        cut = slice(at, at + LANES)
+        precision = jnp.concatenate([prior_ref[c, :, cut], edge[PLANES + c, :, cut]], axis=0)
         root = jnp.sqrt(precision)
         diagonal = (precision + weight) * (1.0 / SPREAD)
         beside = root * (COUPLING / SPREAD)
@@ -429,25 +429,22 @@
 
         for part in range(2):
             p = 2 * c + part
-            zero = jnp.concatenate([rhs_ref[p], edge[p]], axis=0)
+            zero = jnp.concatenate([rhs_ref[p, :, cut], edge[p, :, cut]], axis=0)
             one = apply(zero)
             two = apply(one)
             scaled = root * two
             pair = scaled * pltpu.roll(scaled, rows - 1, 0)
             last = diagonal * two * two - (2.0 * COUPLING / SPREAD) * pair
             zero, one, two, last = zero[:count], one[:count], two[:count], last[:count]
-            one_ref[p] = one
-            two_ref[p] = two
+            one_ref[p, :, cut] = one
+            two_ref[p, :, cut] = two
             for i, term in enumerate(
                 (zero * zero, zero * one, one * one, one * two, two * two, last)
             ):
                 sums[i] = sums[i] + term
     lines = []
     for i in range(6):
-        folded = sums[i][:, :LANES]
-        for at in range(LANES, band, LANES):
-            folded = folded + sums[i][:, at : at + LANES]
-        lines.append(jnp.sum(folded, axis=0, keepdims=True))
+        lines.append(jnp.sum(sums[i], axis=0, keepdims=True))
     column = jnp.sum(jnp.concatenate(lines, axis=0), axis=1, keepdims=True)
     row = lax.broadcasted_iota(jnp.int32, (6, LANES), 0)
     lane = lax.broadcasted_iota(jnp.int32, (6, LANES), 1)

time: 56.2 us -> 56.1 us (level)
  no operation moved by 1% of the time
where the time goes in v8:
time: 56.1 us; the launch traced here: 55.8 us
  blocking collectives  41.7 us (74%)
  Pallas kernels  8.3 us (15%)
  waiting for transfers between devices  2.97 us (5%)
  starting transfers between devices  2.12 us (4%)
  between operations  0.71 us (1%)
    all_to_all x4, blocking collectives, exchange(): lax.all_to_all(values, axes, split_axis=0, concat_axis=0, tiled=True, axi...  41.7 us
    pallas_call x1, Pallas kernels, per_device(): call(bin_kernel, 'bin', [((3 * second, cycles * LANES), f32), ((PLANES *...  2.5 us
    pallas_call x1, Pallas kernels, per_device(): call(lookup_kernel, 'lookup', [((tiles, cap), f32)] * 6 + [((devices, wid...  2.11 us
    ppermute x1, waiting for transfers between devices, per_device(): from_two = lax.ppermute(to_two, 'det', others)  1.76 us
    ppermute x1, starting transfers between devices, per_device(): from_two = lax.ppermute(to_two, 'det', others)  1.47 us
    ppermute x1, waiting for transfers between devices, per_device(): from_one = lax.ppermute(to_one, 'det', pairs)  1.21 us
  transfers between devices with their start and end apart: 2, of which 2 were waited for; matrix products, arithmetic and copies ran while one was open for 0% of the time, Pallas kernels for 2%

profile of v8, /device:TPU:0, one launch (start us, length us, event | category | flops | bytes accessed | tf_op | source)
XLA Modules:
  0.0 55.8 jit_solution(8473729965920110579)
XLA Ops:
  0.6 0.0 copy-start.1
  0.6 1.0 %pack.1 = f32[224,128]{1,0:T(8,128)S(1)} custom-call(f32[32,256]{1,0:T(8,128)} %bitcast.37, f32[32,256]{1,0:T(8,128)} %bitcast.38, s32[32,256]{1,0:T(8,128)} %bitcast.39, s32[1,32]{1,0:T(1,128)} %bitcast.40), custom_call_target="tpu_custom_call" | custom-call | tf_op jit(solution)/shard_map/pack/pallas_call | solution.py:539
  1.6 0.0 copy-start
  1.6 15.1 %all_to_all.36 = f32[32,1,896]{2,1,0:T(1,128)S(1)} all-to-all(f32[32,1,896]{2,1,0:T(1,128)S(1)} %bitcast.28), channel_id=1, replica_groups=mesh['det'=4,'tm'=8] {'det','tm'}, dimensions={0} | all-to-all | bytes 229376 | tf_op jit(solution)/shard_map/all_to_all | solution.py:519
  16.7 0.0 copy-done.1
  16.7 0.0 copy-done
  16.7 0.0 copy-start.4
  16.7 0.0 copy-start.5
  16.7 2.1 %lookup.1 = (f32[32,256]{1,0:T(8,128)S(1)}, f32[32,256]{1,0:T(8,128)S(1)}, f32[32,256]{1,0:T(8,128)S(1)}, f32[32,256]{1,0:T(8,128)S(1)}, f32[32,256]{1,0:T(8,128...) custom-call(f32[224,128]{1,0:T(8,128)S(1)} %bitcast.27, f32[3,128,128]{2,1,0:T(8,128)S(1)} %bitcast.32, ...), custom_call_target="tpu_custom_call" | custom-call | tf_op jit(solution)/shard_map/lookup/pallas_call | solution.py:567
  18.8 0.0 copy-start.6
  18.8 8.8 %all_to_all.37 = f32[32,1,128]{2,1,0:T(1,128)S(1)} all-to-all(f32[32,1,128]{2,1,0:T(1,128)S(1)} %bitcast.35), channel_id=1, replica_groups=mesh['det'=4,'tm'=8] {'det','tm'}, dimensions={0} | all-to-all | bytes 32768 | tf_op jit(solution)/shard_map/all_to_all | solution.py:519
  27.7 0.0 copy-done.4
  27.7 0.0 copy-done.5
  27.7 0.0 copy-done.6
  27.7 2.5 %bin.1 = (f32[192,256]{1,0:T(8,128)S(1)}, f32[384,128]{1,0:T(8,128)S(1)}) custom-call(f32[32,128]{1,0:T(8,128)S(1)} %bitcast.29, f32[32,256]{1,0:T(8,128)S(1)} %get-tuple-element.27.data_ref, f32[32,256]{1,0:T(8,128)S(1)} %get-tuple-element.28.signal_ref, f32[32,256]{1,0:T(8,128)S(1)} %get-tuple-element.29.cosine_ref, ...), custom_call_target="tpu_custom_call" | custom-call | tf_op jit(solution)/shard_map/bin/pallas_call | solution.py:580
  30.2 0.0 copy-start.2
  30.2 0.0 copy-start.3
  30.2 8.1 %all_to_all.38 = f32[8,48,128]{2,1,0:T(8,128)S(1)} all-to-all(f32[8,48,128]{2,1,0:T(8,128)S(1)} %bitcast.33), channel_id=1, replica_groups={{3,2,7,5,1,0,4,6},{11,10,15,13,9,8,12,14},{19,18,23,21,17,16,20,22},{27..., dimensions={0} | all-to-all | bytes 393216 | tf_op jit(solution)/shard_map/all_to_all | solution.py:519
  38.3 0.0 copy-done.2
  38.3 0.0 copy-done.3
  38.3 0.2 rhs.1
  38.5 0.7 %collective-permute-start = (f32[24,512]{1,0:T(8,128)S(1)}, f32[24,512]{1,0:T(8,128)S(1)}, u32[]{:S(2)}, u32[]{:S(2)}) collective-permute-start(f32[24,512]{1,0:T(8,128)S(1)} %get-tuple-element.44), channel_id=1, source_target_pairs={{0,8},{8,0},{16,24},{24,16},{1,9},{9,1},{17,25},{25,17},{2,10},{10... | collective-permute-start | bytes 147464 | tf_op jit(solution)/shard_map/ppermute | solution.py:604
  39.2 1.5 %collective-permute-start.1 = (f32[24,512]{1,0:T(8,128)S(1)}, f32[24,512]{1,0:T(8,128)S(1)}, u32[]{:S(2)}, u32[]{:S(2)}) collective-permute-start(f32[24,512]{1,0:T(8,128)S(1)} %get-tuple-element.45), channel_id=1, source_target_pairs={{0,24},{8,16},{16,8},{24,0},{1,25},{9,17},{17,9},{25,1},{2,26},{10... | collective-permute-start | bytes 147464 | tf_op jit(solution)/shard_map/ppermute | solution.py:605
  40.6 1.1 %report.1 = (f32[3,128,128]{2,1,0:T(8,128)}, f32[1,1]{1,0:T(1,128)}, f32[72,128]{1,0:T(8,128)S(1)}) custom-call(f32[192,256]{1,0:T(8,128)S(1)} %get-tuple-element.37.maps_ref, f32[32,128]{1,0:T(8,128)S(1)} %bitcast.31), custom_call_target="tpu_custom_call" | custom-call | tf_op jit(solution)/shard_map/report/pallas_call | solution.py:606
  41.7 1.2 %collective-permute-done.from_one_ref = f32[24,512]{1,0:T(8,128)S(1)} collective-permute-done((f32[24,512]{1,0:T(8,128)S(1)}, f32[24,512]{1,0:T(8,128)S(1)}, u32[]{:S(2)}, u32[]{:S(2)}) %collective-permute-start) | collective-permute-done | bytes 49184 | tf_op jit(solution)/shard_map/ppermute | solution.py:604
  42.9 1.8 %collective-permute-done.1.from_two_ref = f32[24,512]{1,0:T(8,128)S(1)} collective-permute-done((f32[24,512]{1,0:T(8,128)S(1)}, f32[24,512]{1,0:T(8,128)S(1)}, u32[]{:S(2)}, u32[]{:S(2)}) %collective-permute-start.1) | collective-permute-done | bytes 49184 | tf_op jit(solution)/shard_map/ppermute | solution.py:605
  44.7 0.5 krylov.1
  45.2 9.7 %all_to_all.39 = f32[32,1,128]{2,1,0:T(1,128)S(1)} all-to-all(f32[32,1,128]{2,1,0:T(1,128)S(1)} %bitcast.36), channel_id=1, replica_groups=mesh['det'=4,'tm'=8] {'det','tm'}, dimensions={0} | all-to-all | bytes 32768 | tf_op jit(solution)/shard_map/all_to_all | solution.py:519
  54.9 1.0 %final.1 = f32[6,16,512]{2,1,0:T(8,128)} custom-call(f32[32,128]{1,0:T(8,128)S(1)} %bitcast.34, f32[72,128]{1,0:T(8,128)S(1)} %get-tuple-element.43.weights_ref, f32[6,16,512]{2,1,0:T(8,128)S(1)} %get-tuple-element.42.rhs_ref, f32[6,16,512]{2,1,0:T(8,128)S(1)} %get-tuple-element.47.one_ref, f32[6,16,512]{2,1,0:T(8,128)S(1)} %get-tuple-element.48.two_ref), custom_call_target="tpu_custom_call" | custom-call | tf_op jit(solution)/shard_map/final/pallas_call | solution.py:624
Async XLA Ops:
  0.6 16.1 %copy-start.1 = (f32[3,2,8192]{2,1,0:T(2,128)S(1)}, f32[3,2,8192]{2,1,0:T(2,128)}, u32[]{:S(2)}) copy-start(f32[3,2,8192]{2,1,0:T(2,128)} %param.15) | copy-start | bytes 589828
  1.6 15.1 %copy-start = (f32[3,16,512]{2,1,0:T(8,128)S(1)}, f32[3,16,512]{2,1,0:T(8,128)}, u32[]{:S(2)}) copy-start(f32[3,16,512]{2,1,0:T(8,128)} %prior_ref.5) | copy-start | bytes 294916
  16.7 11.0 %copy-start.4 = (bf16[384,256]{1,0:T(8,128)(2,1)S(1)}, bf16[384,256]{1,0:T(8,128)(2,1)}, u32[]{:S(2)}) copy-start(bf16[384,256]{1,0:T(8,128)(2,1)} %constant.6.clone.stage_a_ref) | copy-start | bytes 589828
  16.7 11.0 %copy-start.5 = (f32[2,64,128]{2,1,0:T(8,128)S(1)}, f32[2,64,128]{2,1,0:T(8,128)}, u32[]{:S(2)}) copy-start(f32[2,64,128]{2,1,0:T(8,128)} %constant.7.clone.twiddle_ref) | copy-start | bytes 196612
  18.8 8.9 %copy-start.6 = (bf16[64,384]{1,0:T(8,128)(2,1)S(1)}, bf16[64,384]{1,0:T(8,128)(2,1)}, u32[]{:S(2)}) copy-start(bf16[64,384]{1,0:T(8,128)(2,1)} %constant.8.clone.stage_b_ref) | copy-start | bytes 147460
  30.2 8.1 %copy-start.2 = (f32[6,16,512]{2,1,0:T(8,128)S(1)}, f32[6,16,512]{2,1,0:T(8,128)}, u32[]{:S(2)}) copy-start(f32[6,16,512]{2,1,0:T(8,128)} %noise_ref.1) | copy-start | bytes 589828
  30.2 8.1 %copy-start.3 = (f32[6,16,512]{2,1,0:T(8,128)S(1)}, f32[6,16,512]{2,1,0:T(8,128)}, u32[]{:S(2)}) copy-start(f32[6,16,512]{2,1,0:T(8,128)} %draw_ref.1) | copy-start | bytes 589828
  38.5 4.4 %collective-permute-start = (f32[24,512]{1,0:T(8,128)S(1)}, f32[24,512]{1,0:T(8,128)S(1)}, u32[]{:S(2)}, u32[]{:S(2)}) collective-permute-start(f32[24,512]{1,0:T(8,128)S(1)} %get-tuple-element.44), channel_id=1, source_target_pairs={{0,8},{8,0},{16,24},{24,16},{1,9},{9,1},{17,25},{25,17},{2,10},{10... | collective-permute-start | bytes 147464 | tf_op jit(solution)/shard_map/ppermute | solution.py:604
  39.2 5.5 %collective-permute-start.1 = (f32[24,512]{1,0:T(8,128)S(1)}, f32[24,512]{1,0:T(8,128)S(1)}, u32[]{:S(2)}, u32[]{:S(2)}) collective-permute-start(f32[24,512]{1,0:T(8,128)S(1)} %get-tuple-element.45), channel_id=1, source_target_pairs={{0,24},{8,16},{16,8},{24,0},{1,25},{9,17},{17,9},{25,1},{2,26},{10... | collective-permute-start | bytes 147464 | tf_op jit(solution)/shard_map/ppermute | solution.py:605

commit v9 on v8

--- a/solution.py
+++ b/solution.py
@@ -453,11 +453,15 @@
 
 
 def inner(left, right, moments):
-    result = 0.0
+    terms = [None] * (len(left) + len(right) - 1)
     for i, a in enumerate(left):
         for j, b in enumerate(right):
-            result = result + a * b * moments[i + j]
-    return result
+            terms[i + j] = a * b if terms[i + j] is None else terms[i + j] + a * b
+    terms = [term * moment for term, moment in zip(terms, moments)]
+    while len(terms) > 1:
+        pairs = [x + y for x, y in zip(terms[::2], terms[1::2])]
+        terms = pairs + terms[2 * len(pairs) :]
+    return terms[0]
 
 
 def operated(coefficients, center):

time: 56.1 us -> 56.1 us (level)
  no operation moved by 1% of the time
where the time goes in v9:
time: 56.1 us; the launch traced here: 55.9 us
  blocking collectives  41.7 us (74%)
  Pallas kernels  8.3 us (15%)
  waiting for transfers between devices  2.97 us (5%)
  starting transfers between devices  2.12 us (4%)
  between operations  0.71 us (1%)
    all_to_all x4, blocking collectives, exchange(): lax.all_to_all(values, axes, split_axis=0, concat_axis=0, tiled=True, axi...  41.7 us
    pallas_call x1, Pallas kernels, per_device(): call(bin_kernel, 'bin', [((3 * second, cycles * LANES), f32), ((PLANES *...  2.5 us
    pallas_call x1, Pallas kernels, per_device(): call(lookup_kernel, 'lookup', [((tiles, cap), f32)] * 6 + [((devices, wid...  2.11 us
    ppermute x1, waiting for transfers between devices, per_device(): from_two = lax.ppermute(to_two, 'det', others)  1.76 us
    ppermute x1, starting transfers between devices, per_device(): from_two = lax.ppermute(to_two, 'det', others)  1.47 us
    ppermute x1, waiting for transfers between devices, per_device(): from_one = lax.ppermute(to_one, 'det', pairs)  1.21 us
  transfers between devices with their start and end apart: 2, of which 2 were waited for; matrix products, arithmetic and copies ran while one was open for 0% of the time, Pallas kernels for 2%

profile of v9, /device:TPU:0, one launch (start us, length us, event | category | flops | bytes accessed | tf_op | source)
XLA Modules:
  0.0 55.9 jit_solution(12946947721091694131)
XLA Ops:
  0.6 0.0 copy-start.1
  0.6 1.0 %pack.1 = f32[224,128]{1,0:T(8,128)S(1)} custom-call(f32[32,256]{1,0:T(8,128)} %bitcast.37, f32[32,256]{1,0:T(8,128)} %bitcast.38, s32[32,256]{1,0:T(8,128)} %bitcast.39, s32[1,32]{1,0:T(1,128)} %bitcast.40), custom_call_target="tpu_custom_call" | custom-call | tf_op jit(solution)/shard_map/pack/pallas_call | solution.py:543
  1.6 0.0 copy-start
  1.6 15.1 %all_to_all.36 = f32[32,1,896]{2,1,0:T(1,128)S(1)} all-to-all(f32[32,1,896]{2,1,0:T(1,128)S(1)} %bitcast.28), channel_id=1, replica_groups=mesh['det'=4,'tm'=8] {'det','tm'}, dimensions={0} | all-to-all | bytes 229376 | tf_op jit(solution)/shard_map/all_to_all | solution.py:523
  16.7 0.0 copy-done.1
  16.7 0.0 copy-done
  16.7 0.0 copy-start.4
  16.7 0.0 copy-start.5
  16.7 2.1 %lookup.1 = (f32[32,256]{1,0:T(8,128)S(1)}, f32[32,256]{1,0:T(8,128)S(1)}, f32[32,256]{1,0:T(8,128)S(1)}, f32[32,256]{1,0:T(8,128)S(1)}, f32[32,256]{1,0:T(8,128...) custom-call(f32[224,128]{1,0:T(8,128)S(1)} %bitcast.27, f32[3,128,128]{2,1,0:T(8,128)S(1)} %bitcast.32, ...), custom_call_target="tpu_custom_call" | custom-call | tf_op jit(solution)/shard_map/lookup/pallas_call | solution.py:571
  18.8 0.0 copy-start.6
  18.8 8.8 %all_to_all.37 = f32[32,1,128]{2,1,0:T(1,128)S(1)} all-to-all(f32[32,1,128]{2,1,0:T(1,128)S(1)} %bitcast.35), channel_id=1, replica_groups=mesh['det'=4,'tm'=8] {'det','tm'}, dimensions={0} | all-to-all | bytes 32768 | tf_op jit(solution)/shard_map/all_to_all | solution.py:523
  27.7 0.0 copy-done.4
  27.7 0.0 copy-done.5
  27.7 0.0 copy-done.6
  27.7 2.5 %bin.1 = (f32[192,256]{1,0:T(8,128)S(1)}, f32[384,128]{1,0:T(8,128)S(1)}) custom-call(f32[32,128]{1,0:T(8,128)S(1)} %bitcast.29, f32[32,256]{1,0:T(8,128)S(1)} %get-tuple-element.27.data_ref, f32[32,256]{1,0:T(8,128)S(1)} %get-tuple-element.28.signal_ref, f32[32,256]{1,0:T(8,128)S(1)} %get-tuple-element.29.cosine_ref, ...), custom_call_target="tpu_custom_call" | custom-call | tf_op jit(solution)/shard_map/bin/pallas_call | solution.py:584
  30.2 0.0 copy-start.2
  30.2 0.0 copy-start.3
  30.2 8.1 %all_to_all.38 = f32[8,48,128]{2,1,0:T(8,128)S(1)} all-to-all(f32[8,48,128]{2,1,0:T(8,128)S(1)} %bitcast.33), channel_id=1, replica_groups={{3,2,7,5,1,0,4,6},{11,10,15,13,9,8,12,14},{19,18,23,21,17,16,20,22},{27..., dimensions={0} | all-to-all | bytes 393216 | tf_op jit(solution)/shard_map/all_to_all | solution.py:523
  38.3 0.0 copy-done.2
  38.3 0.0 copy-done.3
  38.3 0.2 rhs.1
  38.5 0.7 %collective-permute-start = (f32[24,512]{1,0:T(8,128)S(1)}, f32[24,512]{1,0:T(8,128)S(1)}, u32[]{:S(2)}, u32[]{:S(2)}) collective-permute-start(f32[24,512]{1,0:T(8,128)S(1)} %get-tuple-element.44), channel_id=1, source_target_pairs={{0,8},{8,0},{16,24},{24,16},{1,9},{9,1},{17,25},{25,17},{2,10},{10... | collective-permute-start | bytes 147464 | tf_op jit(solution)/shard_map/ppermute | solution.py:608
  39.2 1.5 %collective-permute-start.1 = (f32[24,512]{1,0:T(8,128)S(1)}, f32[24,512]{1,0:T(8,128)S(1)}, u32[]{:S(2)}, u32[]{:S(2)}) collective-permute-start(f32[24,512]{1,0:T(8,128)S(1)} %get-tuple-element.45), channel_id=1, source_target_pairs={{0,24},{8,16},{16,8},{24,0},{1,25},{9,17},{17,9},{25,1},{2,26},{10... | collective-permute-start | bytes 147464 | tf_op jit(solution)/shard_map/ppermute | solution.py:609
  40.6 1.1 %report.1 = (f32[3,128,128]{2,1,0:T(8,128)}, f32[1,1]{1,0:T(1,128)}, f32[72,128]{1,0:T(8,128)S(1)}) custom-call(f32[192,256]{1,0:T(8,128)S(1)} %get-tuple-element.37.maps_ref, f32[32,128]{1,0:T(8,128)S(1)} %bitcast.31), custom_call_target="tpu_custom_call" | custom-call | tf_op jit(solution)/shard_map/report/pallas_call | solution.py:610
  41.7 1.2 %collective-permute-done.from_one_ref = f32[24,512]{1,0:T(8,128)S(1)} collective-permute-done((f32[24,512]{1,0:T(8,128)S(1)}, f32[24,512]{1,0:T(8,128)S(1)}, u32[]{:S(2)}, u32[]{:S(2)}) %collective-permute-start) | collective-permute-done | bytes 49184 | tf_op jit(solution)/shard_map/ppermute | solution.py:608
  42.9 1.8 %collective-permute-done.1.from_two_ref = f32[24,512]{1,0:T(8,128)S(1)} collective-permute-done((f32[24,512]{1,0:T(8,128)S(1)}, f32[24,512]{1,0:T(8,128)S(1)}, u32[]{:S(2)}, u32[]{:S(2)}) %collective-permute-start.1) | collective-permute-done | bytes 49184 | tf_op jit(solution)/shard_map/ppermute | solution.py:609
  44.7 0.5 krylov.1
  45.2 9.7 %all_to_all.39 = f32[32,1,128]{2,1,0:T(1,128)S(1)} all-to-all(f32[32,1,128]{2,1,0:T(1,128)S(1)} %bitcast.36), channel_id=1, replica_groups=mesh['det'=4,'tm'=8] {'det','tm'}, dimensions={0} | all-to-all | bytes 32768 | tf_op jit(solution)/shard_map/all_to_all | solution.py:523
  54.9 1.0 %final.1 = f32[6,16,512]{2,1,0:T(8,128)} custom-call(f32[32,128]{1,0:T(8,128)S(1)} %bitcast.34, f32[72,128]{1,0:T(8,128)S(1)} %get-tuple-element.43.weights_ref, f32[6,16,512]{2,1,0:T(8,128)S(1)} %get-tuple-element.42.rhs_ref, f32[6,16,512]{2,1,0:T(8,128)S(1)} %get-tuple-element.47.one_ref, f32[6,16,512]{2,1,0:T(8,128)S(1)} %get-tuple-element.48.two_ref), custom_call_target="tpu_custom_call" | custom-call | tf_op jit(solution)/shard_map/final/pallas_call | solution.py:628
Async XLA Ops:
  0.6 16.1 %copy-start.1 = (f32[3,2,8192]{2,1,0:T(2,128)S(1)}, f32[3,2,8192]{2,1,0:T(2,128)}, u32[]{:S(2)}) copy-start(f32[3,2,8192]{2,1,0:T(2,128)} %param.15) | copy-start | bytes 589828
  1.6 15.1 %copy-start = (f32[3,16,512]{2,1,0:T(8,128)S(1)}, f32[3,16,512]{2,1,0:T(8,128)}, u32[]{:S(2)}) copy-start(f32[3,16,512]{2,1,0:T(8,128)} %prior_ref.5) | copy-start | bytes 294916
  16.7 11.0 %copy-start.4 = (bf16[384,256]{1,0:T(8,128)(2,1)S(1)}, bf16[384,256]{1,0:T(8,128)(2,1)}, u32[]{:S(2)}) copy-start(bf16[384,256]{1,0:T(8,128)(2,1)} %constant.6.clone.stage_a_ref) | copy-start | bytes 589828
  16.7 11.0 %copy-start.5 = (f32[2,64,128]{2,1,0:T(8,128)S(1)}, f32[2,64,128]{2,1,0:T(8,128)}, u32[]{:S(2)}) copy-start(f32[2,64,128]{2,1,0:T(8,128)} %constant.7.clone.twiddle_ref) | copy-start | bytes 196612
  18.8 8.9 %copy-start.6 = (bf16[64,384]{1,0:T(8,128)(2,1)S(1)}, bf16[64,384]{1,0:T(8,128)(2,1)}, u32[]{:S(2)}) copy-start(bf16[64,384]{1,0:T(8,128)(2,1)} %constant.8.clone.stage_b_ref) | copy-start | bytes 147460
  30.2 8.1 %copy-start.2 = (f32[6,16,512]{2,1,0:T(8,128)S(1)}, f32[6,16,512]{2,1,0:T(8,128)}, u32[]{:S(2)}) copy-start(f32[6,16,512]{2,1,0:T(8,128)} %noise_ref.1) | copy-start | bytes 589828
  30.2 8.1 %copy-start.3 = (f32[6,16,512]{2,1,0:T(8,128)S(1)}, f32[6,16,512]{2,1,0:T(8,128)}, u32[]{:S(2)}) copy-start(f32[6,16,512]{2,1,0:T(8,128)} %draw_ref.1) | copy-start | bytes 589828
  38.5 4.4 %collective-permute-start = (f32[24,512]{1,0:T(8,128)S(1)}, f32[24,512]{1,0:T(8,128)S(1)}, u32[]{:S(2)}, u32[]{:S(2)}) collective-permute-start(f32[24,512]{1,0:T(8,128)S(1)} %get-tuple-element.44), channel_id=1, source_target_pairs={{0,8},{8,0},{16,24},{24,16},{1,9},{9,1},{17,25},{25,17},{2,10},{10... | collective-permute-start | bytes 147464 | tf_op jit(solution)/shard_map/ppermute | solution.py:608
  39.2 5.5 %collective-permute-start.1 = (f32[24,512]{1,0:T(8,128)S(1)}, f32[24,512]{1,0:T(8,128)S(1)}, u32[]{:S(2)}, u32[]{:S(2)}) collective-permute-start(f32[24,512]{1,0:T(8,128)S(1)} %get-tuple-element.45), channel_id=1, source_target_pairs={{0,24},{8,16},{16,8},{24,0},{1,25},{9,17},{17,9},{25,1},{2,26},{10... | collective-permute-start | bytes 147464 | tf_op jit(solution)/shard_map/ppermute | solution.py:609
